TPU v7x, 32 devices: a whole 2x2x4 slice. The times are simulated.
32 devices in a mesh: dp: 8 (over z, x), tensor: 4 (over y, core).
Axes of the slice: x: 2, y: 2, z: 4, core: 2. Of those that a mesh axis runs over, the one named last changes fastest.
Arguments:
- tokens: bfloat16 [6144, 2048], P(('dp', 'tensor')), may hold values from -6 to 6
- query_weight: float32 [2048, 2048], P('dp', 'tensor'), may hold values from -0.125 to 0.125
- key_weight: float32 [2048, 256], P('dp', 'tensor'), may hold values from -0.125 to 0.125
- value_weight: float32 [2048, 256], P('dp', 'tensor'), may hold values from -0.125 to 0.125
- output_weight: float32 [2048, 2048], P('tensor', 'dp'), may hold values from -0.375 to 0.375
- gate_weight: float32 [2048, 5632], P('dp', 'tensor'), may hold values from -0.125 to 0.125
- up_weight: float32 [2048, 5632], P('dp', 'tensor'), may hold values from -0.125 to 0.125
- down_weight: float32 [5632, 2048], P('tensor', 'dp'), may hold values from -0.078125 to 0.078125
- attention_gain: float32 [2048], P('dp'), may hold values from 0.5 to 1.5
- feed_gain: float32 [2048], P('dp'), may hold values from 0.5 to 1.5
- doc_lengths: int32 [8, 6], P('dp'), may hold values from 0 to 614, as said below
- cotangent: bfloat16 [6144, 2048], P(('dp', 'tensor')), may hold values from -6 to 6
Outputs:
- layer_out: bfloat16 [6144, 2048], P(('dp', 'tensor'))
- input_grad: float32 [6144, 2048], P(('dp', 'tensor'))
- query_grad: float32 [2048, 2048], P('dp', 'tensor')
- key_grad: float32 [2048, 256], P('dp', 'tensor')
- value_grad: float32 [2048, 256], P('dp', 'tensor')
- output_grad: float32 [2048, 2048], P('tensor', 'dp')
- gate_grad: float32 [2048, 5632], P('dp', 'tensor')
- up_grad: float32 [2048, 5632], P('dp', 'tensor')
- down_grad: float32 [5632, 2048], P('tensor', 'dp')
- attention_gain_grad: float32 [2048], P('dp')
- feed_gain_grad: float32 [2048], P('dp')
Inputs may be any that keep to these rules, and one draw needn't show every extreme that they name: `doc_lengths`: entry 1 of every row is exactly 614; entry 0 is at most (154) // 2, every later entry at most (154) // 8, so that a row sums to at most 768.
All inputs are finite; a program needn't handle non-finite values.
Results may differ from a plain program's by a relative error of at most 0.025.
Values may be sent and summed in bfloat16 or wider, within the bound.
No kernel may reach another device: no remote copies, remote signals or barrier semaphores. Data moves between devices by JAX's collectives and lax.ppermute only.
A program may use at most 192 MiB of HBM per device.

v0:
```python
import math

import jax
import jax.numpy as jnp
from jax import lax
from jax.sharding import PartitionSpec as P

HEAD_DIM = 64


EPS = 1e-05
NEG = -1e30


def group_layout(counts, total):
    ends = jnp.cumsum(counts)
    starts = ends - counts
    place = jnp.arange(total, dtype=jnp.int32)
    segment = jnp.sum((place[:, None] >= ends[None, :]).astype(jnp.int32), axis=1)
    bounds = jnp.concatenate([starts, ends[-1:]])
    slots = jnp.arange(bounds.shape[0], dtype=jnp.int32)
    begin = jnp.sum(jnp.where(segment[:, None] == slots[None, :], bounds[None, :], 0), axis=1)
    position = (place - begin).astype(jnp.float32)
    valid = (place < ends[-1]).astype(jnp.float32)
    allowed = (segment[:, None] == segment[None, :]) & (place[None, :] <= place[:, None])
    return (position, valid, allowed)


def angle_tables(position):
    half = HEAD_DIM // 2
    freq = jnp.exp(jnp.arange(half, dtype=jnp.float32) * (-2.0 * math.log(10000.0) / HEAD_DIM))
    angle = position[:, None] * freq[None, :]
    return (jnp.cos(angle), jnp.sin(angle))


def rotate(values, cosine, sine, sign):
    rows = values.shape[0]
    split = values.reshape(rows, -1, HEAD_DIM)
    half = HEAD_DIM // 2
    first = split[..., :half]
    second = split[..., half:]
    cos_three = cosine[:, None, :]
    sin_three = sign * sine[:, None, :]
    turned = jnp.concatenate(
        [first * cos_three - second * sin_three, second * cos_three + first * sin_three], axis=-1
    )
    return turned.reshape(rows, -1)


def contract_rows(left, right):
    return lax.dot_general(
        left, right, (((0,), (0,)), ((), ())), preferred_element_type=jnp.float32
    )


def contract_cols(left, right):
    return lax.dot_general(
        left, right, (((1,), (1,)), ((), ())), preferred_element_type=jnp.float32
    )


def product(left, right):
    return jnp.dot(left, right, preferred_element_type=jnp.float32)


def rms_scale(values):
    return lax.rsqrt(jnp.mean(values * values, axis=1, keepdims=True) + EPS)


def per_device(
    tokens,
    query_weight,
    key_weight,
    value_weight,
    output_weight,
    gate_weight,
    up_weight,
    down_weight,
    attention_gain,
    feed_gain,
    doc_lengths,
    cotangent,
):
    half_type = jnp.bfloat16
    copies = (
        lax.all_gather(query_weight.astype(half_type), "dp", axis=0, tiled=True),
        lax.all_gather(key_weight.astype(half_type), "dp", axis=0, tiled=True),
        lax.all_gather(value_weight.astype(half_type), "dp", axis=0, tiled=True),
        lax.all_gather(output_weight.astype(half_type), "dp", axis=1, tiled=True),
        lax.all_gather(gate_weight.astype(half_type), "dp", axis=0, tiled=True),
        lax.all_gather(up_weight.astype(half_type), "dp", axis=0, tiled=True),
        lax.all_gather(down_weight.astype(half_type), "dp", axis=1, tiled=True),
        lax.all_gather(attention_gain.astype(half_type), "dp", axis=0, tiled=True),
        lax.all_gather(feed_gain.astype(half_type), "dp", axis=0, tiled=True),
    )
    (
        query_copy,
        key_copy,
        value_copy,
        output_copy,
        gate_copy,
        up_copy,
        down_copy,
        gain_first,
        gain_second,
    ) = copies
    gain_one = gain_first.astype(jnp.float32)
    gain_two = gain_second.astype(jnp.float32)
    own_rows = tokens.shape[0]
    total = own_rows * lax.axis_size("tensor")
    position, valid, allowed = group_layout(doc_lengths[0], total)
    cosine, sine = angle_tables(position)
    head_dim = HEAD_DIM
    local_heads = query_copy.shape[1] // head_dim
    local_kv = key_copy.shape[1] // head_dim
    per_kv = local_heads // local_kv
    scale = head_dim ** (-0.5)
    resid = tokens.astype(jnp.float32)
    scale_one = rms_scale(resid)
    normed_one = (resid * scale_one * gain_one).astype(half_type)
    rows_one = lax.all_gather(normed_one, "tensor", axis=0, tiled=True)
    queries = rotate(product(rows_one, query_copy), cosine, sine, 1.0).astype(half_type)
    keys = rotate(product(rows_one, key_copy), cosine, sine, 1.0).astype(half_type)
    values = product(rows_one, value_copy).astype(half_type)

    def head_scores(head):
        query_head = lax.dynamic_slice_in_dim(queries, head * head_dim, head_dim, 1)
        kv_start = head // per_kv * head_dim
        scores = jnp.where(allowed, scale * contract_cols(query_head, keys), NEG)
        return (query_head, keys, values, scores, kv_start)

    def forward_head(head, carry):
        mixed, logsum = carry
        _, _, value_head, scores, _ = head_scores(head)
        peak = jnp.max(scores, axis=1, keepdims=True)
        expo = jnp.exp(scores - peak)
        denom = jnp.sum(expo, axis=1, keepdims=True)
        probs = (expo / denom).astype(half_type)
        mixed = lax.dynamic_update_slice_in_dim(
            mixed, product(probs, value_head), head * head_dim, 1
        )
        logsum = lax.dynamic_update_slice_in_dim(
            logsum, (peak + jnp.log(denom)).reshape(1, total), head, 0
        )
        return (mixed, logsum)

    mixed, logsum = lax.fori_loop(
        0,
        local_heads,
        forward_head,
        (
            jnp.zeros((total, local_heads * head_dim), jnp.float32),
            jnp.zeros((local_heads, total), jnp.float32),
        ),
    )
    attended = (mixed * valid[:, None]).astype(half_type)
    middle = resid + lax.psum_scatter(
        product(attended, output_copy).astype(jnp.bfloat16),
        "tensor",
        scatter_dimension=0,
        tiled=True,
    ).astype(jnp.float32)
    scale_two = rms_scale(middle)
    normed_two = (middle * scale_two * gain_two).astype(half_type)
    rows_two = lax.all_gather(normed_two, "tensor", axis=0, tiled=True)
    gate = product(rows_two, gate_copy)
    upper = product(rows_two, up_copy)
    sigma = jax.nn.sigmoid(gate)
    swish = gate * sigma
    hidden = (swish * upper).astype(half_type)
    layer_out = (
        middle
        + lax.psum_scatter(
            product(hidden, down_copy).astype(jnp.bfloat16),
            "tensor",
            scatter_dimension=0,
            tiled=True,
        ).astype(jnp.float32)
    ).astype(half_type)
    grad_out = cotangent.astype(jnp.float32)
    piece = lax.all_gather(cotangent, "tensor", axis=0, tiled=True)
    grad_down = contract_rows(hidden, piece)
    grad_hidden = contract_cols(piece, down_copy)
    grad_down, grad_hidden = (grad_down, grad_hidden)
    grad_gate = (grad_hidden * upper * sigma * (1.0 + gate * (1.0 - sigma))).astype(half_type)
    grad_up = (grad_hidden * swish).astype(half_type)
    grad_gate_w = contract_rows(rows_two, grad_gate)
    grad_up_w = contract_rows(rows_two, grad_up)
    grad_normed_two = lax.psum_scatter(
        (contract_cols(grad_gate, gate_copy) + contract_cols(grad_up, up_copy)).astype(
            jnp.bfloat16
        ),
        "tensor",
        scatter_dimension=0,
        tiled=True,
    ).astype(jnp.float32)
    grad_gain_two = jnp.sum(grad_normed_two * middle * scale_two, axis=0)
    inner_two = grad_normed_two * gain_two
    grad_middle = (
        grad_out
        + scale_two * inner_two
        - middle * scale_two**3 * jnp.mean(inner_two * middle, axis=1, keepdims=True)
    )
    residual_send = grad_middle.astype(half_type)
    mixed_width = attended.shape[1]
    piece = lax.all_gather(residual_send, "tensor", axis=0, tiled=True)
    grad_output = contract_rows(attended, piece)
    grad_mixed = contract_cols(piece, output_copy)
    grad_output_w, grad_mixed = (grad_output, grad_mixed)
    grad_attended = grad_mixed.astype(half_type) * valid[:, None].astype(half_type)

    def backward_head(head, carry):
        grad_query, grad_key, grad_value = carry
        query_head, key_head, value_head, scores, kv_start = head_scores(head)
        lse_row = lax.dynamic_index_in_dim(logsum, head, 0, keepdims=False)
        probs = jnp.exp(scores - lse_row[:, None])
        grad_head = lax.dynamic_slice_in_dim(grad_attended, head * head_dim, head_dim, 1)
        value_term = contract_rows(probs.astype(half_type), grad_head)
        grad_probs = contract_cols(grad_head, value_head)
        grad_scores = (
            probs * (grad_probs - jnp.sum(probs * grad_probs, axis=1, keepdims=True))
        ).astype(half_type)
        query_term = scale * product(grad_scores, key_head)
        key_term = scale * contract_rows(grad_scores, query_head)
        grad_query = lax.dynamic_update_slice_in_dim(grad_query, query_term, head * head_dim, 1)
        grad_key = grad_key + key_term
        grad_value = grad_value + value_term
        return (grad_query, grad_key, grad_value)

    kv_width = local_kv * head_dim
    grad_query, grad_key, grad_value = lax.fori_loop(
        0,
        local_heads,
        backward_head,
        (
            jnp.zeros((total, mixed_width), jnp.float32),
            jnp.zeros((total, kv_width), jnp.float32),
            jnp.zeros((total, kv_width), jnp.float32),
        ),
    )
    grad_query = rotate(grad_query, cosine, sine, -1.0).astype(half_type)
    grad_key = rotate(grad_key, cosine, sine, -1.0).astype(half_type)
    grad_value = grad_value.astype(half_type)
    grad_query_w = contract_rows(rows_one, grad_query)
    grad_key_w = contract_rows(rows_one, grad_key)
    grad_value_w = contract_rows(rows_one, grad_value)
    grad_normed_one = lax.psum_scatter(
        (
            contract_cols(grad_query, query_copy)
            + contract_cols(grad_key, key_copy)
            + contract_cols(grad_value, value_copy)
        ).astype(jnp.bfloat16),
        "tensor",
        scatter_dimension=0,
        tiled=True,
    ).astype(jnp.float32)
    grad_gain_one = jnp.sum(grad_normed_one * resid * scale_one, axis=0)
    inner_one = grad_normed_one * gain_one
    input_grad = (
        grad_middle
        + scale_one * inner_one
        - resid * scale_one**3 * jnp.mean(inner_one * resid, axis=1, keepdims=True)
    )
    every_sum = (
        lax.psum_scatter(
            grad_query_w.astype(jnp.bfloat16), "dp", scatter_dimension=0, tiled=True
        ).astype(jnp.float32),
        lax.psum_scatter(
            grad_key_w.astype(jnp.bfloat16), "dp", scatter_dimension=0, tiled=True
        ).astype(jnp.float32),
        lax.psum_scatter(
            grad_value_w.astype(jnp.bfloat16), "dp", scatter_dimension=0, tiled=True
        ).astype(jnp.float32),
        lax.psum_scatter(
            grad_output_w.astype(jnp.bfloat16), "dp", scatter_dimension=1, tiled=True
        ).astype(jnp.float32),
        lax.psum_scatter(
            grad_gate_w.astype(jnp.bfloat16), "dp", scatter_dimension=0, tiled=True
        ).astype(jnp.float32),
        lax.psum_scatter(
            grad_up_w.astype(jnp.bfloat16), "dp", scatter_dimension=0, tiled=True
        ).astype(jnp.float32),
        lax.psum_scatter(
            grad_down.astype(jnp.bfloat16), "dp", scatter_dimension=1, tiled=True
        ).astype(jnp.float32),
        lax.psum_scatter(
            grad_gain_one.astype(jnp.bfloat16), "dp", scatter_dimension=0, tiled=True
        ).astype(jnp.float32),
        lax.psum_scatter(
            grad_gain_two.astype(jnp.bfloat16), "dp", scatter_dimension=0, tiled=True
        ).astype(jnp.float32),
    )
    (
        query_sum,
        key_sum,
        value_sum,
        output_sum,
        gate_sum,
        up_sum,
        down_sum,
        gain_one_sum,
        gain_two_sum,
    ) = every_sum
    gain_one_total, gain_two_total = lax.psum((gain_one_sum, gain_two_sum), "tensor")
    return (
        layer_out,
        input_grad,
        query_sum,
        key_sum,
        value_sum,
        output_sum,
        gate_sum,
        up_sum,
        down_sum,
        gain_one_total,
        gain_two_total,
    )


def solution(mesh):
    placed = (
        P(("dp", "tensor"), None),
        P("dp", "tensor"),
        P("dp", "tensor"),
        P("dp", "tensor"),
        P("tensor", "dp"),
        P("dp", "tensor"),
        P("dp", "tensor"),
        P("tensor", "dp"),
        P("dp"),
        P("dp"),
        P("dp", None),
        P(("dp", "tensor"), None),
    )
    return jax.shard_map(
        per_device,
        mesh=mesh,
        in_specs=placed,
        out_specs=(
            P(("dp", "tensor"), None),
            P(("dp", "tensor"), None),
            P("dp", "tensor"),
            P("dp", "tensor"),
            P("dp", "tensor"),
            P("tensor", "dp"),
            P("dp", "tensor"),
            P("dp", "tensor"),
            P("tensor", "dp"),
            P("dp"),
            P("dp"),
        ),
        check_vma=False,
    )
```

profile of v0, /device:TPU:0, one launch (start us, length us, event | category | flops | bytes accessed | tf_op | source)
XLA Modules:
  0.0 1437.0 jit_solution(2010027626891738578)
XLA Ops:
  9.9 22.2 %all-gather = bf16[8,1,256]{2,1,0:T(2,128)(2,1)S(1)} all-gather(bf16[1,1,256]{2,1,0:T(2,128)(2,1)S(1)} %reshape.289), channel_id=1, replica_groups=mesh['dp'=8,'tensor'=4] {'dp'}, dimensions={0}, use_global_device_ids=true | all-gather | bytes 4608 | tf_op jit(solution)/shard_map/all_gather | solution.py:93
  37.9 31.6 %all_gather.42 = bf16[2048,64]{0,1:T(8,128)(2,1)S(1)} all-gather(bf16[256,64]{0,1:T(8,128)(2,1)S(1)} %convert_element_type.223), channel_id=1, replica_groups=mesh['dp'=8,'tensor'=4] {'dp'}, dimensions={0}, use_global_device_ids=true | all-gather | bytes 294912 | tf_op jit(solution)/shard_map/all_gather | solution.py:87
  69.6 32.7 %all_gather.43 = bf16[2048,64]{0,1:T(8,128)(2,1)} all-gather(bf16[256,64]{0,1:T(8,128)(2,1)S(1)} %convert_element_type.225), channel_id=1, replica_groups=mesh['dp'=8,'tensor'=4] {'dp'}, dimensions={0}, use_global_device_ids=true | all-gather | bytes 294912 | tf_op jit(solution)/shard_map/all_gather | solution.py:88
  117.6 36.6 %while.34 = (s32[]{:T(128)}, f32[768,512]{0,1:T(8,128)}, f32[8,768]{1,0:T(8,128)}, bf16[768,512]{1,0:T(8,128)(2,1)}, bf16[768,64]{1,0:T(8,128)(2,1)S(1)}, /*inde...) while((s32[]{:T(128)}, f32[768,512]{0,1:T(8,128)}, ...), condition=%wide.region_7.8_spmd.clone, body=%wide.region_4.7_spmd.clone.sunk | while | flops 157482240 | bytes 7811239 | solution.py:147
  162.3 16.3 %all-gather.1 = bf16[8,1,256]{2,1,0:T(2,128)(2,1)S(1)} all-gather(bf16[1,1,256]{2,1,0:T(2,128)(2,1)S(1)} %reshape.291), channel_id=1, replica_groups=mesh['dp'=8,'tensor'=4] {'dp'}, dimensions={0}, use_global_device_ids=true | all-gather | bytes 4608 | tf_op jit(solution)/shard_map/all_gather | solution.py:94
  178.6 16.8 %reduce-scatter.12.cloned.1.call-done = bf16[192,2048]{1,0:T(8,128)(2,1)} async-done(((bf16[768,2048]{1,0:T(8,128)(2,1)}), bf16[192,2048]{1,0:T(8,128)(2,1)}) %reduce-scatter.12.cloned.1.call-update) | async-done | bytes 786448 | tf_op jit(solution)/shard_map/reduce_scatter | solution.py:157
  203.0 87.9 %all-gather.20.cloned.1.call-done = bf16[2048,1408]{1,0:T(8,128)(2,1)} async-done(((bf16[256,1408]{1,0:T(8,128)(2,1)}), bf16[2048,1408]{1,0:T(8,128)(2,1)}) %all-gather.20.cloned.1.call-update) | async-done | bytes 5767184 | tf_op jit(solution)/shard_map/all_gather | solution.py:90
  290.9 28.8 %all-gather.18.cloned.1.call-done = bf16[768,2048]{1,0:T(8,128)(2,1)} async-done(((bf16[192,2048]{1,0:T(8,128)(2,1)}), bf16[768,2048]{1,0:T(8,128)(2,1)}) %all-gather.18.cloned.1.call-update) | async-done | bytes 3145744 | tf_op jit(solution)/shard_map/all_gather | solution.py:165
  329.4 86.0 %all-gather.22.cloned.1.call-done = bf16[2048,1408]{1,0:T(8,128)(2,1)} async-done(((bf16[256,1408]{1,0:T(8,128)(2,1)}), bf16[2048,1408]{1,0:T(8,128)(2,1)}) %all-gather.22.cloned.1.call-update) | async-done | bytes 5767184 | tf_op jit(solution)/shard_map/all_gather | solution.py:91
  425.1 18.7 %all-gather.26.cloned.1.call-done = bf16[768,2048]{1,0:T(8,128)(2,1)} async-done(((bf16[192,2048]{1,0:T(8,128)(2,1)}), bf16[768,2048]{1,0:T(8,128)(2,1)}) %all-gather.26.cloned.1.call-update) | async-done | bytes 3145744 | tf_op jit(solution)/shard_map/all_gather | solution.py:181
  443.8 96.4 %all-gather.24.cloned.1.call-done = bf16[1408,2048]{1,0:T(8,128)(2,1)} async-done(((bf16[1408,256]{1,0:T(8,128)(2,1)}), bf16[1408,2048]{1,0:T(8,128)(2,1)}) %all-gather.24.cloned.1.call-update) | async-done | bytes 5767184 | tf_op jit(solution)/shard_map/all_gather | solution.py:92
  540.2 12.8 multiply_convert_fusion.1
  568.4 36.2 %reduce-scatter.16.cloned.1.call-done = bf16[192,2048]{1,0:T(8,128)(2,1)} async-done(((bf16[768,2048]{1,0:T(8,128)(2,1)}), bf16[192,2048]{1,0:T(8,128)(2,1)}) %reduce-scatter.16.cloned.1.call-update) | async-done | bytes 786448 | tf_op jit(solution)/shard_map/reduce_scatter | solution.py:189
  609.4 27.8 %all-gather.28.cloned.1.call-done = bf16[768,2048]{1,0:T(8,128)(2,1)} async-done(((bf16[192,2048]{1,0:T(8,128)(2,1)}), bf16[768,2048]{1,0:T(8,128)(2,1)}) %all-gather.28.cloned.1.call-update) | async-done | bytes 3145744 | tf_op jit(solution)/shard_map/all_gather | solution.py:206
  643.7 89.2 %while.35 = (s32[]{:T(128)}, f32[768,512]{0,1:T(8,128)}, f32[768,64]{0,1:T(8,128)}, f32[768,64]{0,1:T(8,128)}, bf16[768,512]{1,0:T(8,128)(2,1)}, /*index=5*/bf16...) while((s32[]{:T(128)}, f32[768,512]{0,1:T(8,128)}, ...), condition=%wide.region_15.16_spmd.clone, body=%wide.region_13.15_spmd.clone.sunk | while | flops 384859392 | bytes 21578108 | solution.py:231
  801.5 110.8 %reduce-scatter.28.cloned.1.call-done = bf16[256,1408]{1,0:T(8,128)(2,1)} async-done(((bf16[2048,1408]{1,0:T(8,128)(2,1)}), bf16[256,1408]{1,0:T(8,128)(2,1)}) %reduce-scatter.28.cloned.1.call-update) | async-done | bytes 720912 | tf_op jit(solution)/shard_map/reduce_scatter | solution.py:277
  914.6 111.0 %reduce-scatter.30.cloned.1.call-done = bf16[256,1408]{1,0:T(8,128)(2,1)} async-done(((bf16[2048,1408]{1,0:T(8,128)(2,1)}), bf16[256,1408]{1,0:T(8,128)(2,1)}) %reduce-scatter.30.cloned.1.call-update) | async-done | bytes 720912 | tf_op jit(solution)/shard_map/reduce_scatter | solution.py:280
  1027.9 62.9 %reduce-scatter.24.cloned.1.call-done = bf16[256,64]{0,1:T(8,128)(2,1)} async-done(((bf16[2048,64]{0,1:T(8,128)(2,1)}), bf16[256,64]{0,1:T(8,128)(2,1)}) %reduce-scatter.24.cloned.1.call-update) | async-done | bytes 32784 | tf_op jit(solution)/shard_map/reduce_scatter | solution.py:271
  1092.3 111.5 %reduce-scatter.32.cloned.1.call-done = bf16[1408,256]{1,0:T(8,128)(2,1)} async-done(((bf16[1408,2048]{1,0:T(8,128)(2,1)}), bf16[1408,256]{1,0:T(8,128)(2,1)}) %reduce-scatter.32.cloned.1.call-update) | async-done | bytes 720912 | tf_op jit(solution)/shard_map/reduce_scatter | solution.py:283
  1206.1 69.1 %reduce-scatter.26.cloned.1.call-done = bf16[512,256]{1,0:T(8,128)(2,1)} async-done(((bf16[512,2048]{1,0:T(8,128)(2,1)}), bf16[512,256]{1,0:T(8,128)(2,1)}) %reduce-scatter.26.cloned.1.call-update) | async-done | bytes 262160 | tf_op jit(solution)/shard_map/reduce_scatter | solution.py:274
  1277.0 68.5 %reduce-scatter.20.cloned.1.call-done = bf16[256,512]{1,0:T(8,128)(2,1)} async-done(((bf16[2048,512]{1,0:T(8,128)(2,1)}), bf16[256,512]{1,0:T(8,128)(2,1)}) %reduce-scatter.20.cloned.1.call-update) | async-done | bytes 262160 | tf_op jit(solution)/shard_map/reduce_scatter | solution.py:265
  1347.3 37.7 %reduce-scatter.18.cloned.1.call-done = bf16[192,2048]{1,0:T(8,128)(2,1)} async-done(((bf16[768,2048]{1,0:T(8,128)(2,1)}), bf16[192,2048]{1,0:T(8,128)(2,1)}) %reduce-scatter.18.cloned.1.call-update) | async-done | bytes 786448 | tf_op jit(solution)/shard_map/reduce_scatter | solution.py:247
  1386.7 21.6 %all-reduce.3 = (bf16[2048]{0:T(1024)(128)(2,1)S(1)}, bf16[2048]{0:T(1024)(128)(2,1)S(1)}) all-reduce(bf16[2048]{0:T(1024)(128)(2,1)S(1)} %get-tuple-element.435, bf16[2048]{0:T(1024)(128)(2,1)S(1)} %copy-done.32), channel_id=13, replica_groups=mesh['dp'=8,'tensor'=4] {'dp'}, use_global_device_ids=true, to_apply=%region_26.27.clone | all-reduce | flops 4096 | bytes 16384
  1415.1 10.6 reduce-scatter.14.cloned.1.call-done
  (419 shorter events, 302.2 us)
Async XLA Ops:
  7.2 96.8 %all-gather.14.cloned.1.call-start = ((), (), s32[]{:S(2)}) async-start(), calls=%async_computation.12 | async-start | bytes 2359296 | tf_op jit(solution)/shard_map/all_gather | solution.py:86
  9.2 94.9 %all-gather.12.cloned.1.call-start = ((), (), s32[]{:S(2)}) async-start(), calls=%async_computation.11 | async-start | bytes 3932160 | tf_op jit(solution)/shard_map/all_gather | solution.py:121
  35.3 118.9 %all-gather.16.cloned.1.call-start = ((), (), s32[]{:S(2)}) async-start(), calls=%async_computation.13 | async-start | bytes 2359296 | tf_op jit(solution)/shard_map/all_gather | solution.py:89
  36.2 159.2 %reduce-scatter.12.cloned.1.call-start = ((), (), s32[]{:S(2)}) async-start(), calls=%async_computation.14 | async-start | bytes 3932160 | tf_op jit(solution)/shard_map/reduce_scatter | solution.py:157
  159.9 131.0 %all-gather.20.cloned.1.call-start = ((), (), s32[]{:S(2)}) async-start(), calls=%async_computation.16 | async-start | bytes 6488064 | tf_op jit(solution)/shard_map/all_gather | solution.py:90
  162.2 157.6 %all-gather.18.cloned.1.call-start = ((), (), s32[]{:S(2)}) async-start(), calls=%async_computation.15 | async-start | bytes 3932160 | tf_op jit(solution)/shard_map/all_gather | solution.py:165
  196.9 410.1 %copy-start.37 = (f32[192]{0:T(256)}, f32[192]{0:T(256)S(1)}, u32[]{:S(2)}) copy-start(f32[192]{0:T(256)S(1)} %get-tuple-element.497) | copy-start | bytes 2308
  199.2 216.2 %all-gather.22.cloned.1.call-start = ((), (), s32[]{:S(2)}) async-start(), calls=%async_computation.17 | async-start | bytes 6488064 | tf_op jit(solution)/shard_map/all_gather | solution.py:91
  200.2 243.6 %all-gather.26.cloned.1.call-start = ((), (), s32[]{:S(2)}) async-start(), calls=%async_computation.20 | async-start | bytes 3932160 | tf_op jit(solution)/shard_map/all_gather | solution.py:181
  201.0 339.2 %all-gather.24.cloned.1.call-start = ((), (), s32[]{:S(2)}) async-start(), calls=%async_computation.18 | async-start | bytes 6488064 | tf_op jit(solution)/shard_map/all_gather | solution.py:92
  202.5 402.1 %reduce-scatter.16.cloned.1.call-start = ((), (), s32[]{:S(2)}) async-start(), calls=%async_computation.21 | async-start | bytes 3932160 | tf_op jit(solution)/shard_map/reduce_scatter | solution.py:189
  568.3 68.9 %all-gather.28.cloned.1.call-start = ((), (), s32[]{:S(2)}) async-start(), calls=%async_computation.22 | async-start | bytes 3932160 | tf_op jit(solution)/shard_map/all_gather | solution.py:206
  608.6 191.6 %reduce-scatter.22.cloned.1.call-start = ((), (), s32[]{:S(2)}) async-start(), calls=%async_computation.25 | async-start | bytes 294912 | tf_op jit(solution)/shard_map/reduce_scatter | solution.py:268
  737.8 174.5 %reduce-scatter.28.cloned.1.call-start = ((), (), s32[]{:S(2)}) async-start(), calls=%async_computation.28 | async-start | bytes 6488064 | tf_op jit(solution)/shard_map/reduce_scatter | solution.py:277
  746.4 279.2 %reduce-scatter.30.cloned.1.call-start = ((), (), s32[]{:S(2)}) async-start(), calls=%async_computation.29 | async-start | bytes 6488064 | tf_op jit(solution)/shard_map/reduce_scatter | solution.py:280
  755.0 335.9 %reduce-scatter.24.cloned.1.call-start = ((), (), s32[]{:S(2)}) async-start(), calls=%async_computation.26 | async-start | bytes 294912 | tf_op jit(solution)/shard_map/reduce_scatter | solution.py:271
  758.3 445.5 %reduce-scatter.32.cloned.1.call-start = ((), (), s32[]{:S(2)}) async-start(), calls=%async_computation.30 | async-start | bytes 6488064 | tf_op jit(solution)/shard_map/reduce_scatter | solution.py:283
  768.2 507.0 %reduce-scatter.26.cloned.1.call-start = ((), (), s32[]{:S(2)}) async-start(), calls=%async_computation.27 | async-start | bytes 2359296 | tf_op jit(solution)/shard_map/reduce_scatter | solution.py:274
  774.5 571.0 %reduce-scatter.20.cloned.1.call-start = ((), (), s32[]{:S(2)}) async-start(), calls=%async_computation.24 | async-start | bytes 2359296 | tf_op jit(solution)/shard_map/reduce_scatter | solution.py:265
  781.1 603.9 %reduce-scatter.18.cloned.1.call-start = ((), (), s32[]{:S(2)}) async-start(), calls=%async_computation.23 | async-start | bytes 3932160 | tf_op jit(solution)/shard_map/reduce_scatter | solution.py:247
  787.6 638.1 %reduce-scatter.14.cloned.1.call-start = ((), (), s32[]{:S(2)}) async-start(), calls=%async_computation.19 | async-start | bytes 3932160 | tf_op jit(solution)/shard_map/reduce_scatter | solution.py:173
  1027.9 357.1 %copy-start.4 = (bf16[192,2048]{1,0:T(8,128)(2,1)S(1)}, bf16[192,2048]{1,0:T(8,128)(2,1)}, u32[]{:S(2)}) copy-start(bf16[192,2048]{1,0:T(8,128)(2,1)} %param.16) | copy-start | bytes 2359300
  1027.9 357.1 %copy-start.29 = (f32[8,1,256]{2,1,0:T(1,128)S(1)}, f32[8,1,256]{2,1,0:T(1,128)}, u32[]{:S(2)}) copy-start(f32[8,1,256]{2,1,0:T(1,128)} %copy-done.28) | copy-start | bytes 24580
  1027.9 357.1 %copy-start.36 = (f32[192]{0:T(256)S(1)}, f32[192]{0:T(256)}, u32[]{:S(2)}) copy-start(f32[192]{0:T(256)} %copy-done.35) | copy-start | bytes 2308
  (91 other events, 3036.7 us)
Sparse Core Ops, SparseCore 0:
  10.7 54.2 all-gather.13
  67.2 28.0 all-gather.11
  97.9 51.0 all-gather.15
  160.0 35.3 reduce-scatter.11
  198.2 92.6 all-gather.19
  293.0 26.7 all-gather.17
  322.7 92.6 all-gather.21
  417.0 26.7 all-gather.25
  446.6 93.5 all-gather.23
  568.4 36.1 reduce-scatter.15
  608.7 28.5 all-gather.27
  737.9 61.6 reduce-scatter.21
  803.3 108.9 reduce-scatter.27
  915.8 109.7 reduce-scatter.29
  1029.4 61.4 reduce-scatter.23
  1094.4 109.3 reduce-scatter.31
  1207.2 67.9 reduce-scatter.25
  1278.6 66.8 reduce-scatter.19
  1348.0 36.9 reduce-scatter.17
  1387.6 38.0 reduce-scatter.13
where the time goes:
time: 1450 us; the launch traced here: 1440 us
  waiting for transfers between devices  982 us (68%)
  matrix products  223 us (15%)
  blocking collectives  131 us (9%)
  other arithmetic  49.8 us (3%)
  local copies, waits for them, and re-layouts  32.8 us (2%)
  between operations  16 us (1%)
    reduce_scatter x1, waiting for transfers between devices, per_device(): lax.psum_scatter(grad_down.astype(jnp.bfloat16), 'dp', scatter_dimension=...  112 us
    reduce_scatter x1, waiting for transfers between devices, per_device(): lax.psum_scatter(grad_up_w.astype(jnp.bfloat16), 'dp', scatter_dimension=...  111 us
    reduce_scatter x1, waiting for transfers between devices, per_device(): lax.psum_scatter(grad_gate_w.astype(jnp.bfloat16), 'dp', scatter_dimensio...  111 us
    all_gather x1, waiting for transfers between devices, per_device(): lax.all_gather(down_weight.astype(half_type), 'dp', axis=1, tiled=True)  96.4 us
    all_gather x1, waiting for transfers between devices, per_device(): lax.all_gather(gate_weight.astype(half_type), 'dp', axis=0, tiled=True)  87.9 us
    all_gather x1, waiting for transfers between devices, per_device(): lax.all_gather(up_weight.astype(half_type), 'dp', axis=0, tiled=True)  86 us
    dot_general x31, matrix products, contract_cols(): lax.dot_general(left, right, (((1,), (1,)), ((), ())), preferred_element_...  78.4 us
    dot_general x23, matrix products, contract_rows(): lax.dot_general(left, right, (((0,), (0,)), ((), ())), preferred_element_...  76.8 us
  transfers between devices with their start and end apart: 20, of which 16 were waited for; matrix products, arithmetic and copies ran while one was open for 11% of the time, Pallas kernels for 0%

commit v1 on v0

v1 whole, which is shorter than its diff:
```python
import math

import jax
import jax.numpy as jnp
from jax import lax
from jax.sharding import PartitionSpec as P

HEAD_DIM = 64


EPS = 1e-05
NEG = -1e30
HALF = jnp.bfloat16
FULL = jnp.float32


def group_layout(counts, total):
    ends = jnp.cumsum(counts)
    starts = ends - counts
    place = jnp.arange(total, dtype=jnp.int32)
    segment = jnp.sum((place[:, None] >= ends[None, :]).astype(jnp.int32), axis=1)
    bounds = jnp.concatenate([starts, ends[-1:]])
    slots = jnp.arange(bounds.shape[0], dtype=jnp.int32)
    begin = jnp.sum(jnp.where(segment[:, None] == slots[None, :], bounds[None, :], 0), axis=1)
    position = (place - begin).astype(FULL)
    valid = (place < ends[-1]).astype(FULL)
    allowed = (segment[:, None] == segment[None, :]) & (place[None, :] <= place[:, None])
    return (position, valid, allowed)


def angle_tables(position):
    half = HEAD_DIM // 2
    freq = jnp.exp(jnp.arange(half, dtype=FULL) * (-2.0 * math.log(10000.0) / HEAD_DIM))
    angle = position[:, None] * freq[None, :]
    return (jnp.cos(angle), jnp.sin(angle))


def rotate(values, cosine, sine, sign):
    rows = values.shape[0]
    split = values.reshape(rows, -1, HEAD_DIM)
    half = HEAD_DIM // 2
    first = split[..., :half]
    second = split[..., half:]
    cos_three = cosine[:, None, :]
    sin_three = sign * sine[:, None, :]
    turned = jnp.concatenate(
        [first * cos_three - second * sin_three, second * cos_three + first * sin_three], axis=-1
    )
    return turned.reshape(rows, -1)


def contract_rows(left, right):
    return lax.dot_general(left, right, (((0,), (0,)), ((), ())), preferred_element_type=FULL)


def contract_cols(left, right):
    return lax.dot_general(left, right, (((1,), (1,)), ((), ())), preferred_element_type=FULL)


def product(left, right):
    return jnp.dot(left, right, preferred_element_type=FULL)


def rms_scale(values):
    return lax.rsqrt(jnp.mean(values * values, axis=1, keepdims=True) + EPS)


def ring_order(count):
    return list(range(0, count, 2)) + list(range(count - 1, 0, -2))


class Ring:
    def __init__(self, count):
        self.count = count
        self.half = count // 2
        self.order = ring_order(count)
        self.up = [(self.order[i], self.order[(i + 1) % count]) for i in range(count)]
        self.down = [(b, a) for a, b in self.up]
        place = [0] * count
        for spot, member in enumerate(self.order):
            place[member] = spot
        here = jnp.asarray(place, jnp.int32)[lax.axis_index("dp")]
        self.offsets = [0]
        for step in range(1, self.half):
            self.offsets += [-step, step]
        self.offsets.append(self.half)
        order = jnp.asarray(self.order, jnp.int32)
        self.members = [order[(here + offset) % count] for offset in self.offsets]

    def shuffle(self, values):
        width = values.shape[1] // self.count
        return jnp.concatenate(
            [lax.dynamic_slice_in_dim(values, m * width, width, 1) for m in self.members], axis=1
        )

    def unshuffle(self, values):
        width = values.shape[1] // self.count
        out = jnp.zeros_like(values)
        for slot, member in enumerate(self.members):
            piece = values[:, slot * width : (slot + 1) * width]
            out = lax.dynamic_update_slice_in_dim(out, piece, member * width, 1)
        return out

    def gather(self, shard):
        blocks = [shard]
        above = below = shard
        for _ in range(1, self.half):
            above = lax.ppermute(above, "dp", self.up)
            below = lax.ppermute(below, "dp", self.down)
            blocks += [above, below]
        cut = shard.shape[0] // 2
        upper = lax.ppermute(above[:cut], "dp", self.up)
        lower = lax.ppermute(below[cut:], "dp", self.down)
        blocks.append(jnp.concatenate([upper, lower], axis=0))
        return blocks

    def reduce(self, part):
        far = part(self.count - 1)
        cut = far.shape[0] // 2
        above = lax.ppermute(far[:cut].astype(HALF), "dp", self.up).astype(FULL)
        below = lax.ppermute(far[cut:].astype(HALF), "dp", self.down).astype(FULL)
        for step in range(self.half - 1, 0, -1):
            top = part(2 * step)
            low = part(2 * step - 1)
            if step == self.half - 1:
                top = jnp.concatenate([top[:cut] + above, top[cut:]], axis=0)
                low = jnp.concatenate([low[:cut], low[cut:] + below], axis=0)
            else:
                top = top + above
                low = low + below
            above = lax.ppermute(top.astype(HALF), "dp", self.up).astype(FULL)
            below = lax.ppermute(low.astype(HALF), "dp", self.down).astype(FULL)
        return part(0) + above + below


def beside(index):
    return [(i, i ^ index) for i in range(4)]


def gather_rows(rows):
    mine = lax.axis_index("tensor")
    count = rows.shape[0]
    first = lax.ppermute(rows, "tensor", beside(2))
    pieces = (
        (0, rows),
        (1, lax.ppermute(rows, "tensor", beside(1))),
        (2, first),
        (3, lax.ppermute(first, "tensor", beside(1))),
    )
    out = jnp.zeros((4 * count, rows.shape[1]), rows.dtype)
    for index, piece in pieces:
        out = lax.dynamic_update_slice_in_dim(out, piece, (mine ^ index) * count, 0)
    return out


def scatter_rows(values):
    mine = lax.axis_index("tensor")
    values = values.astype(HALF)
    count = values.shape[0] // 4

    def piece(index):
        return lax.dynamic_slice_in_dim(values, (mine ^ index) * count, count, 0)

    across = lax.ppermute(piece(3), "tensor", beside(1)).astype(FULL)
    near = lax.ppermute(piece(1), "tensor", beside(1)).astype(FULL)
    send = (piece(2).astype(FULL) + across).astype(HALF)
    far = lax.ppermute(send, "tensor", beside(2)).astype(FULL)
    return piece(0).astype(FULL) + near + far


def per_device(
    tokens,
    query_weight,
    key_weight,
    value_weight,
    output_weight,
    gate_weight,
    up_weight,
    down_weight,
    attention_gain,
    feed_gain,
    doc_lengths,
    cotangent,
):
    ring = Ring(lax.axis_size("dp"))
    own_rows, width = tokens.shape
    block = query_weight.shape[0]
    tokens = ring.shuffle(tokens)
    cotangent = ring.shuffle(cotangent)

    inner = query_weight.shape[1]
    kv_width = key_weight.shape[1]
    gains = jnp.stack([attention_gain, feed_gain]).astype(HALF)
    gains = jnp.pad(gains, ((0, 30), (0, inner + 2 * kv_width - block)))
    first_shard = jnp.concatenate(
        [
            jnp.concatenate([query_weight, key_weight, value_weight], axis=1).astype(HALF),
            gains,
        ],
        axis=0,
    )
    first_blocks = ring.gather(first_shard)
    first_copy = jnp.concatenate([b[:block] for b in first_blocks], axis=0)
    gain_one = jnp.concatenate([b[block, :block] for b in first_blocks]).astype(FULL)
    gain_two = jnp.concatenate([b[block + 1, :block] for b in first_blocks]).astype(FULL)
    output_copy = jnp.concatenate(ring.gather(output_weight.astype(HALF)), axis=1)
    gate_copy = jnp.concatenate(ring.gather(gate_weight.astype(HALF)), axis=0)
    up_copy = jnp.concatenate(ring.gather(up_weight.astype(HALF)), axis=0)
    down_copy = jnp.concatenate(ring.gather(down_weight.astype(HALF)), axis=1)

    total = own_rows * lax.axis_size("tensor")
    position, valid, allowed = group_layout(doc_lengths[0], total)
    cosine, sine = angle_tables(position)
    head_dim = HEAD_DIM
    local_heads = inner // head_dim
    scale = head_dim ** (-0.5)
    resid = tokens.astype(FULL)
    scale_one = rms_scale(resid)
    rows_in = gather_rows(tokens).astype(FULL)
    rows_one = (rows_in * rms_scale(rows_in) * gain_one).astype(HALF)
    joined = product(rows_one, first_copy)
    queries = rotate(joined[:, :inner], cosine, sine, 1.0).astype(HALF)
    keys = rotate(joined[:, inner : inner + kv_width], cosine, sine, 1.0).astype(HALF)
    values = joined[:, inner + kv_width :].astype(HALF)

    def head_scores(head):
        query_head = lax.dynamic_slice_in_dim(queries, head * head_dim, head_dim, 1)
        scores = jnp.where(allowed, scale * contract_cols(query_head, keys), NEG)
        return (query_head, scores)

    def forward_head(head, carry):
        mixed, logsum = carry
        _, scores = head_scores(head)
        peak = jnp.max(scores, axis=1, keepdims=True)
        expo = jnp.exp(scores - peak)
        denom = jnp.sum(expo, axis=1, keepdims=True)
        probs = (expo / denom).astype(HALF)
        mixed = lax.dynamic_update_slice_in_dim(
            mixed, product(probs, values), head * head_dim, 1
        )
        logsum = lax.dynamic_update_slice_in_dim(
            logsum, (peak + jnp.log(denom)).reshape(1, total), head, 0
        )
        return (mixed, logsum)

    mixed, logsum = lax.fori_loop(
        0,
        local_heads,
        forward_head,
        (
            jnp.zeros((total, local_heads * head_dim), FULL),
            jnp.zeros((local_heads, total), FULL),
        ),
    )
    attended = (mixed * valid[:, None]).astype(HALF)
    middle = resid + scatter_rows(product(attended, output_copy))
    scale_two = rms_scale(middle)
    rows_two = gather_rows((middle * scale_two * gain_two).astype(HALF))
    gate = product(rows_two, gate_copy)
    upper = product(rows_two, up_copy)
    sigma = jax.nn.sigmoid(gate)
    swish = gate * sigma
    hidden = (swish * upper).astype(HALF)
    layer_out = (middle + scatter_rows(product(hidden, down_copy))).astype(HALF)

    grad_out = cotangent.astype(FULL)
    grad_rows = gather_rows(cotangent)
    down_sum = ring.reduce(
        lambda slot: contract_rows(hidden, grad_rows[:, slot * block : (slot + 1) * block])
    )
    grad_hidden = contract_cols(grad_rows, down_copy)
    grad_gate = (grad_hidden * upper * sigma * (1.0 + gate * (1.0 - sigma))).astype(HALF)
    grad_up = (grad_hidden * swish).astype(HALF)
    gate_sum = ring.reduce(
        lambda slot: contract_rows(rows_two[:, slot * block : (slot + 1) * block], grad_gate)
    )
    up_sum = ring.reduce(
        lambda slot: contract_rows(rows_two[:, slot * block : (slot + 1) * block], grad_up)
    )
    grad_normed_two = scatter_rows(
        contract_cols(grad_gate, gate_copy) + contract_cols(grad_up, up_copy)
    )
    grad_gain_two = jnp.sum(grad_normed_two * middle * scale_two, axis=0)
    inner_two = grad_normed_two * gain_two
    grad_middle = (
        grad_out
        + scale_two * inner_two
        - middle * scale_two**3 * jnp.mean(inner_two * middle, axis=1, keepdims=True)
    )
    middle_rows = gather_rows(grad_middle.astype(HALF))
    output_sum = ring.reduce(
        lambda slot: contract_rows(attended, middle_rows[:, slot * block : (slot + 1) * block])
    )
    grad_mixed = contract_cols(middle_rows, output_copy)
    grad_attended = grad_mixed.astype(HALF) * valid[:, None].astype(HALF)

    def backward_head(head, carry):
        grad_query, grad_key, grad_value = carry
        query_head, scores = head_scores(head)
        lse_row = lax.dynamic_index_in_dim(logsum, head, 0, keepdims=False)
        probs = jnp.exp(scores - lse_row[:, None])
        grad_head = lax.dynamic_slice_in_dim(grad_attended, head * head_dim, head_dim, 1)
        value_term = contract_rows(probs.astype(HALF), grad_head)
        grad_probs = contract_cols(grad_head, values)
        grad_scores = (
            probs * (grad_probs - jnp.sum(probs * grad_probs, axis=1, keepdims=True))
        ).astype(HALF)
        query_term = scale * product(grad_scores, keys)
        key_term = scale * contract_rows(grad_scores, query_head)
        grad_query = lax.dynamic_update_slice_in_dim(grad_query, query_term, head * head_dim, 1)
        grad_key = grad_key + key_term
        grad_value = grad_value + value_term
        return (grad_query, grad_key, grad_value)

    grad_query, grad_key, grad_value = lax.fori_loop(
        0,
        local_heads,
        backward_head,
        (
            jnp.zeros((total, inner), FULL),
            jnp.zeros((total, kv_width), FULL),
            jnp.zeros((total, kv_width), FULL),
        ),
    )
    grad_joined = jnp.concatenate(
        [
            rotate(grad_query, cosine, sine, -1.0).astype(HALF),
            rotate(grad_key, cosine, sine, -1.0).astype(HALF),
            grad_value.astype(HALF),
        ],
        axis=1,
    )
    first_sum = ring.reduce(
        lambda slot: contract_rows(rows_one[:, slot * block : (slot + 1) * block], grad_joined)
    )
    grad_normed_one = scatter_rows(contract_cols(grad_joined, first_copy))
    grad_gain_one = jnp.sum(grad_normed_one * resid * scale_one, axis=0)
    inner_one = grad_normed_one * gain_one
    input_grad = (
        grad_middle
        + scale_one * inner_one
        - resid * scale_one**3 * jnp.mean(inner_one * resid, axis=1, keepdims=True)
    )
    both = jnp.stack([grad_gain_one, grad_gain_two])
    gain_sum = ring.reduce(lambda slot: both[:, slot * block : (slot + 1) * block])
    gain_sum = lax.psum(gain_sum, "tensor")
    return (
        ring.unshuffle(layer_out),
        ring.unshuffle(input_grad),
        first_sum[:, :inner],
        first_sum[:, inner : inner + kv_width],
        first_sum[:, inner + kv_width :],
        output_sum,
        gate_sum,
        up_sum,
        down_sum,
        gain_sum[0],
        gain_sum[1],
    )


def solution(mesh):
    placed = (
        P(("dp", "tensor"), None),
        P("dp", "tensor"),
        P("dp", "tensor"),
        P("dp", "tensor"),
        P("tensor", "dp"),
        P("dp", "tensor"),
        P("dp", "tensor"),
        P("tensor", "dp"),
        P("dp"),
        P("dp"),
        P("dp", None),
        P(("dp", "tensor"), None),
    )
    return jax.shard_map(
        per_device,
        mesh=mesh,
        in_specs=placed,
        out_specs=(
            P(("dp", "tensor"), None),
            P(("dp", "tensor"), None),
            P("dp", "tensor"),
            P("dp", "tensor"),
            P("dp", "tensor"),
            P("tensor", "dp"),
            P("dp", "tensor"),
            P("dp", "tensor"),
            P("tensor", "dp"),
            P("dp"),
            P("dp"),
        ),
        check_vma=False,
    )
```

time: 1450 us -> 783 us (0.54)
  waiting for transfers between devices: 982 us -> 269 us
  blocking collectives: 131 us -> 5.67 us
  starting transfers between devices: 1.93 us -> 106 us
  local copies, waits for them, and re-layouts: 32.8 us -> 116 us
  matrix products: 223 us -> 207 us
    reduce_scatter x11 -> x0, waiting for transfers between devices: 635 us -> none  [the longest x1 112 us: per_device(): lax.psum_scatter(grad_down.astype(jnp.bfloat16), 'dp', scatter_dimension=...]
    all_gather x9 -> x0, waiting for transfers between devices: 346 us -> none  [the longest x1 96.4 us: per_device(): lax.all_gather(down_weight.astype(half_type), 'dp', axis=1, tiled=True)]
    ppermute x0 -> x112, waiting for transfers between devices: none -> 269 us  [the longest x18 87.6 us: reduce(): above = lax.ppermute(top.astype(HALF), 'dp', self.up).astype(FULL)]
    ppermute x0 -> x112, starting transfers between devices: none -> 106 us  [the longest x15 28.2 us: gather(): above = lax.ppermute(above, 'dp', self.up)]
    all_gather x4 -> x0, blocking collectives: 103 us -> none  [the longest x1 32.7 us: per_device(): lax.all_gather(value_weight.astype(half_type), 'dp', axis=0, tiled=True)]
    unnamed x100 -> x198, local copies, waits for them, and re-layouts: 12.4 us -> 59.3 us
    unnamed x1 -> x0, blocking collectives: 21.6 us -> none
    convert_element_type x26 -> x16, other arithmetic: 25.7 us -> 7.98 us  [the longest x4 2.04 us: scatter_rows(): send = (piece(2).astype(FULL) + across).astype(HALF)]
  transfers between devices with their start and end apart: 20 -> 112, of which waited for: 16 -> 50; matrix products, arithmetic and copies ran while one was open for 11% -> 42% of each run, Pallas kernels for 0% -> 0%
where the time goes in v1:
time: 783 us; the launch traced here: 768 us
  waiting for transfers between devices  269 us (34%)
  matrix products  207 us (26%)
  local copies, waits for them, and re-layouts  116 us (15%)
  starting transfers between devices  106 us (14%)
  other arithmetic  49.2 us (6%)
  between operations  14.6 us (2%)
    ppermute x18, waiting for transfers between devices, reduce(): above = lax.ppermute(top.astype(HALF), 'dp', self.up).astype(FULL)  87.6 us
    dot_general x56, matrix products, contract_rows(): lax.dot_general(left, right, (((0,), (0,)), ((), ())), preferred_element_...  81.3 us
    dot_general x29, matrix products, contract_cols(): lax.dot_general(left, right, (((1,), (1,)), ((), ())), preferred_element_...  69 us
    unnamed x198, local copies, waits for them, and re-layouts  59.3 us
    dot_general x21, matrix products, product(): return jnp.dot(left, right, preferred_element_type=FULL)  56.5 us
    ppermute x15, waiting for transfers between devices, gather(): above = lax.ppermute(above, 'dp', self.up)  32.4 us
    ppermute x15, waiting for transfers between devices, gather(): below = lax.ppermute(below, 'dp', self.down)  29.2 us
    ppermute x6, waiting for transfers between devices, reduce(): above = lax.ppermute(far[:cut].astype(HALF), 'dp', self.up).astype(FULL)  28.8 us
  transfers between devices with their start and end apart: 112, of which 50 were waited for; matrix products, arithmetic and copies ran while one was open for 42% of the time, Pallas kernels for 0%

profile of v1, /device:TPU:0, one launch (start us, length us, event | category | flops | bytes accessed | tf_op | source)
XLA Modules:
  0.0 768.1 jit_solution(10361291926960753380)
XLA Ops:
  67.2 11.0 %collective-permute-done.13 = bf16[512,256]{1,0:T(8,128)(2,1)S(1)} collective-permute-done((bf16[512,256]{1,0:T(8,128)(2,1)}, bf16[512,256]{1,0:T(8,128)(2,1)S(1)}, u32[]{:S(2)}, u32[]{:S(2)}) %collective-permute-start.13) | collective-permute-done | bytes 262176 | tf_op jit(solution)/shard_map/ppermute | solution.py:108
  149.9 10.2 %collective-permute-done.17 = bf16[256,256]{1,0:T(8,128)(2,1)S(1)} collective-permute-done((bf16[256,256]{1,0:T(8,128)(2,1)S(1)}, bf16[256,256]{1,0:T(8,128)(2,1)S(1)}, u32[]{:S(2)}, u32[]{:S(2)}) %collective-permute-start.17) | collective-permute-done | bytes 131104 | tf_op jit(solution)/shard_map/ppermute | solution.py:112
  169.5 10.7 %collective-permute-done.9 = bf16[144,640]{1,0:T(8,128)(2,1)S(1)} collective-permute-done((bf16[144,640]{1,0:T(8,128)(2,1)}, bf16[144,640]{1,0:T(8,128)(2,1)S(1)}, u32[]{:S(2)}, u32[]{:S(2)}) %collective-permute-start.9) | collective-permute-done | bytes 184352 | tf_op jit(solution)/shard_map/ppermute | solution.py:113
  191.6 7.4 collective-permute-done.44
  204.5 9.9 %collective-permute-done.28 = bf16[256,1408]{1,0:T(8,128)(2,1)S(1)} collective-permute-done((bf16[256,1408]{1,0:T(8,128)(2,1)}, bf16[256,1408]{1,0:T(8,128)(2,1)S(1)}, u32[]{:S(2)}, u32[]{:S(2)}) %collective-permute-start.28) | collective-permute-done | bytes 720928 | tf_op jit(solution)/shard_map/ppermute | solution.py:109
  228.2 35.2 %while.34 = (s32[]{:T(128)}, f32[768,512]{0,1:T(8,128)}, f32[8,768]{1,0:T(8,128)}, bf16[768,512]{1,0:T(8,128)(2,1)S(1)}, bf16[768,64]{1,0:T(8,128)(2,1)S(1)}, /*...) while((s32[]{:T(128)}, f32[768,512]{0,1:T(8,128)}, ...), condition=%wide.region_7.8_spmd.clone, body=%wide.region_4.7_spmd.clone.sunk | while | flops 157482240 | bytes 7811239 | solution.py:246
  306.4 7.4 fusion.180
  315.4 7.5 collective-permute-done.23
  332.0 9.4 %multiply_convert_fusion.2 = (bf16[768,1408]{1,0:T(8,128)(2,1)S(1)}, bf16[768,1408]{1,0:T(8,128)(2,1)S(1)}, bf16[768,1408]{1,0:T(8,128)(2,1)}) fusion(f32[768,1408]{1,0:T(8,128)S(1)} %fusion.180, f32[768,1408]{1,0:T(8,128)} %fusion.179, bf16[768,2048]{1,0:T(8,128)(2,1)S(1)} %constant_dynamic-update-slice_fusion.56, ...), kind=kOutput, calls=%fused_computation.42 | convolution fusion | flops 4445405184 | bytes 24051712 | tf_op jit(solution)/shard_map/dot_general | solution.py:61
  341.3 7.7 %convolution_convert_fusion.2 = bf16[768,2048]{1,0:T(8,128)(2,1)S(1)} fusion(bf16[768,1408]{1,0:T(8,128)(2,1)} %get-tuple-element.522, bf16[1408,2048]{1,0:T(8,128)(2,1)S(1)} %maximum_dynamic-update-slice_fusion), kind=kOutput, calls=%fused_computation.48 | convolution fusion | flops 4430757888 | bytes 11075584 | tf_op jit(solution)/shard_map/dot_general | solution.py:61
  354.7 7.1 fusion.181
  368.5 9.0 %add_convert_fusion = bf16[768,2048]{1,0:T(8,128)(2,1)S(1)} fusion(f32[768,2048]{1,0:T(8,128)} %fusion.181, bf16[768,1408]{1,0:T(8,128)(2,1)S(1)} %get-tuple-element.520, bf16[2048,1408]{1,0:T(8,128)(2,1)} %copy-done.49), kind=kOutput, calls=%fused_computation.40 | convolution fusion | flops 4432330752 | bytes 17367040 | tf_op jit(solution)/shard_map/dot_general | solution.py:57
  381.6 14.8 %collective-permute-done.88 = bf16[128,1408]{1,0:T(8,128)(2,1)S(1)} collective-permute-done((bf16[128,1408]{1,0:T(8,128)(2,1)S(1)}, bf16[128,1408]{1,0:T(8,128)(2,1)S(1)}, u32[]{:S(2)}, u32[]{:S(2)}) %collective-permute-start.88) | collective-permute-done | bytes 360480 | tf_op jit(solution)/shard_map/ppermute | solution.py:120
  396.9 9.3 %collective-permute-done.92 = bf16[128,1408]{1,0:T(8,128)(2,1)S(1)} collective-permute-done((bf16[128,1408]{1,0:T(8,128)(2,1)S(1)}, bf16[128,1408]{1,0:T(8,128)(2,1)S(1)}, u32[]{:S(2)}, u32[]{:S(2)}) %collective-permute-start.92) | collective-permute-done | bytes 360480 | tf_op jit(solution)/shard_map/ppermute | solution.py:121
  408.5 6.7 collective-permute-done.80
  429.0 23.2 %collective-permute-done.89 = bf16[256,1408]{1,0:T(8,128)(2,1)S(1)} collective-permute-done((bf16[256,1408]{1,0:T(8,128)(2,1)S(1)}, bf16[256,1408]{1,0:T(8,128)(2,1)S(1)}, u32[]{:S(2)}, u32[]{:S(2)}) %collective-permute-start.89) | collective-permute-done | bytes 720928 | tf_op jit(solution)/shard_map/ppermute | solution.py:131
  454.3 8.7 %collective-permute-done.81 = bf16[256,1408]{1,0:T(8,128)(2,1)S(1)} collective-permute-done((bf16[256,1408]{1,0:T(8,128)(2,1)S(1)}, bf16[256,1408]{1,0:T(8,128)(2,1)S(1)}, u32[]{:S(2)}, u32[]{:S(2)}) %collective-permute-start.81) | collective-permute-done | bytes 720928 | tf_op jit(solution)/shard_map/ppermute | solution.py:131
  469.4 9.6 %collective-permute-done.101 = bf16[1408,256]{1,0:T(8,128)(2,1)S(1)} collective-permute-done((bf16[1408,256]{1,0:T(8,128)(2,1)S(1)}, bf16[1408,256]{1,0:T(8,128)(2,1)S(1)}, u32[]{:S(2)}, u32[]{:S(2)}) %collective-permute-start.101) | collective-permute-done | bytes 720928 | tf_op jit(solution)/shard_map/ppermute | solution.py:132
  486.6 9.6 %collective-permute-done.57 = bf16[192,2048]{1,0:T(8,128)(2,1)S(1)} collective-permute-done((bf16[192,2048]{1,0:T(8,128)(2,1)S(1)}, bf16[192,2048]{1,0:T(8,128)(2,1)S(1)}, u32[]{:S(2)}, u32[]{:S(2)}) %collective-permute-start.57) | collective-permute-done | bytes 786464 | tf_op jit(solution)/shard_map/ppermute | solution.py:167
  505.2 8.2 %collective-permute-done.108 = bf16[1,256]{1,0:T(2,128)(2,1)S(1)} collective-permute-done((bf16[1,256]{1,0:T(2,128)(2,1)S(1)}, bf16[1,256]{1,0:T(2,128)(2,1)S(1)}, u32[]{:S(2)}, u32[]{:S(2)}) %collective-permute-start.108) | collective-permute-done | bytes 544 | tf_op jit(solution)/shard_map/ppermute | solution.py:121
  520.2 7.9 %collective-permute-done.82 = bf16[256,1408]{1,0:T(8,128)(2,1)S(1)} collective-permute-done((bf16[256,1408]{1,0:T(8,128)(2,1)S(1)}, bf16[256,1408]{1,0:T(8,128)(2,1)S(1)}, u32[]{:S(2)}, u32[]{:S(2)}) %collective-permute-start.82) | collective-permute-done | bytes 720928 | tf_op jit(solution)/shard_map/ppermute | solution.py:131
  538.8 20.8 %collective-permute-done.91 = bf16[256,1408]{1,0:T(8,128)(2,1)S(1)} collective-permute-done((bf16[256,1408]{1,0:T(8,128)(2,1)S(1)}, bf16[256,1408]{1,0:T(8,128)(2,1)S(1)}, u32[]{:S(2)}, u32[]{:S(2)}) %collective-permute-start.91) | collective-permute-done | bytes 720928 | tf_op jit(solution)/shard_map/ppermute | solution.py:131
  574.1 89.3 %while.35 = (s32[]{:T(128)}, f32[768,512]{0,1:T(8,128)}, f32[768,64]{0,1:T(8,128)}, f32[768,64]{0,1:T(8,128)}, bf16[768,512]{1,0:T(8,128)(2,1)S(1)}, /*index=5*/...) while((s32[]{:T(128)}, f32[768,512]{0,1:T(8,128)}, ...), condition=%wide.region_13.14_spmd.clone, body=%wide.region_11.13_spmd.clone.sunk | while | flops 384859392 | bytes 27844988 | solution.py:315
  709.0 6.9 collective-permute-done.78
  (837 shorter events, 529.6 us)
Async XLA Ops:
  6.2 53.0 %collective-permute-start.3 = (bf16[288,640]{1,0:T(8,128)(2,1)}, bf16[288,640]{1,0:T(8,128)(2,1)}, u32[]{:S(2)}, u32[]{:S(2)}) collective-permute-start(bf16[288,640]{1,0:T(8,128)(2,1)} %pad_maximum_fusion.9), channel_id=1, source_target_pairs={{0,8},{8,16},{16,24},{24,28},{28,20},{20,12},{12,4},{4,0},{1,9},{9... | collective-permute-start | bytes 1105928 | tf_op jit(solution)/shard_map/ppermute | solution.py:108
  9.2 54.5 %collective-permute-start.4 = (bf16[288,640]{1,0:T(8,128)(2,1)}, bf16[288,640]{1,0:T(8,128)(2,1)}, u32[]{:S(2)}, u32[]{:S(2)}) collective-permute-start(bf16[288,640]{1,0:T(8,128)(2,1)} %pad_maximum_fusion.9), channel_id=1, source_target_pairs={{8,0},{16,8},{24,16},{28,24},{20,28},{12,20},{4,12},{0,4},{9,1},{1... | collective-permute-start | bytes 1105928 | tf_op jit(solution)/shard_map/ppermute | solution.py:109
  10.1 43.7 %collective-permute-start.11 = (bf16[512,256]{1,0:T(8,128)(2,1)}, bf16[512,256]{1,0:T(8,128)(2,1)}, u32[]{:S(2)}, u32[]{:S(2)}) collective-permute-start(bf16[512,256]{1,0:T(8,128)(2,1)} %get-tuple-element.515), channel_id=1, source_target_pairs={{0,8},{8,16},{16,24},{24,28},{28,20},{20,12},{12,4},{4,0},{1,9},{9... | collective-permute-start | bytes 786440 | tf_op jit(solution)/shard_map/ppermute | solution.py:108
  12.1 45.3 %collective-permute-start.12 = (bf16[512,256]{1,0:T(8,128)(2,1)}, bf16[512,256]{1,0:T(8,128)(2,1)}, u32[]{:S(2)}, u32[]{:S(2)}) collective-permute-start(bf16[512,256]{1,0:T(8,128)(2,1)} %get-tuple-element.515), channel_id=1, source_target_pairs={{8,0},{16,8},{24,16},{28,24},{20,28},{12,20},{4,12},{0,4},{9,1},{1... | collective-permute-start | bytes 786440 | tf_op jit(solution)/shard_map/ppermute | solution.py:109
  31.5 105.9 %collective-permute-start = (bf16[192,2048]{1,0:T(8,128)(2,1)}, bf16[192,2048]{1,0:T(8,128)(2,1)}, u32[]{:S(2)}, u32[]{:S(2)}) collective-permute-start(bf16[192,2048]{1,0:T(8,128)(2,1)} %constant_dynamic-update-slice_fusion), channel_id=1, source_target_pairs={{0,1},{1,0},{2,3},{3,2},{4,5},{5,4},{6,7},{7,6},{8,9},{9,8},{10,11... | collective-permute-start | bytes 2359304 | tf_op jit(solution)/shard_map/ppermute | solution.py:146
  81.6 61.3 %collective-permute-start.1 = (bf16[192,2048]{1,0:T(8,128)(2,1)}, bf16[192,2048]{1,0:T(8,128)(2,1)}, u32[]{:S(2)}, u32[]{:S(2)}) collective-permute-start(bf16[192,2048]{1,0:T(8,128)(2,1)} %constant_dynamic-update-slice_fusion), channel_id=1, source_target_pairs={{0,2},{1,3},{2,0},{3,1},{4,6},{5,7},{6,4},{7,5},{8,10},{9,11},{10,... | collective-permute-start | bytes 2359304 | tf_op jit(solution)/shard_map/ppermute | solution.py:143
  104.1 36.1 %collective-permute-start.52 = (bf16[192,2048]{1,0:T(8,128)(2,1)}, bf16[192,2048]{1,0:T(8,128)(2,1)}, u32[]{:S(2)}, u32[]{:S(2)}) collective-permute-start(bf16[192,2048]{1,0:T(8,128)(2,1)} %constant_dynamic-update-slice_fusion.40), channel_id=1, source_target_pairs={{0,1},{1,0},{2,3},{3,2},{4,5},{5,4},{6,7},{7,6},{8,9},{9,8},{10,11... | collective-permute-start | bytes 2359304 | tf_op jit(solution)/shard_map/ppermute | solution.py:146
  133.2 51.8 %collective-permute-start.35 = (bf16[256,1408]{1,0:T(8,128)(2,1)}, bf16[256,1408]{1,0:T(8,128)(2,1)}, u32[]{:S(2)}, u32[]{:S(2)}) collective-permute-start(bf16[256,1408]{1,0:T(8,128)(2,1)} %collective-permute-done.33), channel_id=1, source_target_pairs={{0,8},{8,16},{16,24},{24,28},{28,20},{20,12},{12,4},{4,0},{1,9},{9... | collective-permute-start | bytes 2162696 | tf_op jit(solution)/shard_map/ppermute | solution.py:108
  189.1 78.4 %collective-permute-start.54 = (bf16[192,2048]{1,0:T(8,128)(2,1)}, bf16[192,2048]{1,0:T(8,128)(2,1)}, u32[]{:S(2)}, u32[]{:S(2)}) collective-permute-start(bf16[192,2048]{1,0:T(8,128)(2,1)} %collective-permute-done.53), channel_id=1, source_target_pairs={{0,1},{1,0},{2,3},{3,2},{4,5},{5,4},{6,7},{7,6},{8,9},{9,8},{10,11... | collective-permute-start | bytes 2359304 | tf_op jit(solution)/shard_map/ppermute | solution.py:148
  199.1 74.5 %collective-permute-start.37 = (bf16[256,1408]{1,0:T(8,128)(2,1)}, bf16[256,1408]{1,0:T(8,128)(2,1)}, u32[]{:S(2)}, u32[]{:S(2)}) collective-permute-start(bf16[256,1408]{1,0:T(8,128)(2,1)} %collective-permute-done.35), channel_id=1, source_target_pairs={{0,8},{8,16},{16,24},{24,28},{28,20},{20,12},{12,4},{4,0},{1,9},{9... | collective-permute-start | bytes 2162696 | tf_op jit(solution)/shard_map/ppermute | solution.py:108
  203.2 73.0 %collective-permute-start.38 = (bf16[256,1408]{1,0:T(8,128)(2,1)}, bf16[256,1408]{1,0:T(8,128)(2,1)}, u32[]{:S(2)}, u32[]{:S(2)}) collective-permute-start(bf16[256,1408]{1,0:T(8,128)(2,1)} %collective-permute-done.36), channel_id=1, source_target_pairs={{8,0},{16,8},{24,16},{28,24},{20,28},{12,20},{4,12},{0,4},{9,1},{1... | collective-permute-start | bytes 2162696 | tf_op jit(solution)/shard_map/ppermute | solution.py:109
  214.4 55.3 %collective-permute-start.45 = (bf16[1408,256]{1,0:T(8,128)(2,1)}, bf16[1408,256]{1,0:T(8,128)(2,1)}, u32[]{:S(2)}, u32[]{:S(2)}) collective-permute-start(bf16[1408,256]{1,0:T(8,128)(2,1)} %collective-permute-done.43), channel_id=1, source_target_pairs={{0,8},{8,16},{16,24},{24,28},{28,20},{20,12},{12,4},{4,0},{1,9},{9... | collective-permute-start | bytes 2162696 | tf_op jit(solution)/shard_map/ppermute | solution.py:108
  216.9 63.1 %collective-permute-start.46 = (bf16[1408,256]{1,0:T(8,128)(2,1)}, bf16[1408,256]{1,0:T(8,128)(2,1)}, u32[]{:S(2)}, u32[]{:S(2)}) collective-permute-start(bf16[1408,256]{1,0:T(8,128)(2,1)} %collective-permute-done.44), channel_id=1, source_target_pairs={{8,0},{16,8},{24,16},{28,24},{20,28},{12,20},{4,12},{0,4},{9,1},{1... | collective-permute-start | bytes 2162696 | tf_op jit(solution)/shard_map/ppermute | solution.py:109
  368.0 58.3 %collective-permute-start.50 = (bf16[192,2048]{1,0:T(8,128)(2,1)}, bf16[192,2048]{1,0:T(8,128)(2,1)S(1)}, u32[]{:S(2)}, u32[]{:S(2)}) collective-permute-start(bf16[192,2048]{1,0:T(8,128)(2,1)} %get-tuple-element.528), channel_id=1, source_target_pairs={{0,1},{1,0},{2,3},{3,2},{4,5},{5,4},{6,7},{7,6},{8,9},{9,8},{10,11... | collective-permute-start | bytes 2359304 | tf_op jit(solution)/shard_map/ppermute | solution.py:164
  368.1 114.2 %collective-permute-start.49 = (bf16[192,2048]{1,0:T(8,128)(2,1)}, bf16[192,2048]{1,0:T(8,128)(2,1)}, u32[]{:S(2)}, u32[]{:S(2)}) collective-permute-start(bf16[192,2048]{1,0:T(8,128)(2,1)} %get-tuple-element.527), channel_id=1, source_target_pairs={{0,1},{1,0},{2,3},{3,2},{4,5},{5,4},{6,7},{7,6},{8,9},{9,8},{10,11... | collective-permute-start | bytes 2359304 | tf_op jit(solution)/shard_map/ppermute | solution.py:165
  377.6 49.4 %collective-permute-start.56 = (bf16[192,2048]{1,0:T(8,128)(2,1)S(1)}, bf16[192,2048]{1,0:T(8,128)(2,1)S(1)}, u32[]{:S(2)}, u32[]{:S(2)}) collective-permute-start(bf16[192,2048]{1,0:T(8,128)(2,1)S(1)} %get-tuple-element.526), channel_id=1, source_target_pairs={{0,1},{1,0},{2,3},{3,2},{4,5},{5,4},{6,7},{7,6},{8,9},{9,8},{10,11... | collective-permute-start | bytes 2359304 | tf_op jit(solution)/shard_map/ppermute | solution.py:164
  417.7 47.0 %collective-permute-start.97 = (bf16[1408,256]{1,0:T(8,128)(2,1)S(1)}, bf16[1408,256]{1,0:T(8,128)(2,1)S(1)}, u32[]{:S(2)}, u32[]{:S(2)}) collective-permute-start(bf16[1408,256]{1,0:T(8,128)(2,1)S(1)} %pad_maximum_fusion.7), channel_id=1, source_target_pairs={{0,8},{8,16},{16,24},{24,28},{28,20},{20,12},{12,4},{4,0},{1,9},{9... | collective-permute-start | bytes 2162696 | tf_op jit(solution)/shard_map/ppermute | solution.py:131
  427.0 36.0 %collective-permute-start.81 = (bf16[256,1408]{1,0:T(8,128)(2,1)S(1)}, bf16[256,1408]{1,0:T(8,128)(2,1)S(1)}, u32[]{:S(2)}, u32[]{:S(2)}) collective-permute-start(bf16[256,1408]{1,0:T(8,128)(2,1)S(1)} %pad_maximum_fusion.3), channel_id=1, source_target_pairs={{0,8},{8,16},{16,24},{24,28},{28,20},{20,12},{12,4},{4,0},{1,9},{9... | collective-permute-start | bytes 2162696 | tf_op jit(solution)/shard_map/ppermute | solution.py:131
  482.3 48.3 %collective-permute-start.102 = (bf16[1408,256]{1,0:T(8,128)(2,1)S(1)}, bf16[1408,256]{1,0:T(8,128)(2,1)S(1)}, u32[]{:S(2)}, u32[]{:S(2)}) collective-permute-start(bf16[1408,256]{1,0:T(8,128)(2,1)S(1)} %fusion.45), channel_id=1, source_target_pairs={{8,0},{16,8},{24,16},{28,24},{20,28},{12,20},{4,12},{0,4},{9,1},{1... | collective-permute-start | bytes 2162696 | tf_op jit(solution)/shard_map/ppermute | solution.py:132
  528.1 35.6 %collective-permute-start.99 = (bf16[1408,256]{1,0:T(8,128)(2,1)S(1)}, bf16[1408,256]{1,0:T(8,128)(2,1)S(1)}, u32[]{:S(2)}, u32[]{:S(2)}) collective-permute-start(bf16[1408,256]{1,0:T(8,128)(2,1)S(1)} %fusion.42), channel_id=1, source_target_pairs={{0,8},{8,16},{16,24},{24,28},{28,20},{20,12},{12,4},{4,0},{1,9},{9... | collective-permute-start | bytes 2162696 | tf_op jit(solution)/shard_map/ppermute | solution.py:131
  559.6 169.4 %collective-permute-start.83 = (bf16[256,1408]{1,0:T(8,128)(2,1)}, bf16[256,1408]{1,0:T(8,128)(2,1)}, u32[]{:S(2)}, u32[]{:S(2)}) collective-permute-start(bf16[256,1408]{1,0:T(8,128)(2,1)} %fusion.34), channel_id=1, source_target_pairs={{0,8},{8,16},{16,24},{24,28},{28,20},{20,12},{12,4},{4,0},{1,9},{9... | collective-permute-start | bytes 2162696 | tf_op jit(solution)/shard_map/ppermute | solution.py:131
  560.4 170.6 %collective-permute-start.87 = (bf16[256,1408]{1,0:T(8,128)(2,1)}, bf16[256,1408]{1,0:T(8,128)(2,1)}, u32[]{:S(2)}, u32[]{:S(2)}) collective-permute-start(bf16[256,1408]{1,0:T(8,128)(2,1)} %fusion.36), channel_id=1, source_target_pairs={{8,0},{16,8},{24,16},{28,24},{20,28},{12,20},{4,12},{0,4},{9,1},{1... | collective-permute-start | bytes 2162696 | tf_op jit(solution)/shard_map/ppermute | solution.py:132
  675.0 42.0 %collective-permute-start.62 = (bf16[192,2048]{1,0:T(8,128)(2,1)S(1)}, bf16[192,2048]{1,0:T(8,128)(2,1)S(1)}, u32[]{:S(2)}, u32[]{:S(2)}) collective-permute-start(bf16[192,2048]{1,0:T(8,128)(2,1)S(1)} %get-tuple-element.524), channel_id=1, source_target_pairs={{0,1},{1,0},{2,3},{3,2},{4,5},{5,4},{6,7},{7,6},{8,9},{9,8},{10,11... | collective-permute-start | bytes 2359304 | tf_op jit(solution)/shard_map/ppermute | solution.py:164
  703.2 39.1 %collective-permute-start.61 = (bf16[192,2048]{1,0:T(8,128)(2,1)}, bf16[192,2048]{1,0:T(8,128)(2,1)S(1)}, u32[]{:S(2)}, u32[]{:S(2)}) collective-permute-start(bf16[192,2048]{1,0:T(8,128)(2,1)} %get-tuple-element.523), channel_id=1, source_target_pairs={{0,1},{1,0},{2,3},{3,2},{4,5},{5,4},{6,7},{7,6},{8,9},{9,8},{10,11... | collective-permute-start | bytes 2359304 | tf_op jit(solution)/shard_map/ppermute | solution.py:165
  (203 other events, 3672.6 us)

commit v2 on v1

v2 whole, which is shorter than its diff:
```python
import functools
import math

import jax
import jax.numpy as jnp
from jax import lax
from jax.experimental import pallas as pl
from jax.experimental.pallas import tpu as pltpu
from jax.sharding import PartitionSpec as P

HEAD_DIM = 64


EPS = 1e-05
NEG = -1e30
HALF = jnp.bfloat16
FULL = jnp.float32


def group_layout(counts, total):
    ends = jnp.cumsum(counts)
    starts = ends - counts
    place = jnp.arange(total, dtype=jnp.int32)
    segment = jnp.sum((place[:, None] >= ends[None, :]).astype(jnp.int32), axis=1)
    bounds = jnp.concatenate([starts, ends[-1:]])
    slots = jnp.arange(bounds.shape[0], dtype=jnp.int32)
    begin = jnp.sum(jnp.where(segment[:, None] == slots[None, :], bounds[None, :], 0), axis=1)
    position = (place - begin).astype(FULL)
    valid = (place < ends[-1]).astype(FULL)
    allowed = (segment[:, None] == segment[None, :]) & (place[None, :] <= place[:, None])
    return (position, valid, allowed)


def angle_tables(position):
    half = HEAD_DIM // 2
    freq = jnp.exp(jnp.arange(half, dtype=FULL) * (-2.0 * math.log(10000.0) / HEAD_DIM))
    angle = position[:, None] * freq[None, :]
    return (jnp.cos(angle), jnp.sin(angle))


def contract_rows(left, right):
    return lax.dot_general(left, right, (((0,), (0,)), ((), ())), preferred_element_type=FULL)


def contract_cols(left, right):
    return lax.dot_general(left, right, (((1,), (1,)), ((), ())), preferred_element_type=FULL)


def product(left, right):
    return jnp.dot(left, right, preferred_element_type=FULL)


def rms_scale(values):
    return lax.rsqrt(jnp.mean(values * values, axis=1, keepdims=True) + EPS)


TILE = 256
VMEM = 56 * 2**20

def lasting(time):
    return pl.CostEstimate(flops=int(time * 1.1e9), bytes_accessed=0, transcendentals=0)


def tie(value, *marks):
    return lax.optimization_barrier((value, marks))[0]


def nt(left, right):
    return lax.dot_general(left, right, (((1,), (1,)), ((), ())), preferred_element_type=FULL)

def nn(left, right):
    return lax.dot_general(left, right, (((1,), (0,)), ((), ())), preferred_element_type=FULL)

def swap_halves(x):
    lane = lax.broadcasted_iota(jnp.int32, x.shape, 1)
    return jnp.where(lane % 64 < 32, pltpu.roll(x, 96, 1), pltpu.roll(x, 32, 1))

def fill_bias(begin_ref, bias_ref, total):
    for i in range(total // TILE):
        size = (i + 1) * TILE
        key = lax.broadcasted_iota(jnp.int32, (size, TILE), 0)
        query = lax.broadcasted_iota(jnp.int32, (size, TILE), 1) + i * TILE
        begin = begin_ref[:, i * TILE:(i + 1) * TILE]
        keep = (key >= begin) & (key <= query)
        bias_ref[i, 0:size, :] = jnp.where(keep, 0.0, NEG)

def fwd_kernel(joined_ref, cos_ref, sin_ref, begin_ref, valid_ref, q_ref, kv_ref, out_ref, lse_ref, bias_ref, ka_ref, vt_ref):
    total, wide = joined_ref.shape
    pairs = wide // 128 - 1
    lane = lax.broadcasted_iota(jnp.int32, (total, 128), 1)
    kv = joined_ref[:, pairs * 128:]
    cosine = cos_ref[...]
    sine = sin_ref[...]
    turned = kv * cosine + swap_halves(kv) * sine
    kv = jnp.where(lane < 64, turned, kv)
    kv_ref[...] = kv.astype(HALF)
    ka_ref[0] = jnp.where(lane < 64, kv, 0.0).astype(HALF)
    ka_ref[1] = jnp.where(lane < 64, 0.0, pltpu.roll(kv, 64, 1)).astype(HALF)
    vt_ref[...] = kv.T[64:, :].astype(HALF)
    fill_bias(begin_ref, bias_ref, total)
    for p in range(pairs):
        q = joined_ref[:, p * 128:(p + 1) * 128]
        q_ref[:, p * 128:(p + 1) * 128] = ((q * cosine + swap_halves(q) * sine) * (HEAD_DIM ** -0.5)).astype(HALF)

    def pair(p, carry):
        column = pl.multiple_of(p * 128, 128)
        for i in range(total // TILE):
            size = (i + 1) * TILE
            q = q_ref[i * TILE:(i + 1) * TILE, pl.ds(column, 128)]
            parts = []
            for a in range(2):
                s = nt(ka_ref[a, 0:size, :], q) + bias_ref[i, 0:size, :]
                peak = jnp.max(s, axis=0, keepdims=True)
                expo = jnp.exp(s - peak)
                denom = jnp.sum(expo, axis=0, keepdims=True)
                o = nn(vt_ref[:, 0:size], expo.astype(HALF)) / denom
                lse_ref[2 * p + a, :, i * TILE:(i + 1) * TILE] = peak + jnp.log(denom)
                parts.append(o)
            o = jnp.concatenate(parts, axis=0) * valid_ref[:, i * TILE:(i + 1) * TILE]
            out_ref[i * TILE:(i + 1) * TILE, pl.ds(column, 128)] = o.T.astype(HALF)
        return carry
    lax.fori_loop(0, pairs, pair, 0)

def attend(joined, cosine, sine, begin, valid):
    total, wide = joined.shape
    heads = wide // 64 - 2
    return pl.pallas_call(
        fwd_kernel,
        out_shape=(
            jax.ShapeDtypeStruct((total, heads * 64), HALF),
            jax.ShapeDtypeStruct((total, 128), HALF),
            jax.ShapeDtypeStruct((total, heads * 64), HALF),
            jax.ShapeDtypeStruct((heads, 1, total), FULL),
        ),
        scratch_shapes=[
            pltpu.VMEM((total // TILE, total, TILE), FULL),
            pltpu.VMEM((2, total, 128), HALF),
            pltpu.VMEM((64, total), HALF),
        ],
        compiler_params=pltpu.CompilerParams(vmem_limit_bytes=VMEM),
        cost_estimate=lasting(13.0),
        name="attend",
    )(joined, cosine, sine, begin, valid)

def bwd_kernel(q_ref, kv_ref, do_ref, lse_ref, cos_ref, sin_ref, begin_ref, out_ref, bias_ref, ka_ref, va_ref, kt_ref, dk_ref, dv_ref):
    total = kv_ref.shape[0]
    pairs = q_ref.shape[1] // 128
    lane = lax.broadcasted_iota(jnp.int32, (total, 128), 1)
    kv = kv_ref[...].astype(FULL)
    rolled = pltpu.roll(kv, 64, 1)
    ka_ref[0] = jnp.where(lane < 64, kv, 0.0).astype(HALF)
    ka_ref[1] = jnp.where(lane < 64, 0.0, rolled).astype(HALF)
    va_ref[0] = jnp.where(lane < 64, rolled, 0.0).astype(HALF)
    va_ref[1] = jnp.where(lane < 64, 0.0, kv).astype(HALF)
    kt_ref[...] = kv.T[:64, :].astype(HALF)
    dk_ref[...] = jnp.zeros_like(dk_ref)
    dv_ref[...] = jnp.zeros_like(dv_ref)
    fill_bias(begin_ref, bias_ref, total)
    low = lax.broadcasted_iota(jnp.int32, (TILE, 128), 1) < 64

    def pair(p, carry):
        column = pl.multiple_of(p * 128, 128)
        for i in range(total // TILE):
            size = (i + 1) * TILE
            rows = slice(i * TILE, (i + 1) * TILE)
            q = q_ref[rows, pl.ds(column, 128)]
            do = do_ref[rows, pl.ds(column, 128)]
            parts = []
            for a in range(2):
                keep = low if a == 0 else jnp.logical_not(low)
                s = nt(ka_ref[a, 0:size, :], q) + bias_ref[i, 0:size, :]
                probs = jnp.exp(s - lse_ref[2 * p + a, :, rows])
                dprobs = nt(va_ref[a, 0:size, :], do)
                delta = jnp.sum(probs * dprobs, axis=0, keepdims=True)
                ds = (probs * (dprobs - delta)).astype(HALF)
                dv_ref[0:size, :] += nn(probs.astype(HALF), jnp.where(keep, do, jnp.zeros_like(do)))
                dk_ref[0:size, :] += nn(ds, jnp.where(keep, q, jnp.zeros_like(q)))
                parts.append(nn(kt_ref[:, 0:size], ds))
            dq = jnp.concatenate(parts, axis=0).T * (HEAD_DIM ** -0.5)
            dq = dq * cos_ref[rows, :] - swap_halves(dq) * sin_ref[rows, :]
            out_ref[rows, pl.ds(column, 128)] = dq.astype(HALF)
        return carry
    lax.fori_loop(0, pairs, pair, 0)
    dk = dk_ref[...]
    dk = dk + pltpu.roll(dk, 64, 1)
    dk = dk * cos_ref[...] - swap_halves(dk) * sin_ref[...]
    dv = dv_ref[...]
    dv = dv + pltpu.roll(dv, 64, 1)
    out_ref[:, pairs * 128:] = jnp.where(lane < 64, dk, dv).astype(HALF)

def attend_back(q, kv, do, lse, cosine, sine, begin):
    total, wide = q.shape
    return pl.pallas_call(
        bwd_kernel,
        out_shape=jax.ShapeDtypeStruct((total, wide + 128), HALF),
        scratch_shapes=[
            pltpu.VMEM((total // TILE, total, TILE), FULL),
            pltpu.VMEM((2, total, 128), HALF),
            pltpu.VMEM((2, total, 128), HALF),
            pltpu.VMEM((64, total), HALF),
            pltpu.VMEM((total, 128), FULL),
            pltpu.VMEM((total, 128), FULL),
        ],
        compiler_params=pltpu.CompilerParams(vmem_limit_bytes=VMEM),
        cost_estimate=lasting(14.5),
        name="attend_back",
    )(q, kv, do, lse, cosine, sine, begin)


def block_of(refs, slot, extent, slots):
    if slot < slots - 1 or len(refs) == slots:
        return refs[slot][0:extent, :]
    cut = refs[-2].shape[0]
    return jnp.concatenate([refs[-2][...], refs[-1][0 : extent - cut, :]], axis=0)


def whole(array):
    return pl.BlockSpec(array.shape, lambda i: (0,) * array.ndim)

def rows_of(width, tile=TILE):
    return pl.BlockSpec((tile, width), lambda i: (i, 0))

def gate_up_kernel(units, x_ref, grad_ref, *refs):
    pieces, hidden_ref, out_ref = refs[:-2], refs[-2], refs[-1]
    for start in range(0, units, 128):
        there = slice(start, start + 128)
        pairs = [
            jnp.concatenate([ref[:, there], ref[:, units + start : units + start + 128]], axis=1)
            for ref in pieces
        ]
        both = nn(x_ref[...], jnp.concatenate(pairs, axis=0))
        gate, up = both[:, :128], both[:, 128:]
        sigma = jax.nn.sigmoid(gate)
        swish = gate * sigma
        grad = grad_ref[:, there]
        hidden_ref[:, there] = (swish * up).astype(HALF)
        out_ref[:, there] = (grad * up * sigma * (1.0 + gate * (1.0 - sigma))).astype(HALF)
        out_ref[:, units + start : units + start + 128] = (grad * swish).astype(HALF)


def gate_up(x, grad, pieces):
    total, wide = x.shape
    units = pieces[0].shape[1] // 2
    return pl.pallas_call(
        functools.partial(gate_up_kernel, units),
        grid=(total // TILE,),
        in_specs=[rows_of(wide), rows_of(units)] + [whole(p) for p in pieces],
        out_specs=[rows_of(units), rows_of(2 * units)],
        out_shape=(
            jax.ShapeDtypeStruct((total, units), HALF),
            jax.ShapeDtypeStruct((total, 2 * units), HALF),
        ),
        compiler_params=pltpu.CompilerParams(vmem_limit_bytes=VMEM),
        cost_estimate=lasting(16.5),
        name="gate_up",
    )(x, grad, *pieces)


def hidden_back_kernel(slots, x_ref, *refs):
    pieces, out_ref = refs[:-1], refs[-1]
    units, depth = pieces[0].shape
    total = None
    for slot in range(slots):
        part = nt(x_ref[:, slot * depth : (slot + 1) * depth], block_of(pieces, slot, units, slots))
        total = part if total is None else total + part
    out_ref[...] = total


def hidden_back(x, pieces, slots):
    total, wide = x.shape
    units = pieces[0].shape[0]
    return pl.pallas_call(
        functools.partial(hidden_back_kernel, slots),
        grid=(total // TILE,),
        in_specs=[rows_of(wide)] + [whole(p) for p in pieces],
        out_specs=rows_of(units),
        out_shape=jax.ShapeDtypeStruct((total, units), FULL),
        compiler_params=pltpu.CompilerParams(vmem_limit_bytes=VMEM),
        cost_estimate=lasting(10.8),
        name="hidden_back",
    )(x, *pieces)


def outward_kernel(slots, depth, view, transposed, x_ref, *refs):
    pieces, out_ref = refs[:-1], refs[-1]
    for slot in range(slots):
        block = view(block_of(pieces, slot, depth, slots))
        part = nt(x_ref[...], block) if transposed else nn(x_ref[...], block)
        width = part.shape[1]
        out_ref[:, slot * width : (slot + 1) * width] = part.astype(HALF)


def outward(x, pieces, slots, depth, width, transposed, time, name, view=lambda block: block):
    total, wide = x.shape
    return pl.pallas_call(
        functools.partial(outward_kernel, slots, depth, view, transposed),
        grid=(total // TILE,),
        in_specs=[rows_of(wide)] + [whole(p) for p in pieces],
        out_specs=rows_of(slots * width),
        out_shape=jax.ShapeDtypeStruct((total, slots * width), HALF),
        compiler_params=pltpu.CompilerParams(vmem_limit_bytes=VMEM),
        cost_estimate=lasting(time),
        name=name,
    )(x, *pieces)


def output_view(depth, start, block):
    packed = block[:depth, start:]
    return jnp.concatenate(
        [packed[:, at : at + depth] for at in range(0, packed.shape[1], depth)], axis=0
    )


def first_kernel(slots, depth, x_ref, *refs):
    pieces = refs[:-3]
    normed_ref, joined_ref, gains_ref = refs[-3:]
    values = x_ref[...].astype(FULL)
    values = values * lax.rsqrt(jnp.mean(values * values, axis=1, keepdims=True) + EPS)
    parts = []
    for slot in range(slots):
        there = slice(slot * depth, (slot + 1) * depth)
        block = block_of(pieces, slot, pieces[0].shape[0], slots)
        gains = block[depth:, :depth].astype(FULL)[0:2]
        gains_ref[:, there] = gains
        normed_ref[:, there] = (values[:, there] * gains[0:1]).astype(HALF)
        parts.append(block[:depth, : joined_ref.shape[1]])
    joined_ref[...] = nn(normed_ref[...], jnp.concatenate(parts, axis=0))


def first(x, pieces, slots, depth, units):
    total, wide = x.shape
    return pl.pallas_call(
        functools.partial(first_kernel, slots, depth),
        grid=(total // TILE,),
        in_specs=[rows_of(wide)] + [whole(p) for p in pieces],
        out_specs=[rows_of(wide), rows_of(units), pl.BlockSpec((2, wide), lambda i: (0, 0))],
        out_shape=(
            jax.ShapeDtypeStruct((total, wide), HALF),
            jax.ShapeDtypeStruct((total, units), FULL),
            jax.ShapeDtypeStruct((2, wide), FULL),
        ),
        compiler_params=pltpu.CompilerParams(vmem_limit_bytes=VMEM),
        cost_estimate=lasting(7.0),
        name="first",
    )(x, *pieces)


def first_back_kernel(slots, depth, grad_ref, x_ref, *refs):
    pieces = refs[:-2]
    out_ref, gain_ref = refs[-2:]

    @pl.when(pl.program_id(0) == 0)
    def _():
        gain_ref[...] = jnp.zeros_like(gain_ref)

    values = x_ref[...].astype(FULL)
    values = values * lax.rsqrt(jnp.mean(values * values, axis=1, keepdims=True) + EPS)
    for slot in range(slots):
        there = slice(slot * depth, (slot + 1) * depth)
        block = block_of(pieces, slot, pieces[0].shape[0], slots)[:depth, : grad_ref.shape[1]]
        part = nt(grad_ref[...], block).astype(HALF)
        out_ref[:, there] = part
        gain_ref[:, there] += jnp.sum(part.astype(FULL) * values[:, there], axis=0, keepdims=True)


def first_back(grad, x, pieces, slots, depth):
    total, wide = x.shape
    return pl.pallas_call(
        functools.partial(first_back_kernel, slots, depth),
        grid=(total // TILE,),
        in_specs=[rows_of(grad.shape[1]), rows_of(wide)] + [whole(p) for p in pieces],
        out_specs=[rows_of(wide), pl.BlockSpec((1, wide), lambda i: (0, 0))],
        out_shape=(jax.ShapeDtypeStruct((total, wide), HALF), jax.ShapeDtypeStruct((1, wide), FULL)),
        compiler_params=pltpu.CompilerParams(vmem_limit_bytes=VMEM),
        cost_estimate=lasting(7.0),
        name="first_back",
    )(grad, x, *pieces)


def mixed_back_kernel(slots, view, x_ref, *refs):
    pieces, valid_ref, out_ref = refs[:-2], refs[-2], refs[-1]
    total = None
    for slot in range(slots):
        block = view(block_of(pieces, slot, pieces[0].shape[0], slots))
        width = block.shape[1]
        part = nt(x_ref[:, slot * width : (slot + 1) * width], block)
        total = part if total is None else total + part
    out_ref[...] = (total.astype(HALF).astype(FULL) * valid_ref[...]).astype(HALF)


def mixed_back(x, pieces, valid, slots, units, view):
    total, wide = x.shape
    return pl.pallas_call(
        functools.partial(mixed_back_kernel, slots, view),
        grid=(total // TILE,),
        in_specs=[rows_of(wide)] + [whole(p) for p in pieces] + [rows_of(1)],
        out_specs=rows_of(units),
        out_shape=jax.ShapeDtypeStruct((total, units), HALF),
        compiler_params=pltpu.CompilerParams(vmem_limit_bytes=VMEM),
        cost_estimate=lasting(5.4),
        name="mixed_back",
    )(x, *pieces, valid)


def shuffle_kernel(members, count, inverse, *refs):
    half = len(refs) // 2
    for source, target in zip(refs[:half], refs[half:]):
        width = source.shape[1] // count
        for slot, member in enumerate(members()):
            there = pl.ds(pl.multiple_of(member * width, width), width)
            here = slice(slot * width, (slot + 1) * width)
            if inverse:
                target[:, there] = source[:, here]
            else:
                target[:, here] = source[:, there]


def join_kernel(*refs):
    out_ref = refs[-1]
    mine = lax.axis_index("tensor")
    count = refs[0].shape[0]
    for index, ref in enumerate(refs[:-1]):
        out_ref[pl.ds(pl.multiple_of((mine ^ index) * count, count), count), :] = ref[...]


def ring_order(count):
    return list(range(0, count, 2)) + list(range(count - 1, 0, -2))


class Ring:
    def __init__(self, count):
        self.count = count
        self.half = count // 2
        order = ring_order(count)
        self.up = [(order[i], order[(i + 1) % count]) for i in range(count)]
        self.down = [(b, a) for a, b in self.up]
        self.offsets = [0]
        for step in range(1, self.half):
            self.offsets += [-step, step]
        self.offsets.append(self.half)

    def members(self):
        count = self.count
        index = lax.axis_index("dp")
        here = jnp.where(index % 2 == 0, index // 2, count - 1 - index // 2)
        spots = [lax.rem(here + (offset + count), count) for offset in self.offsets]
        return [jnp.where(spot < count // 2, 2 * spot, 2 * (count - 1 - spot) + 1) for spot in spots]

    def shuffle(self, *arrays, inverse=False):
        if arrays[0].shape[1] // self.count % 128:
            return [self.shuffle_narrow(array, inverse) for array in arrays]
        return pl.pallas_call(
            functools.partial(shuffle_kernel, self.members, self.count, inverse),
            out_shape=[jax.ShapeDtypeStruct(array.shape, array.dtype) for array in arrays],
            compiler_params=pltpu.CompilerParams(vmem_limit_bytes=VMEM),
            cost_estimate=lasting(1.5),
            name="shuffle",
        )(*arrays)

    def shuffle_narrow(self, values, inverse):
        width = values.shape[1] // self.count
        if not inverse:
            pieces = [lax.dynamic_slice_in_dim(values, m * width, width, 1) for m in self.members()]
            return jnp.concatenate(pieces, axis=1)
        out = jnp.zeros_like(values)
        for slot, member in enumerate(self.members()):
            piece = values[:, slot * width : (slot + 1) * width]
            out = lax.dynamic_update_slice_in_dim(out, piece, member * width, 1)
        return out

    def gather(self, shard):
        pieces = [shard]
        marks = []
        above = below = shard
        for _ in range(1, self.half):
            above = lax.ppermute(above, "dp", self.up)
            below = lax.ppermute(below, "dp", self.down)
            pieces += [above, below]
            marks.append((above, below))
        cut = shard.shape[0] // 2
        upper = lax.ppermute(above[:cut], "dp", self.up)
        lower = lax.ppermute(below[cut:], "dp", self.down)
        pieces += [upper, lower]
        marks.append((upper, lower))
        return pieces, marks

    def reduce_far(self, far):
        cut = far.shape[0] // 2
        above = lax.ppermute(far[:cut].astype(HALF), "dp", self.up)
        below = lax.ppermute(far[cut:].astype(HALF), "dp", self.down)
        return above, below

    def reduce_second(self, part, first):
        above, below = first
        cut = above.shape[0]
        top = part(self.count - 2).astype(FULL)
        low = part(self.count - 3).astype(FULL)
        top = jnp.concatenate([top[:cut] + above.astype(FULL), top[cut:]], axis=0)
        low = jnp.concatenate([low[:cut], low[cut:] + below.astype(FULL)], axis=0)
        return top.astype(HALF), low.astype(HALF)

    def reduce(self, part, second=None):
        if second is None:
            second = self.reduce_second(part, self.reduce_far(part(self.count - 1)))
        top, low = second
        arrived, sent = [], []
        for step in range(self.half - 1, 0, -1):
            if step < self.half - 1:
                top = (part(2 * step).astype(FULL) + above.astype(FULL)).astype(HALF)
                low = (part(2 * step - 1).astype(FULL) + below.astype(FULL)).astype(HALF)
            above = lax.ppermute(top, "dp", self.up)
            below = lax.ppermute(low, "dp", self.down)
            sent.append((top, low))
            arrived.append((above, below))
        return part(0).astype(FULL) + above.astype(FULL) + below.astype(FULL), arrived, sent

    def gather_rows(self, rows):
        first = lax.ppermute(rows, "tensor", beside(2))
        near = lax.ppermute(rows, "tensor", beside(1))
        far = lax.ppermute(first, "tensor", beside(1))
        return pl.pallas_call(
            join_kernel,
            out_shape=jax.ShapeDtypeStruct((4 * rows.shape[0], rows.shape[1]), rows.dtype),
            compiler_params=pltpu.CompilerParams(vmem_limit_bytes=VMEM),
            cost_estimate=lasting(2.0),
            name="join",
        )(rows, near, first, far)

    def scatter_rows(self, values):
        mine = lax.axis_index("tensor")
        count = values.shape[0] // 4

        def piece(index):
            return lax.dynamic_slice_in_dim(values, (mine ^ index) * count, count, 0)

        across = lax.ppermute(piece(3), "tensor", beside(1)).astype(FULL)
        near = lax.ppermute(piece(1), "tensor", beside(1)).astype(FULL)
        send = (piece(2).astype(FULL) + across).astype(HALF)
        far = lax.ppermute(send, "tensor", beside(2)).astype(FULL)
        return piece(0).astype(FULL) + near + far

    def lengths(self, counts):
        return counts[0]


def beside(index):
    return [(i, i ^ index) for i in range(4)]


def per_device(
    tokens,
    query_weight,
    key_weight,
    value_weight,
    output_weight,
    gate_weight,
    up_weight,
    down_weight,
    attention_gain,
    feed_gain,
    doc_lengths,
    cotangent,
):
    ring = Ring(lax.axis_size("dp"))
    own_rows, width = tokens.shape
    block = query_weight.shape[0]

    inner = query_weight.shape[1]
    kv_width = key_weight.shape[1]
    joint = inner + 2 * kv_width
    units = gate_weight.shape[1]
    slots = ring.count
    output_shard = output_weight.astype(HALF)
    gains = jnp.stack([attention_gain, feed_gain]).astype(HALF)
    first_shard = jnp.concatenate(
        [
            jnp.concatenate([query_weight, key_weight, value_weight], axis=1).astype(HALF),
            *[output_shard[at : at + block] for at in range(0, inner, block)],
        ],
        axis=1,
    )
    gains = jnp.pad(gains, ((0, 30), (0, first_shard.shape[1] - block)))
    first_shard = jnp.concatenate([first_shard, gains], axis=0)
    first_pieces, first_marks = ring.gather(first_shard)
    down_pieces, down_marks = ring.gather(tie(down_weight.astype(HALF), first_marks[-2]))
    feed_shard = jnp.concatenate([gate_weight, up_weight], axis=1).astype(HALF)
    feed_pieces, feed_marks = ring.gather(tie(feed_shard, down_marks[-2]))
    tokens, cotangent = ring.shuffle(tie(tokens, first_shard), cotangent)
    view = functools.partial(output_view, block, joint)

    total = own_rows * lax.axis_size("tensor")
    position, valid, allowed = group_layout(ring.lengths(doc_lengths), total)
    begin = (jnp.arange(total, dtype=jnp.int32) - position.astype(jnp.int32)).reshape(1, total)
    cosine, sine = angle_tables(position)
    cosine = jnp.tile(cosine, (1, 4))
    sine = jnp.concatenate([-sine, sine, -sine, sine], axis=1)
    resid = tokens.astype(FULL)
    scale_one = rms_scale(resid)
    rows_in = ring.gather_rows(tokens)
    rows_one, joined, gains = first(rows_in, first_pieces, slots, block, joint)
    gain_one, gain_two = gains[0], gains[1]
    queries, keys_values, attended, logsum = attend(
        tie(joined, down_marks[0]), cosine, sine, begin, valid.reshape(1, total)
    )
    middle = resid + ring.scatter_rows(
        outward(
            tie(attended, down_marks[1]),
            first_pieces,
            slots,
            first_shard.shape[0],
            block,
            False,
            5.2,
            "output",
            view,
        )
    )
    scale_two = rms_scale(middle)
    rows_two = ring.gather_rows((middle * scale_two * gain_two).astype(HALF))
    grad_out = cotangent.astype(FULL)
    grad_rows = ring.gather_rows(cotangent)
    grad_hidden = hidden_back(grad_rows, down_pieces, slots)
    hidden, grad_feed = gate_up(rows_two, grad_hidden, feed_pieces)

    mid, far = (slots - 3) * block, (slots - 1) * block
    feed_far = contract_rows(rows_two[:, far:], grad_feed).astype(HALF)
    down_far = contract_rows(hidden, grad_rows[:, far:]).astype(HALF)
    feed_first = ring.reduce_far(feed_far)
    down_first = ring.reduce_far(down_far)
    partial_two = outward(
        tie(grad_feed, feed_far, down_far), feed_pieces, slots, block, block, True, 16.2, "feed_back"
    )
    rows_mid, hidden_mid = tie((rows_two, hidden), partial_two, feed_first, down_first)
    feed_mid = contract_rows(rows_mid[:, mid:far], grad_feed).astype(HALF)
    down_mid = contract_rows(hidden_mid, grad_rows[:, mid:far]).astype(HALF)
    feed_near = down_near = None

    def feed_part(slot):
        if slot >= slots - 3:
            return feed_mid[(slot - slots + 3) * block :][:block]
        return feed_near[slot * block : (slot + 1) * block]

    def down_part(slot):
        if slot >= slots - 3:
            return down_mid[:, (slot - slots + 3) * block :][:, :block]
        return down_near[:, slot * block : (slot + 1) * block]

    feed_second = ring.reduce_second(feed_part, feed_first)
    down_second = ring.reduce_second(down_part, down_first)
    rows_near, hidden_near = tie((rows_two, hidden), feed_second, down_second)
    feed_near = contract_rows(rows_near[:, :mid], grad_feed).astype(HALF)
    down_near = contract_rows(hidden_near, grad_rows[:, :mid]).astype(HALF)
    feed_sum, feed_steps, feed_sent = ring.reduce(feed_part, feed_second)
    down_sum, down_steps, down_sent = ring.reduce(down_part, down_second)
    grad_normed_two = ring.scatter_rows(partial_two)
    grad_gain_two = jnp.sum(grad_normed_two * middle * scale_two, axis=0)
    inner_two = grad_normed_two * gain_two
    grad_middle = (
        grad_out
        + scale_two * inner_two
        - middle * scale_two**3 * jnp.mean(inner_two * middle, axis=1, keepdims=True)
    )
    middle_rows = ring.gather_rows(grad_middle.astype(HALF))
    grad_attended = mixed_back(tie(middle_rows, feed_sent[1], down_sent[1]), first_pieces, valid[:, None], slots, inner, view)
    grad_joined = attend_back(queries, keys_values, grad_attended, logsum, cosine, sine, begin)
    late_joined = tie(grad_joined, feed_sent[2], down_sent[2])
    first_sum, _, _ = ring.reduce(
        lambda slot: contract_rows(rows_one[:, slot * block : (slot + 1) * block], late_joined)
    )
    partial_one, grad_gain_one = first_back(late_joined, rows_in, first_pieces, slots, block)
    both = jnp.concatenate([grad_gain_one, grad_gain_two[None]], axis=0)

    def output_part(slot):
        there = slice(slot * block, (slot + 1) * block)
        extra = jnp.pad(both[:, there], ((0, 30), (0, 0)))
        return jnp.concatenate([contract_rows(attended, middle_rows[:, there]), extra], axis=0)

    output_sum, _, _ = ring.reduce(output_part)
    gain_sum = lax.psum(output_sum[inner : inner + 2], "tensor")
    output_sum = output_sum[:inner]
    layer_out = (
        middle
        + ring.scatter_rows(
            outward(tie(hidden, grad_joined), down_pieces, slots, units, block, False, 9.2, "down")
        )
    ).astype(HALF)
    grad_normed_one = ring.scatter_rows(partial_one)
    inner_one = grad_normed_one * gain_one
    input_grad = (
        grad_middle
        + scale_one * inner_one
        - resid * scale_one**3 * jnp.mean(inner_one * resid, axis=1, keepdims=True)
    )
    layer_out, input_grad = ring.shuffle(layer_out, input_grad, inverse=True)
    return (
        layer_out,
        input_grad,
        first_sum[:, :inner],
        first_sum[:, inner : inner + kv_width],
        first_sum[:, inner + kv_width :],
        output_sum,
        feed_sum[:, :units],
        feed_sum[:, units:],
        down_sum,
        gain_sum[0],
        gain_sum[1],
    )


def solution(mesh):
    placed = (
        P(("dp", "tensor"), None),
        P("dp", "tensor"),
        P("dp", "tensor"),
        P("dp", "tensor"),
        P("tensor", "dp"),
        P("dp", "tensor"),
        P("dp", "tensor"),
        P("tensor", "dp"),
        P("dp"),
        P("dp"),
        P("dp", None),
        P(("dp", "tensor"), None),
    )
    return jax.shard_map(
        per_device,
        mesh=mesh,
        in_specs=placed,
        out_specs=(
            P(("dp", "tensor"), None),
            P(("dp", "tensor"), None),
            P("dp", "tensor"),
            P("dp", "tensor"),
            P("dp", "tensor"),
            P("tensor", "dp"),
            P("dp", "tensor"),
            P("dp", "tensor"),
            P("tensor", "dp"),
            P("dp"),
            P("dp"),
        ),
        check_vma=False,
    )
```

time: 783 us -> 547 us (0.70)
  matrix products: 207 us -> 39.3 us
  Pallas kernels: 0 us -> 132 us
  local copies, waits for them, and re-layouts: 116 us -> 21.2 us
  waiting for transfers between devices: 269 us -> 222 us
  starting transfers between devices: 106 us -> 74.3 us
  between operations: 14.6 us -> 2.21 us
  other arithmetic: 49.2 us -> 39.1 us
    pallas_call x0 -> x16, Pallas kernels: none -> 132 us  [the longest x3 30.7 us: outward(): pl.pallas_call(functools.partial(outward_kernel, slots, depth, view, tran...]
    dot_general x50 -> x0, matrix products: 125 us -> none  [the longest x29 69 us: contract_cols(): lax.dot_general(left, right, (((1,), (1,)), ((), ())), preferred_element_...]
    ppermute x56 -> x40, waiting for transfers between devices: 162 us -> 103 us  [the longest x12 78.2 us: reduce(): above = lax.ppermute(top, 'dp', self.up)]
    ppermute x15 -> x9, waiting for transfers between devices: 32.4 us -> 87.8 us  [gather(): above = lax.ppermute(above, 'dp', self.up)]
    unnamed x198 -> x116, local copies, waits for them, and re-layouts: 59.3 us -> 5.63 us
    dot_general x56 -> x22, matrix products: 81.3 us -> 39.3 us  [contract_rows(): lax.dot_general(left, right, (((0,), (0,)), ((), ())), preferred_element_...]
    ppermute x15 -> x9, waiting for transfers between devices: 29.2 us -> 2.17 us  [gather(): below = lax.ppermute(below, 'dp', self.down)]
    dynamic_update_slice x38 -> x0, local copies, waits for them, and re-layouts: 23.9 us -> none  [the longest x14 12.7 us: gather_rows(): out = lax.dynamic_update_slice_in_dim(out, piece, (mine ^ index) * count, 0)]
  transfers between devices with their start and end apart: 112 -> 80, of which waited for: 50 -> 37; matrix products, arithmetic and copies ran while one was open for 42% -> 16% of each run, Pallas kernels for 0% -> 21%
where the time goes in v2:
time: 547 us; the launch traced here: 538 us
  waiting for transfers between devices  222 us (41%)
  Pallas kernels  132 us (24%)
  starting transfers between devices  74.3 us (14%)
  matrix products  39.3 us (7%)
  other arithmetic  39.1 us (7%)
  local copies, waits for them, and re-layouts  21.2 us (4%)
  blocking collectives  7.54 us (1%)
    ppermute x9, waiting for transfers between devices, gather(): above = lax.ppermute(above, 'dp', self.up)  87.8 us
    ppermute x12, waiting for transfers between devices, reduce(): above = lax.ppermute(top, 'dp', self.up)  78.2 us
    dot_general x22, matrix products, contract_rows(): lax.dot_general(left, right, (((0,), (0,)), ((), ())), preferred_element_...  39.3 us
    pallas_call x3, Pallas kernels, outward(): pl.pallas_call(functools.partial(outward_kernel, slots, depth, view, tran...  30.7 us
    pallas_call x1, Pallas kernels, gate_up(): pl.pallas_call(functools.partial(gate_up_kernel, units), grid=(total // T...  17 us
    pallas_call x1, Pallas kernels, attend_back(): pl.pallas_call(bwd_kernel, out_shape=jax.ShapeDtypeStruct((total, wide +...  16.3 us
    ppermute x9, starting transfers between devices, gather(): above = lax.ppermute(above, 'dp', self.up)  15.9 us
    pallas_call x1, Pallas kernels, attend(): pl.pallas_call(fwd_kernel, out_shape=(jax.ShapeDtypeStruct((total, heads...  14.9 us
  transfers between devices with their start and end apart: 80, of which 37 were waited for; matrix products, arithmetic and copies ran while one was open for 16% of the time, Pallas kernels for 21%

profile of v2, /device:TPU:0, one launch (start us, length us, event | category | flops | bytes accessed | tf_op | source)
XLA Modules:
  0.0 537.7 jit_solution(1577276752294024795)
XLA Ops:
  5.7 14.9 %collective-permute-done.3.refs_1_ = bf16[288,1152]{1,0:T(8,128)(2,1)} collective-permute-done((bf16[288,1152]{1,0:T(8,128)(2,1)S(1)}, bf16[288,1152]{1,0:T(8,128)(2,1)}, u32[]{:S(2)}, u32[]{:S(2)}) %collective-permute-start.3) | collective-permute-done | bytes 663584 | tf_op jit(solution)/shard_map/ppermute | solution.py:476
  44.1 8.4 %collective-permute-done.7.refs_5_ = bf16[288,1152]{1,0:T(8,128)(2,1)S(1)} collective-permute-done((bf16[288,1152]{1,0:T(8,128)(2,1)}, bf16[288,1152]{1,0:T(8,128)(2,1)S(1)}, u32[]{:S(2)}, u32[]{:S(2)}) %collective-permute-start.7) | collective-permute-done | bytes 663584 | tf_op jit(solution)/shard_map/ppermute | solution.py:476
  66.2 6.4 %collective-permute-done.11.refs_1_ = bf16[1408,256]{1,0:T(8,128)(2,1)} collective-permute-done((bf16[1408,256]{1,0:T(8,128)(2,1)S(1)}, bf16[1408,256]{1,0:T(8,128)(2,1)}, u32[]{:S(2)}, u32[]{:S(2)}) %collective-permute-start.11) | collective-permute-done | bytes 720928 | tf_op jit(solution)/shard_map/ppermute | solution.py:476
  74.6 6.7 %collective-permute-done.10.refs_8_ = bf16[144,1152]{1,0:T(8,128)(2,1)} collective-permute-done((bf16[144,1152]{1,0:T(8,128)(2,1)S(1)}, bf16[144,1152]{1,0:T(8,128)(2,1)}, u32[]{:S(2)}, u32[]{:S(2)}) %collective-permute-start.10) | collective-permute-done | bytes 331808 | tf_op jit(solution)/shard_map/ppermute | solution.py:482
  81.2 7.6 %first.1 = (bf16[768,2048]{1,0:T(8,128)(2,1)}, f32[768,640]{1,0:T(8,128)}, f32[2,2048]{1,0:T(2,128)}) custom-call(bf16[768,2048]{1,0:T(8,128)(2,1)} %join.4.x_ref, bf16[288,1152]{1,0:T(8,128)(2,1)} %copy-done.16, bf16[288,1152]{1,0:T(8,128)(2,1)} %collective-permute-done.3.refs_1_, bf16[288,1152]{1,0:T(8,128)(2,1)} %collective-permute-done.4.refs_2_, ...), custom_call_target="tpu_custom_call" | custom-call | flops 7699999744 | tf_op jit(solution)/shard_map/first/pallas_call | solution.py:332
  94.3 14.9 %attend.1 = (bf16[768,512]{1,0:T(8,128)(2,1)}, bf16[768,128]{1,0:T(8,128)(2,1)}, bf16[768,512]{1,0:T(8,128)(2,1)}, f32[8,1,768]{2,1,0:T(1,128)}) custom-call(f32[768,640]{1,0:T(8,128)} %get-tuple-element.43.joined_ref, f32[768,128]{1,0:T(8,128)} %copy.45.cos_ref, f32[768,128]{1,0:T(8,128)} %pad_maximum_fusion.6.sin_ref, ...), custom_call_target="tpu_custom_call" | custom-call | flops 14300000256 | tf_op jit(solution)/shard_map/attend/pallas_call | solution.py:127
  111.3 6.1 %output.1 = bf16[768,2048]{1,0:T(8,128)(2,1)} custom-call(bf16[768,512]{1,0:T(8,128)(2,1)} %get-tuple-element.45.x_ref, bf16[288,1152]{1,0:T(8,128)(2,1)} %copy-done.16, bf16[288,1152]{1,0:T(8,128)(2,1)} %collective-permute-done.3.refs_1_, bf16[288,1152]{1,0:T(8,128)(2,1)} %collective-permute-done.4.refs_2_, ...), custom_call_target="tpu_custom_call" | custom-call | flops 5720000000 | tf_op jit(solution)/shard_map/output/pallas_call | solution.py:295
  121.7 19.3 %collective-permute-done.28.refs_1_ = bf16[256,2816]{1,0:T(8,128)(2,1)} collective-permute-done((bf16[256,2816]{1,0:T(8,128)(2,1)}, bf16[256,2816]{1,0:T(8,128)(2,1)}, u32[]{:S(2)}, u32[]{:S(2)}) %collective-permute-start.28) | collective-permute-done | bytes 1441824 | tf_op jit(solution)/shard_map/ppermute | solution.py:476
  147.4 9.5 %collective-permute-done.17 = bf16[192,2048]{1,0:T(8,128)(2,1)} collective-permute-done((bf16[192,2048]{1,0:T(8,128)(2,1)S(1)}, bf16[192,2048]{1,0:T(8,128)(2,1)}, u32[]{:S(2)}, u32[]{:S(2)}) %collective-permute-start.17) | collective-permute-done | bytes 786464 | tf_op jit(solution)/shard_map/ppermute | solution.py:539
  159.0 13.8 %collective-permute-done.30.refs_3_ = bf16[256,2816]{1,0:T(8,128)(2,1)} collective-permute-done((bf16[256,2816]{1,0:T(8,128)(2,1)}, bf16[256,2816]{1,0:T(8,128)(2,1)}, u32[]{:S(2)}, u32[]{:S(2)}) %collective-permute-start.30) | collective-permute-done | bytes 1441824 | tf_op jit(solution)/shard_map/ppermute | solution.py:476
  187.2 15.6 %collective-permute-done.32.refs_5_ = bf16[256,2816]{1,0:T(8,128)(2,1)S(1)} collective-permute-done((bf16[256,2816]{1,0:T(8,128)(2,1)}, bf16[256,2816]{1,0:T(8,128)(2,1)S(1)}, u32[]{:S(2)}, u32[]{:S(2)}) %collective-permute-start.32) | collective-permute-done | bytes 1441824 | tf_op jit(solution)/shard_map/ppermute | solution.py:476
  208.6 9.6 %hidden_back.1.grad_ref = f32[768,1408]{1,0:T(8,128)} custom-call(bf16[768,2048]{1,0:T(8,128)(2,1)} %join.6.x_ref, bf16[1408,256]{1,0:T(8,128)(2,1)} %convert_element_type.365.refs_0_, bf16[1408,256]{1,0:T(8,128)(2,1)} %collective-permute-done.11.refs_1_, bf16[1408,256]{1,0:T(8,128)(2,1)} %collective-permute-done.12.refs_2_, bf16[1408,256]{1,0:T(8,128)(2,1)} %copy-done.43, ...), custom_call_target="tpu_custom_call" | custom-call | flops 11879999488 | tf_op jit(solution)/shard_map/hidden_back/pallas_call | solution.py:272
  223.5 17.0 %gate_up.1 = (bf16[768,1408]{1,0:T(8,128)(2,1)}, bf16[768,2816]{1,0:T(8,128)(2,1)}) custom-call(bf16[768,2048]{1,0:T(8,128)(2,1)} %join.5.x_ref, f32[768,1408]{1,0:T(8,128)} %hidden_back.1.grad_ref, bf16[256,2816]{1,0:T(8,128)(2,1)} %pad_maximum_fusion.refs_0_, bf16[256,2816]{1,0:T(8,128)(2,1)} %collective-permute-done.28.refs_1_, ...), custom_call_target="tpu_custom_call" | custom-call | flops 18150000640 | tf_op jit(solution)/shard_map/gate_up/pallas_call | solution.py:244
  250.5 15.3 %feed_back.1 = bf16[768,2048]{1,0:T(8,128)(2,1)} custom-call(bf16[768,2816]{1,0:T(8,128)(2,1)} %get-tuple-element.53.x_ref, bf16[256,2816]{1,0:T(8,128)(2,1)} %pad_maximum_fusion.refs_0_, bf16[256,2816]{1,0:T(8,128)(2,1)} %collective-permute-done.28.refs_1_, bf16[256,2816]{1,0:T(8,128)(2,1)} %collective-permute-done.29.refs_2_, ...), custom_call_target="tpu_custom_call" | custom-call | flops 17820000256 | tf_op jit(solution)/shard_map/feed_back/pallas_call | solution.py:295
  287.7 7.6 %collective-permute-done.49 = bf16[1408,256]{1,0:T(8,128)(2,1)S(1)} collective-permute-done((bf16[1408,256]{1,0:T(8,128)(2,1)S(1)}, bf16[1408,256]{1,0:T(8,128)(2,1)S(1)}, u32[]{:S(2)}, u32[]{:S(2)}) %collective-permute-start.49) | collective-permute-done | bytes 720928 | tf_op jit(solution)/shard_map/ppermute | solution.py:512
  305.2 6.4 %convolution_convert_fusion = bf16[1280,2816]{1,0:T(8,128)(2,1)S(1)} fusion(bf16[768,2816]{1,0:T(8,128)(2,1)S(1)} %bitcast.48, bf16[768,2048]{1,0:T(8,128)(2,1)S(1)} %copy-done.52), kind=kOutput, calls=%fused_computation | convolution fusion | flops 5540085760 | bytes 13500416 | tf_op jit(solution)/shard_map/dot_general | solution.py:42
  311.6 31.6 %collective-permute-done.55 = bf16[1408,256]{1,0:T(8,128)(2,1)S(1)} collective-permute-done((bf16[1408,256]{1,0:T(8,128)(2,1)S(1)}, bf16[1408,256]{1,0:T(8,128)(2,1)S(1)}, u32[]{:S(2)}, u32[]{:S(2)}) %collective-permute-start.55) | collective-permute-done | bytes 720928 | tf_op jit(solution)/shard_map/ppermute | solution.py:511
  347.7 15.2 %collective-permute-done.78 = bf16[1408,256]{1,0:T(8,128)(2,1)S(1)} collective-permute-done((bf16[1408,256]{1,0:T(8,128)(2,1)S(1)}, bf16[1408,256]{1,0:T(8,128)(2,1)S(1)}, u32[]{:S(2)}, u32[]{:S(2)}) %collective-permute-start.78) | collective-permute-done | bytes 720928 | tf_op jit(solution)/shard_map/ppermute | solution.py:511
  374.9 6.6 %mixed_back.1.do_ref = bf16[768,512]{1,0:T(8,128)(2,1)} custom-call(bf16[768,2048]{1,0:T(8,128)(2,1)} %join.7.x_ref, bf16[288,1152]{1,0:T(8,128)(2,1)} %copy-done.16, bf16[288,1152]{1,0:T(8,128)(2,1)} %collective-permute-done.3.refs_1_, bf16[288,1152]{1,0:T(8,128)(2,1)} %collective-permute-done.4.refs_2_, bf16[288,1152]{1,0:T(8,128)(2,1)} %collective-permute-done.5.refs_3_, ...), custom_call_target="tpu_custom_call" | custom-call | flops 5939999744 | tf_op jit(solution)/shard_map/mixed_back/pallas_call | solution.py:393
  381.5 16.3 %attend_back.1.grad_ref = bf16[768,640]{1,0:T(8,128)(2,1)} custom-call(bf16[768,512]{1,0:T(8,128)(2,1)} %get-tuple-element.50.q_ref, bf16[768,128]{1,0:T(8,128)(2,1)} %get-tuple-element.51.kv_ref, bf16[768,512]{1,0:T(8,128)(2,1)} %mixed_back.1.do_ref, f32[8,1,768]{2,1,0:T(1,128)} %get-tuple-element.59.lse_ref, f32[768,128]{1,0:T(8,128)} %copy.45.cos_ref, ...), custom_call_target="tpu_custom_call" | custom-call | flops 15950000128 | tf_op jit(solution)/shard_map/attend_back/pallas_call | solution.py:193
  397.9 9.3 %down.1 = bf16[768,2048]{1,0:T(8,128)(2,1)} custom-call(bf16[768,1408]{1,0:T(8,128)(2,1)} %get-tuple-element.60.x_ref, bf16[1408,256]{1,0:T(8,128)(2,1)} %convert_element_type.365.refs_0_, bf16[1408,256]{1,0:T(8,128)(2,1)} %collective-permute-done.11.refs_1_, bf16[1408,256]{1,0:T(8,128)(2,1)} %collective-permute-done.12.refs_2_, ...), custom_call_target="tpu_custom_call" | custom-call | flops 10119999488 | tf_op jit(solution)/shard_map/down/pallas_call | solution.py:295
  422.5 7.9 %first_back.1 = (bf16[768,2048]{1,0:T(8,128)(2,1)}, f32[1,2048]{1,0:T(1,128)}) custom-call(bf16[768,640]{1,0:T(8,128)(2,1)} %attend_back.1.grad_ref, bf16[768,2048]{1,0:T(8,128)(2,1)} %join.4.x_ref, bf16[288,1152]{1,0:T(8,128)(2,1)} %copy-done.16, bf16[288,1152]{1,0:T(8,128)(2,1)} %collective-permute-done.3.refs_1_, ...), custom_call_target="tpu_custom_call" | custom-call | flops 7699999744 | tf_op jit(solution)/shard_map/first_back/pallas_call | solution.py:368
  485.3 7.5 %psum.7 = f32[2,256]{1,0:T(2,128)S(1)} all-reduce(f32[2,256]{1,0:T(2,128)S(1)} %slice.454), channel_id=1, replica_groups=mesh['dp'=8,'tensor'=4] {'tensor'}, use_global_device_ids=true, to_apply=%region_8.9 | all-reduce | flops 512 | bytes 4096 | tf_op jit(solution)/shard_map/psum | solution.py:679
  498.4 16.5 %collective-permute-done.63 = bf16[256,640]{1,0:T(8,128)(2,1)S(1)} collective-permute-done((bf16[256,640]{1,0:T(8,128)(2,1)}, bf16[256,640]{1,0:T(8,128)(2,1)S(1)}, u32[]{:S(2)}, u32[]{:S(2)}) %collective-permute-start.63) | collective-permute-done | bytes 327712 | tf_op jit(solution)/shard_map/ppermute | solution.py:511
  (396 shorter events, 245.6 us)
Async XLA Ops:
  27.3 30.5 %collective-permute-start = (bf16[192,2048]{1,0:T(8,128)(2,1)}, bf16[192,2048]{1,0:T(8,128)(2,1)}, u32[]{:S(2)}, u32[]{:S(2)}) collective-permute-start(bf16[192,2048]{1,0:T(8,128)(2,1)} %get-tuple-element.40.refs_0_), channel_id=1, source_target_pairs={{0,1},{1,0},{2,3},{3,2},{4,5},{5,4},{6,7},{7,6},{8,9},{9,8},{10,11... | collective-permute-start | bytes 2359304 | tf_op jit(solution)/shard_map/ppermute | solution.py:519
  109.2 31.8 %collective-permute-start.28 = (bf16[256,2816]{1,0:T(8,128)(2,1)}, bf16[256,2816]{1,0:T(8,128)(2,1)}, u32[]{:S(2)}, u32[]{:S(2)}) collective-permute-start(bf16[256,2816]{1,0:T(8,128)(2,1)} %pad_maximum_fusion.refs_0_), channel_id=1, source_target_pairs={{0,8},{8,16},{16,24},{24,28},{28,20},{20,12},{12,4},{4,0},{1,9},{9... | collective-permute-start | bytes 4325384 | tf_op jit(solution)/shard_map/ppermute | solution.py:476
  110.9 31.8 %collective-permute-start.29 = (bf16[256,2816]{1,0:T(8,128)(2,1)}, bf16[256,2816]{1,0:T(8,128)(2,1)}, u32[]{:S(2)}, u32[]{:S(2)}) collective-permute-start(bf16[256,2816]{1,0:T(8,128)(2,1)} %pad_maximum_fusion.refs_0_), channel_id=1, source_target_pairs={{8,0},{16,8},{24,16},{28,24},{20,28},{12,20},{4,12},{0,4},{9,1},{1... | collective-permute-start | bytes 4325384 | tf_op jit(solution)/shard_map/ppermute | solution.py:477
  141.0 31.8 %collective-permute-start.30 = (bf16[256,2816]{1,0:T(8,128)(2,1)}, bf16[256,2816]{1,0:T(8,128)(2,1)}, u32[]{:S(2)}, u32[]{:S(2)}) collective-permute-start(bf16[256,2816]{1,0:T(8,128)(2,1)} %collective-permute-done.28.refs_1_), channel_id=1, source_target_pairs={{0,8},{8,16},{16,24},{24,28},{28,20},{20,12},{12,4},{4,0},{1,9},{9... | collective-permute-start | bytes 4325384 | tf_op jit(solution)/shard_map/ppermute | solution.py:476
  142.6 31.8 %collective-permute-start.31 = (bf16[256,2816]{1,0:T(8,128)(2,1)}, bf16[256,2816]{1,0:T(8,128)(2,1)}, u32[]{:S(2)}, u32[]{:S(2)}) collective-permute-start(bf16[256,2816]{1,0:T(8,128)(2,1)} %collective-permute-done.29.refs_2_), channel_id=1, source_target_pairs={{8,0},{16,8},{24,16},{28,24},{20,28},{12,20},{4,12},{0,4},{9,1},{1... | collective-permute-start | bytes 4325384 | tf_op jit(solution)/shard_map/ppermute | solution.py:477
  146.9 31.5 %collective-permute-start.23 = (bf16[192,2048]{1,0:T(8,128)(2,1)}, bf16[192,2048]{1,0:T(8,128)(2,1)S(1)}, u32[]{:S(2)}, u32[]{:S(2)}) collective-permute-start(bf16[192,2048]{1,0:T(8,128)(2,1)} %collective-permute-done.22.refs_2_), channel_id=1, source_target_pairs={{0,1},{1,0},{2,3},{3,2},{4,5},{5,4},{6,7},{7,6},{8,9},{9,8},{10,11... | collective-permute-start | bytes 2359304 | tf_op jit(solution)/shard_map/ppermute | solution.py:520
  172.8 30.0 %collective-permute-start.32 = (bf16[256,2816]{1,0:T(8,128)(2,1)}, bf16[256,2816]{1,0:T(8,128)(2,1)S(1)}, u32[]{:S(2)}, u32[]{:S(2)}) collective-permute-start(bf16[256,2816]{1,0:T(8,128)(2,1)} %collective-permute-done.30.refs_3_), channel_id=1, source_target_pairs={{0,8},{8,16},{16,24},{24,28},{28,20},{20,12},{12,4},{4,0},{1,9},{9... | collective-permute-start | bytes 4325384 | tf_op jit(solution)/shard_map/ppermute | solution.py:476
  176.7 30.6 %collective-permute-start.26 = (bf16[704,256]{1,0:T(8,128)(2,1)S(1)}, bf16[704,256]{1,0:T(8,128)(2,1)}, u32[]{:S(2)}, u32[]{:S(2)}) collective-permute-start(bf16[704,256]{1,0:T(8,128)(2,1)S(1)} %slice.387), channel_id=1, source_target_pairs={{0,8},{8,16},{16,24},{24,28},{28,20},{20,12},{12,4},{4,0},{1,9},{9... | collective-permute-start | bytes 1081352 | tf_op jit(solution)/shard_map/ppermute | solution.py:481
  178.4 30.2 %collective-permute-start.27 = (bf16[704,256]{1,0:T(8,128)(2,1)S(1)}, bf16[704,256]{1,0:T(8,128)(2,1)}, u32[]{:S(2)}, u32[]{:S(2)}) collective-permute-start(bf16[704,256]{1,0:T(8,128)(2,1)S(1)} %slice.388), channel_id=1, source_target_pairs={{8,0},{16,8},{24,16},{28,24},{20,28},{12,20},{4,12},{0,4},{9,1},{1... | collective-permute-start | bytes 1081352 | tf_op jit(solution)/shard_map/ppermute | solution.py:482
  187.2 31.0 %collective-permute-start.18 = (bf16[192,2048]{1,0:T(8,128)(2,1)S(1)}, bf16[192,2048]{1,0:T(8,128)(2,1)S(1)}, u32[]{:S(2)}, u32[]{:S(2)}) collective-permute-start(bf16[192,2048]{1,0:T(8,128)(2,1)S(1)} %multiply_convert_fusion.refs_0_), channel_id=1, source_target_pairs={{0,1},{1,0},{2,3},{3,2},{4,5},{5,4},{6,7},{7,6},{8,9},{9,8},{10,11... | collective-permute-start | bytes 2359304 | tf_op jit(solution)/shard_map/ppermute | solution.py:519
  269.7 30.0 %collective-permute-start.36 = (bf16[192,2048]{1,0:T(8,128)(2,1)S(1)}, bf16[192,2048]{1,0:T(8,128)(2,1)S(1)}, u32[]{:S(2)}, u32[]{:S(2)}) collective-permute-start(bf16[192,2048]{1,0:T(8,128)(2,1)S(1)} %get-tuple-element.131), channel_id=1, source_target_pairs={{0,1},{1,0},{2,3},{3,2},{4,5},{5,4},{6,7},{7,6},{8,9},{9,8},{10,11... | collective-permute-start | bytes 2359304 | tf_op jit(solution)/shard_map/ppermute | solution.py:537
  280.7 63.8 %collective-permute-start.46 = (bf16[256,2816]{1,0:T(8,128)(2,1)S(1)}, bf16[256,2816]{1,0:T(8,128)(2,1)S(1)}, u32[]{:S(2)}, u32[]{:S(2)}) collective-permute-start(bf16[256,2816]{1,0:T(8,128)(2,1)S(1)} %pad_maximum_fusion.1), channel_id=1, source_target_pairs={{0,8},{8,16},{16,24},{24,28},{28,20},{20,12},{12,4},{4,0},{1,9},{9... | collective-permute-start | bytes 4325384 | tf_op jit(solution)/shard_map/ppermute | solution.py:511
  295.3 50.8 %collective-permute-start.47 = (bf16[256,2816]{1,0:T(8,128)(2,1)S(1)}, bf16[256,2816]{1,0:T(8,128)(2,1)S(1)}, u32[]{:S(2)}, u32[]{:S(2)}) collective-permute-start(bf16[256,2816]{1,0:T(8,128)(2,1)S(1)} %pad_maximum_fusion.2), channel_id=1, source_target_pairs={{8,0},{16,8},{24,16},{28,24},{20,28},{12,20},{4,12},{0,4},{9,1},{1... | collective-permute-start | bytes 4325384 | tf_op jit(solution)/shard_map/ppermute | solution.py:512
  298.2 45.0 %collective-permute-start.55 = (bf16[1408,256]{1,0:T(8,128)(2,1)S(1)}, bf16[1408,256]{1,0:T(8,128)(2,1)S(1)}, u32[]{:S(2)}, u32[]{:S(2)}) collective-permute-start(bf16[1408,256]{1,0:T(8,128)(2,1)S(1)} %get-tuple-element.126), channel_id=1, source_target_pairs={{0,8},{8,16},{16,24},{24,28},{28,20},{20,12},{12,4},{4,0},{1,9},{9... | collective-permute-start | bytes 2162696 | tf_op jit(solution)/shard_map/ppermute | solution.py:511
  299.7 43.5 %collective-permute-start.56 = (bf16[1408,256]{1,0:T(8,128)(2,1)S(1)}, bf16[1408,256]{1,0:T(8,128)(2,1)S(1)}, u32[]{:S(2)}, u32[]{:S(2)}) collective-permute-start(bf16[1408,256]{1,0:T(8,128)(2,1)S(1)} %get-tuple-element.125), channel_id=1, source_target_pairs={{8,0},{16,8},{24,16},{28,24},{20,28},{12,20},{4,12},{0,4},{9,1},{1... | collective-permute-start | bytes 2162696 | tf_op jit(solution)/shard_map/ppermute | solution.py:512
  303.7 42.3 %collective-permute-start.40 = (bf16[192,2048]{1,0:T(8,128)(2,1)S(1)}, bf16[192,2048]{1,0:T(8,128)(2,1)S(1)}, u32[]{:S(2)}, u32[]{:S(2)}) collective-permute-start(bf16[192,2048]{1,0:T(8,128)(2,1)S(1)} %get-tuple-element.115.refs_0_), channel_id=1, source_target_pairs={{0,2},{1,3},{2,0},{3,1},{4,6},{5,7},{6,4},{7,5},{8,10},{9,11},{10,... | collective-permute-start | bytes 2359304 | tf_op jit(solution)/shard_map/ppermute | solution.py:518
  346.9 71.5 %collective-permute-start.53 = (bf16[256,2816]{1,0:T(8,128)(2,1)S(1)}, bf16[256,2816]{1,0:T(8,128)(2,1)S(1)}, u32[]{:S(2)}, u32[]{:S(2)}) collective-permute-start(bf16[256,2816]{1,0:T(8,128)(2,1)S(1)} %get-tuple-element.122), channel_id=1, source_target_pairs={{0,8},{8,16},{16,24},{24,28},{28,20},{20,12},{12,4},{4,0},{1,9},{9... | collective-permute-start | bytes 4325384 | tf_op jit(solution)/shard_map/ppermute | solution.py:511
  362.9 55.6 %collective-permute-start.54 = (bf16[256,2816]{1,0:T(8,128)(2,1)S(1)}, bf16[256,2816]{1,0:T(8,128)(2,1)S(1)}, u32[]{:S(2)}, u32[]{:S(2)}) collective-permute-start(bf16[256,2816]{1,0:T(8,128)(2,1)S(1)} %get-tuple-element.121), channel_id=1, source_target_pairs={{8,0},{16,8},{24,16},{28,24},{20,28},{12,20},{4,12},{0,4},{9,1},{1... | collective-permute-start | bytes 4325384 | tf_op jit(solution)/shard_map/ppermute | solution.py:512
  411.8 33.7 %collective-permute-start.51 = (bf16[192,2048]{1,0:T(8,128)(2,1)}, bf16[192,2048]{1,0:T(8,128)(2,1)}, u32[]{:S(2)}, u32[]{:S(2)}) collective-permute-start(bf16[192,2048]{1,0:T(8,128)(2,1)} %get-tuple-element.130), channel_id=1, source_target_pairs={{0,1},{1,0},{2,3},{3,2},{4,5},{5,4},{6,7},{7,6},{8,9},{9,8},{10,11... | collective-permute-start | bytes 2359304 | tf_op jit(solution)/shard_map/ppermute | solution.py:536
  411.8 81.6 %collective-permute-start.50 = (bf16[192,2048]{1,0:T(8,128)(2,1)}, bf16[192,2048]{1,0:T(8,128)(2,1)}, u32[]{:S(2)}, u32[]{:S(2)}) collective-permute-start(bf16[192,2048]{1,0:T(8,128)(2,1)} %get-tuple-element.129), channel_id=1, source_target_pairs={{0,1},{1,0},{2,3},{3,2},{4,5},{5,4},{6,7},{7,6},{8,9},{9,8},{10,11... | collective-permute-start | bytes 2359304 | tf_op jit(solution)/shard_map/ppermute | solution.py:537
  453.3 40.6 %collective-permute-start.52 = (bf16[192,2048]{1,0:T(8,128)(2,1)}, bf16[192,2048]{1,0:T(8,128)(2,1)}, u32[]{:S(2)}, u32[]{:S(2)}) collective-permute-start(bf16[192,2048]{1,0:T(8,128)(2,1)} %add_convert_fusion.6), channel_id=1, source_target_pairs={{0,2},{1,3},{2,0},{3,1},{4,6},{5,7},{6,4},{7,5},{8,10},{9,11},{10,... | collective-permute-start | bytes 2359304 | tf_op jit(solution)/shard_map/ppermute | solution.py:539
  477.4 44.3 %collective-permute-start.76 = (bf16[256,2816]{1,0:T(8,128)(2,1)}, bf16[256,2816]{1,0:T(8,128)(2,1)}, u32[]{:S(2)}, u32[]{:S(2)}) collective-permute-start(bf16[256,2816]{1,0:T(8,128)(2,1)} %get-tuple-element.120), channel_id=1, source_target_pairs={{0,8},{8,16},{16,24},{24,28},{28,20},{20,12},{12,4},{4,0},{1,9},{9... | collective-permute-start | bytes 4325384 | tf_op jit(solution)/shard_map/ppermute | solution.py:511
  480.7 41.0 %collective-permute-start.77 = (bf16[256,2816]{1,0:T(8,128)(2,1)}, bf16[256,2816]{1,0:T(8,128)(2,1)}, u32[]{:S(2)}, u32[]{:S(2)}) collective-permute-start(bf16[256,2816]{1,0:T(8,128)(2,1)} %get-tuple-element.119), channel_id=1, source_target_pairs={{8,0},{16,8},{24,16},{28,24},{20,28},{12,20},{4,12},{0,4},{9,1},{1... | collective-permute-start | bytes 4325384 | tf_op jit(solution)/shard_map/ppermute | solution.py:512
  484.4 41.8 %collective-permute-start.57 = (bf16[192,2048]{1,0:T(8,128)(2,1)}, bf16[192,2048]{1,0:T(8,128)(2,1)S(1)}, u32[]{:S(2)}, u32[]{:S(2)}) collective-permute-start(bf16[192,2048]{1,0:T(8,128)(2,1)} %get-tuple-element.127), channel_id=1, source_target_pairs={{0,1},{1,0},{2,3},{3,2},{4,5},{5,4},{6,7},{7,6},{8,9},{9,8},{10,11... | collective-permute-start | bytes 2359304 | tf_op jit(solution)/shard_map/ppermute | solution.py:537
  (113 other events, 1447.7 us)

commit v3 on v2

--- a/solution.py
+++ b/solution.py
@@ -202,7 +202,7 @@
             pltpu.VMEM((total, 128), FULL),
         ],
         compiler_params=pltpu.CompilerParams(vmem_limit_bytes=VMEM),
-        cost_estimate=lasting(14.5),
+        cost_estimate=lasting(0.0),
         name="attend_back",
     )(q, kv, do, lse, cosine, sine, begin)
 
@@ -281,6 +281,61 @@
     )(x, *pieces)
 
 
+def feed_grads_kernel(early, x_ref, feed_ref, grad_ref, hidden_ref, *out_refs):
+    wide = feed_ref.shape[1]
+    half = x_ref.shape[1] // 2
+    over_rows = (((0,), (0,)), ((), ()))
+
+    def make(write):
+        for left, right, there in (
+            (x_ref, feed_ref, slice(0, wide)),
+            (grad_ref, hidden_ref, slice(wide, wide + hidden_ref.shape[1])),
+        ):
+            part = lax.dot_general(left[...], right[...], over_rows, preferred_element_type=FULL)
+            write(there, part.astype(HALF))
+
+    def write_whole(there, part):
+        out_refs[-1][:, there] = part
+
+    def write_halves(there, part):
+        out_refs[0][:, there] = part[:half]
+        out_refs[1][:, there] = part[half:]
+
+    if early:
+        pl.when(pl.program_id(0) == 0)(functools.partial(make, write_halves))
+        pl.when(pl.program_id(0) > 0)(functools.partial(make, write_whole))
+    else:
+        make(write_whole)
+
+
+def feed_grads(x, feed, grad, hidden, slots, block, early):
+    total = x.shape[0]
+    units = hidden.shape[1]
+    if block % 128:
+        parts = []
+        for start, stop in ((slots - 1, slots), (slots - 3, slots - 1)) if early else ((0, slots - 3),):
+            there = slice(start * block, stop * block)
+            part = [contract_rows(x[:, there], feed), contract_rows(grad[:, there], hidden)]
+            parts.append(jnp.concatenate(part, axis=1).astype(HALF))
+        return [*jnp.split(parts[0], 2), parts[1]] if early else parts
+    place = (lambda i: (0, slots - 1 - i)) if early else (lambda i: (0, i))
+    columns = pl.BlockSpec((total, block), place)
+    shapes = [(block // 2, 3 * units)] * 2 + [(2 * block, 3 * units)] if early else [((slots - 3) * block, 3 * units)]
+    out_specs = [pl.BlockSpec((block, 3 * units), (lambda i: (2 - jnp.maximum(i, 1), 0)) if early else (lambda i: (i, 0)))]
+    if early:
+        out_specs = [pl.BlockSpec((block // 2, 3 * units), lambda i: (0, 0))] * 2 + out_specs
+    return pl.pallas_call(
+        functools.partial(feed_grads_kernel, early),
+        grid=(3 if early else slots - 3,),
+        in_specs=[columns, whole(feed), columns, whole(hidden)],
+        out_specs=out_specs,
+        out_shape=[jax.ShapeDtypeStruct(shape, HALF) for shape in shapes],
+        compiler_params=pltpu.CompilerParams(vmem_limit_bytes=VMEM),
+        cost_estimate=lasting(0.0),
+        name="feed_grads",
+    )(x, feed, grad, hidden)
+
+
 def outward_kernel(slots, depth, view, transposed, x_ref, *refs):
     pieces, out_ref = refs[:-1], refs[-1]
     for slot in range(slots):
@@ -345,36 +400,25 @@
     )(x, *pieces)
 
 
-def first_back_kernel(slots, depth, grad_ref, x_ref, *refs):
-    pieces = refs[:-2]
-    out_ref, gain_ref = refs[-2:]
-
-    @pl.when(pl.program_id(0) == 0)
-    def _():
-        gain_ref[...] = jnp.zeros_like(gain_ref)
-
-    values = x_ref[...].astype(FULL)
-    values = values * lax.rsqrt(jnp.mean(values * values, axis=1, keepdims=True) + EPS)
+def first_back_kernel(slots, depth, grad_ref, *refs):
+    pieces, out_ref = refs[:-1], refs[-1]
     for slot in range(slots):
-        there = slice(slot * depth, (slot + 1) * depth)
         block = block_of(pieces, slot, pieces[0].shape[0], slots)[:depth, : grad_ref.shape[1]]
-        part = nt(grad_ref[...], block).astype(HALF)
-        out_ref[:, there] = part
-        gain_ref[:, there] += jnp.sum(part.astype(FULL) * values[:, there], axis=0, keepdims=True)
-
-
-def first_back(grad, x, pieces, slots, depth):
-    total, wide = x.shape
+        out_ref[:, slot * depth : (slot + 1) * depth] = nt(grad_ref[...], block).astype(HALF)
+
+
+def first_back(grad, pieces, slots, depth):
+    total, wide = grad.shape
     return pl.pallas_call(
         functools.partial(first_back_kernel, slots, depth),
         grid=(total // TILE,),
-        in_specs=[rows_of(grad.shape[1]), rows_of(wide)] + [whole(p) for p in pieces],
-        out_specs=[rows_of(wide), pl.BlockSpec((1, wide), lambda i: (0, 0))],
-        out_shape=(jax.ShapeDtypeStruct((total, wide), HALF), jax.ShapeDtypeStruct((1, wide), FULL)),
+        in_specs=[rows_of(wide)] + [whole(p) for p in pieces],
+        out_specs=rows_of(slots * depth),
+        out_shape=jax.ShapeDtypeStruct((total, slots * depth), HALF),
         compiler_params=pltpu.CompilerParams(vmem_limit_bytes=VMEM),
-        cost_estimate=lasting(7.0),
+        cost_estimate=lasting(0.0),
         name="first_back",
-    )(grad, x, *pieces)
+    )(grad, *pieces)
 
 
 def mixed_back_kernel(slots, view, x_ref, *refs):
@@ -397,7 +441,7 @@
         out_specs=rows_of(units),
         out_shape=jax.ShapeDtypeStruct((total, units), HALF),
         compiler_params=pltpu.CompilerParams(vmem_limit_bytes=VMEM),
-        cost_estimate=lasting(5.4),
+        cost_estimate=lasting(0.0),
         name="mixed_back",
     )(x, *pieces, valid)
 
@@ -423,6 +467,70 @@
         out_ref[pl.ds(pl.multiple_of((mine ^ index) * count, count), count), :] = ref[...]
 
 
+class Travel:
+    def __init__(self, ring, shard):
+        self.ring = ring
+        self.pieces = [shard]
+        self.marks = []
+        self.above = self.below = shard
+
+    def step(self, *after):
+        ring = self.ring
+        if after:
+            self.above, self.below = tie((self.above, self.below), *after)
+        if len(self.marks) == ring.half - 1:
+            cut = self.above.shape[0] // 2
+            self.above, self.below = self.above[:cut], self.below[cut:]
+        self.above = lax.ppermute(self.above, "dp", ring.up)
+        self.below = lax.ppermute(self.below, "dp", ring.down)
+        self.pieces += [self.above, self.below]
+        self.marks.append((self.above, self.below))
+
+    def steps(self, count):
+        for _ in range(count):
+            self.step()
+        return self
+
+
+class Homeward:
+    def __init__(self, ring, part, far):
+        self.ring = ring
+        self.part = part
+        self.left = ring.half - 1
+        self.cut = far[0].shape[0]
+        self.send(*far)
+
+    def send(self, top, low):
+        self.above = lax.ppermute(top, "dp", self.ring.up)
+        self.below = lax.ppermute(low, "dp", self.ring.down)
+        self.sent, self.arrived = (top, low), (self.above, self.below)
+
+    def total(self, slot, arrived, upper):
+        own = self.part(slot)
+        first = 0 if upper else own.shape[0] - arrived.shape[0]
+        last = first + arrived.shape[0]
+        joined = (own[first:last].astype(FULL) + arrived.astype(FULL)).astype(HALF)
+        return jnp.concatenate([own[:first], joined, own[last:]], axis=0)
+
+    def step(self, *after):
+        above, below = self.above, self.below
+        if after:
+            above, below = tie((above, below), *after)
+        top = self.total(2 * self.left, above, True)
+        low = self.total(2 * self.left - 1, below, False)
+        self.left -= 1
+        self.send(top, low)
+        return self
+
+    def steps(self, count):
+        for _ in range(count):
+            self.step()
+        return self
+
+    def own(self):
+        return self.part(0).astype(FULL) + self.above.astype(FULL) + self.below.astype(FULL)
+
+
 def ring_order(count):
     return list(range(0, count, 2)) + list(range(count - 1, 0, -2))
 
@@ -469,50 +577,7 @@
         return out
 
     def gather(self, shard):
-        pieces = [shard]
-        marks = []
-        above = below = shard
-        for _ in range(1, self.half):
-            above = lax.ppermute(above, "dp", self.up)
-            below = lax.ppermute(below, "dp", self.down)
-            pieces += [above, below]
-            marks.append((above, below))
-        cut = shard.shape[0] // 2
-        upper = lax.ppermute(above[:cut], "dp", self.up)
-        lower = lax.ppermute(below[cut:], "dp", self.down)
-        pieces += [upper, lower]
-        marks.append((upper, lower))
-        return pieces, marks
-
-    def reduce_far(self, far):
-        cut = far.shape[0] // 2
-        above = lax.ppermute(far[:cut].astype(HALF), "dp", self.up)
-        below = lax.ppermute(far[cut:].astype(HALF), "dp", self.down)
-        return above, below
-
-    def reduce_second(self, part, first):
-        above, below = first
-        cut = above.shape[0]
-        top = part(self.count - 2).astype(FULL)
-        low = part(self.count - 3).astype(FULL)
-        top = jnp.concatenate([top[:cut] + above.astype(FULL), top[cut:]], axis=0)
-        low = jnp.concatenate([low[:cut], low[cut:] + below.astype(FULL)], axis=0)
-        return top.astype(HALF), low.astype(HALF)
-
-    def reduce(self, part, second=None):
-        if second is None:
-            second = self.reduce_second(part, self.reduce_far(part(self.count - 1)))
-        top, low = second
-        arrived, sent = [], []
-        for step in range(self.half - 1, 0, -1):
-            if step < self.half - 1:
-                top = (part(2 * step).astype(FULL) + above.astype(FULL)).astype(HALF)
-                low = (part(2 * step - 1).astype(FULL) + below.astype(FULL)).astype(HALF)
-            above = lax.ppermute(top, "dp", self.up)
-            below = lax.ppermute(low, "dp", self.down)
-            sent.append((top, low))
-            arrived.append((above, below))
-        return part(0).astype(FULL) + above.astype(FULL) + below.astype(FULL), arrived, sent
+        return Travel(self, shard)
 
     def gather_rows(self, rows):
         first = lax.ppermute(rows, "tensor", beside(2))
@@ -533,11 +598,11 @@
         def piece(index):
             return lax.dynamic_slice_in_dim(values, (mine ^ index) * count, count, 0)
 
-        across = lax.ppermute(piece(3), "tensor", beside(1)).astype(FULL)
-        near = lax.ppermute(piece(1), "tensor", beside(1)).astype(FULL)
-        send = (piece(2).astype(FULL) + across).astype(HALF)
+        given = jnp.concatenate([piece(3), piece(1)], axis=0)
+        given = lax.ppermute(given, "tensor", beside(1)).astype(FULL)
+        send = (piece(2).astype(FULL) + given[:count]).astype(HALF)
         far = lax.ppermute(send, "tensor", beside(2)).astype(FULL)
-        return piece(0).astype(FULL) + near + far
+        return piece(0).astype(FULL) + given[count:] + far
 
     def lengths(self, counts):
         return counts[0]
@@ -581,10 +646,13 @@
     )
     gains = jnp.pad(gains, ((0, 30), (0, first_shard.shape[1] - block)))
     first_shard = jnp.concatenate([first_shard, gains], axis=0)
-    first_pieces, first_marks = ring.gather(first_shard)
-    down_pieces, down_marks = ring.gather(tie(down_weight.astype(HALF), first_marks[-2]))
+    whole_way = ring.half
+    first_travel = ring.gather(first_shard).steps(whole_way)
+    first_pieces, first_marks = first_travel.pieces, first_travel.marks
+    down_travel = ring.gather(tie(down_weight.astype(HALF), first_marks[-2])).steps(whole_way)
+    down_pieces, down_marks = down_travel.pieces, down_travel.marks
     feed_shard = jnp.concatenate([gate_weight, up_weight], axis=1).astype(HALF)
-    feed_pieces, feed_marks = ring.gather(tie(feed_shard, down_marks[-2]))
+    feed_pieces = ring.gather(tie(feed_shard, down_marks[-2])).steps(whole_way).pieces
     tokens, cotangent = ring.shuffle(tie(tokens, first_shard), cotangent)
     view = functools.partial(output_view, block, joint)
 
@@ -597,14 +665,17 @@
     resid = tokens.astype(FULL)
     scale_one = rms_scale(resid)
     rows_in = ring.gather_rows(tokens)
-    rows_one, joined, gains = first(rows_in, first_pieces, slots, block, joint)
+    grad_rows = ring.gather_rows(cotangent)
+    rows_one, joined, gains = first(
+        tie(rows_in, down_marks[0]), first_pieces, slots, block, joint
+    )
     gain_one, gain_two = gains[0], gains[1]
     queries, keys_values, attended, logsum = attend(
-        tie(joined, down_marks[0]), cosine, sine, begin, valid.reshape(1, total)
+        tie(joined, down_marks[1]), cosine, sine, begin, valid.reshape(1, total)
     )
     middle = resid + ring.scatter_rows(
         outward(
-            tie(attended, down_marks[1]),
+            tie(attended, down_marks[2]),
             first_pieces,
             slots,
             first_shard.shape[0],
@@ -618,71 +689,64 @@
     scale_two = rms_scale(middle)
     rows_two = ring.gather_rows((middle * scale_two * gain_two).astype(HALF))
     grad_out = cotangent.astype(FULL)
-    grad_rows = ring.gather_rows(cotangent)
     grad_hidden = hidden_back(grad_rows, down_pieces, slots)
     hidden, grad_feed = gate_up(rows_two, grad_hidden, feed_pieces)
 
-    mid, far = (slots - 3) * block, (slots - 1) * block
-    feed_far = contract_rows(rows_two[:, far:], grad_feed).astype(HALF)
-    down_far = contract_rows(hidden, grad_rows[:, far:]).astype(HALF)
-    feed_first = ring.reduce_far(feed_far)
-    down_first = ring.reduce_far(down_far)
-    partial_two = outward(
-        tie(grad_feed, feed_far, down_far), feed_pieces, slots, block, block, True, 16.2, "feed_back"
-    )
-    rows_mid, hidden_mid = tie((rows_two, hidden), partial_two, feed_first, down_first)
-    feed_mid = contract_rows(rows_mid[:, mid:far], grad_feed).astype(HALF)
-    down_mid = contract_rows(hidden_mid, grad_rows[:, mid:far]).astype(HALF)
-    feed_near = down_near = None
+    *feed_far, feed_mid = feed_grads(rows_two, grad_feed, grad_rows, hidden, slots, block, True)
+    feed_near = None
 
     def feed_part(slot):
         if slot >= slots - 3:
             return feed_mid[(slot - slots + 3) * block :][:block]
         return feed_near[slot * block : (slot + 1) * block]
 
-    def down_part(slot):
-        if slot >= slots - 3:
-            return down_mid[:, (slot - slots + 3) * block :][:, :block]
-        return down_near[:, slot * block : (slot + 1) * block]
-
-    feed_second = ring.reduce_second(feed_part, feed_first)
-    down_second = ring.reduce_second(down_part, down_first)
-    rows_near, hidden_near = tie((rows_two, hidden), feed_second, down_second)
-    feed_near = contract_rows(rows_near[:, :mid], grad_feed).astype(HALF)
-    down_near = contract_rows(hidden_near, grad_rows[:, :mid]).astype(HALF)
-    feed_sum, feed_steps, feed_sent = ring.reduce(feed_part, feed_second)
-    down_sum, down_steps, down_sent = ring.reduce(down_part, down_second)
+    feed_sums = Homeward(ring, feed_part, feed_far)
+    partial_two = outward(
+        tie(grad_feed, feed_mid), feed_pieces, slots, block, block, True, 0.0, "feed_back"
+    )
+    feed_sums.step(partial_two)
     grad_normed_two = ring.scatter_rows(partial_two)
-    grad_gain_two = jnp.sum(grad_normed_two * middle * scale_two, axis=0)
     inner_two = grad_normed_two * gain_two
     grad_middle = (
         grad_out
         + scale_two * inner_two
         - middle * scale_two**3 * jnp.mean(inner_two * middle, axis=1, keepdims=True)
     )
-    middle_rows = ring.gather_rows(grad_middle.astype(HALF))
-    grad_attended = mixed_back(tie(middle_rows, feed_sent[1], down_sent[1]), first_pieces, valid[:, None], slots, inner, view)
+    middle_given = grad_middle.astype(HALF)
+    middle_rows = ring.gather_rows(middle_given)
+    (feed_near,) = feed_grads(
+        tie(rows_two, feed_sums.sent, middle_given), grad_feed, grad_rows, hidden, slots, block, False
+    )
+    partial_out = outward(
+        tie(hidden, feed_near), down_pieces, slots, units, block, False, 0.0, "down"
+    )
+    feed_sums.step(partial_out).steps(ring.half - 4)
+    grad_attended = mixed_back(
+        tie(middle_rows, feed_sums.sent), first_pieces, valid[:, None], slots, inner, view
+    )
     grad_joined = attend_back(queries, keys_values, grad_attended, logsum, cosine, sine, begin)
-    late_joined = tie(grad_joined, feed_sent[2], down_sent[2])
-    first_sum, _, _ = ring.reduce(
-        lambda slot: contract_rows(rows_one[:, slot * block : (slot + 1) * block], late_joined)
-    )
-    partial_one, grad_gain_one = first_back(late_joined, rows_in, first_pieces, slots, block)
-    both = jnp.concatenate([grad_gain_one, grad_gain_two[None]], axis=0)
-
-    def output_part(slot):
-        there = slice(slot * block, (slot + 1) * block)
-        extra = jnp.pad(both[:, there], ((0, 30), (0, 0)))
-        return jnp.concatenate([contract_rows(attended, middle_rows[:, there]), extra], axis=0)
-
-    output_sum, _, _ = ring.reduce(output_part)
-    gain_sum = lax.psum(output_sum[inner : inner + 2], "tensor")
-    output_sum = output_sum[:inner]
+    last_grad = jnp.concatenate(
+        [
+            contract_rows(rows_one, grad_joined).astype(HALF),
+            contract_rows(middle_rows, attended).astype(HALF),
+        ],
+        axis=1,
+    )
+    partial_one = first_back(tie(grad_joined, last_grad), first_pieces, slots, block)
+
+    def last_part(slot):
+        return last_grad[slot * block : (slot + 1) * block]
+
+    last_sums = Homeward(ring, last_part, jnp.split(last_part(slots - 1), 2))
+    last_sums.step(partial_one)
+    feed_sums.step(last_sums.sent)
+    last_sums.step(feed_sums.sent).steps(ring.half - 4).step(feed_sums.arrived)
+    feed_sum, last_sum = feed_sums.own(), last_sums.own()
+    first_sum = last_sum[:, :joint]
+    output_sum = last_sum[:, joint:].T
     layer_out = (
         middle
-        + ring.scatter_rows(
-            outward(tie(hidden, grad_joined), down_pieces, slots, units, block, False, 9.2, "down")
-        )
+        + ring.scatter_rows(partial_out)
     ).astype(HALF)
     grad_normed_one = ring.scatter_rows(partial_one)
     inner_one = grad_normed_one * gain_one
@@ -692,6 +756,14 @@
         - resid * scale_one**3 * jnp.mean(inner_one * resid, axis=1, keepdims=True)
     )
     layer_out, input_grad = ring.shuffle(layer_out, input_grad, inverse=True)
+    gain_sums = [
+        jnp.sum(grads * shard.astype(FULL), axis=1) / gain.astype(HALF).astype(FULL)
+        for grads, shard, gain in (
+            (first_sum, first_shard[:block, :joint], attention_gain),
+            (feed_sum[:, : 2 * units], feed_shard, feed_gain),
+        )
+    ]
+    gain_sums = lax.psum(jnp.stack(gain_sums), "tensor")
     return (
         layer_out,
         input_grad,
@@ -700,10 +772,10 @@
         first_sum[:, inner + kv_width :],
         output_sum,
         feed_sum[:, :units],
-        feed_sum[:, units:],
-        down_sum,
-        gain_sum[0],
-        gain_sum[1],
+        feed_sum[:, units : 2 * units],
+        feed_sum[:, 2 * units :].T,
+        gain_sums[0],
+        gain_sums[1],
     )
 
 

time: 547 us -> 524 us (0.958)
  matrix products: 39.3 us -> 6.15 us
  Pallas kernels: 132 us -> 157 us
  starting transfers between devices: 74.3 us -> 54.4 us
  other arithmetic: 39.1 us -> 57.4 us
  waiting for transfers between devices: 222 us -> 206 us
    ppermute x64 -> x44, waiting for transfers between devices: 202 us -> 141 us  [the longest x12 91.9 us: step(): self.above = lax.ppermute(self.above, 'dp', ring.up)]
    ppermute x4, waiting for transfers between devices: 14.5 us -> 51.9 us  [scatter_rows(): far = lax.ppermute(send, 'tensor', beside(2)).astype(FULL)]
    dot_general x22 -> x2, matrix products: 39.3 us -> 6.15 us  [contract_rows(): lax.dot_general(left, right, (((0,), (0,)), ((), ())), preferred_element_...]
    pallas_call x0 -> x2, Pallas kernels: none -> 25.5 us  [feed_grads(): pl.pallas_call(functools.partial(feed_grads_kernel, early), grid=(3 if ea...]
    ppermute x64 -> x44, starting transfers between devices: 60.6 us -> 42.8 us  [the longest x12 22.5 us: step(): self.above = lax.ppermute(self.above, 'dp', ring.up)]
    convert_element_type x14 -> x16, other arithmetic: 16.2 us -> 27.4 us  [the longest x6 17.3 us: total(): joined = (own[first:last].astype(FULL) + arrived.astype(FULL)).astype(HALF)]
    ppermute x4, waiting for transfers between devices: 6.3 us -> 13.1 us  [gather_rows(): first = lax.ppermute(rows, 'tensor', beside(2))]
    unnamed x116 -> x110, local copies, waits for them, and re-layouts: 5.63 us -> 12.1 us
  transfers between devices with their start and end apart: 80 -> 60, of which waited for: 37 -> 33; matrix products, arithmetic and copies ran while one was open for 16% -> 14% of each run, Pallas kernels for 21% -> 24%
where the time goes in v3:
time: 524 us; the launch traced here: 515 us
  waiting for transfers between devices  206 us (39%)
  Pallas kernels  157 us (30%)
  other arithmetic  57.4 us (11%)
  starting transfers between devices  54.4 us (10%)
  local copies, waits for them, and re-layouts  26.3 us (5%)
  matrix products  6.15 us (1%)
  blocking collectives  5.89 us (1%)
    ppermute x12, waiting for transfers between devices, step(): self.above = lax.ppermute(self.above, 'dp', ring.up)  91.9 us
    ppermute x4, waiting for transfers between devices, scatter_rows(): far = lax.ppermute(send, 'tensor', beside(2)).astype(FULL)  51.9 us
    pallas_call x3, Pallas kernels, outward(): pl.pallas_call(functools.partial(outward_kernel, slots, depth, view, tran...  31.2 us
    ppermute x8, waiting for transfers between devices, send(): self.above = lax.ppermute(top, 'dp', self.ring.up)  30.6 us
    pallas_call x2, Pallas kernels, feed_grads(): pl.pallas_call(functools.partial(feed_grads_kernel, early), grid=(3 if ea...  25.5 us
    ppermute x12, starting transfers between devices, step(): self.above = lax.ppermute(self.above, 'dp', ring.up)  22.5 us
    convert_element_type x6, other arithmetic, total(): joined = (own[first:last].astype(FULL) + arrived.astype(FULL)).astype(HALF)  17.3 us
    pallas_call x1, Pallas kernels, gate_up(): pl.pallas_call(functools.partial(gate_up_kernel, units), grid=(total // T...  16.9 us
  transfers between devices with their start and end apart: 60, of which 33 were waited for; matrix products, arithmetic and copies ran while one was open for 14% of the time, Pallas kernels for 24%

profile of v3, /device:TPU:0, one launch (start us, length us, event | category | flops | bytes accessed | tf_op | source)
XLA Modules:
  0.0 514.6 jit_solution(1360498853058072165)
XLA Ops:
  5.7 14.8 %collective-permute-done.3.refs_1_ = bf16[288,1152]{1,0:T(8,128)(2,1)S(1)} collective-permute-done((bf16[288,1152]{1,0:T(8,128)(2,1)S(1)}, bf16[288,1152]{1,0:T(8,128)(2,1)S(1)}, u32[]{:S(2)}, u32[]{:S(2)}) %collective-permute-start.3) | collective-permute-done | bytes 663584 | tf_op jit(solution)/shard_map/ppermute | solution.py:484
  28.2 8.5 %collective-permute-done.4.refs_3_ = bf16[288,1152]{1,0:T(8,128)(2,1)S(1)} collective-permute-done((bf16[288,1152]{1,0:T(8,128)(2,1)S(1)}, bf16[288,1152]{1,0:T(8,128)(2,1)S(1)}, u32[]{:S(2)}, u32[]{:S(2)}) %collective-permute-start.4) | collective-permute-done | bytes 663584 | tf_op jit(solution)/shard_map/ppermute | solution.py:484
  44.0 7.9 %collective-permute-done.5.refs_5_ = bf16[288,1152]{1,0:T(8,128)(2,1)S(1)} collective-permute-done((bf16[288,1152]{1,0:T(8,128)(2,1)S(1)}, bf16[288,1152]{1,0:T(8,128)(2,1)S(1)}, u32[]{:S(2)}, u32[]{:S(2)}) %collective-permute-start.5) | collective-permute-done | bytes 663584 | tf_op jit(solution)/shard_map/ppermute | solution.py:484
  80.9 7.6 %first.1 = (bf16[768,2048]{1,0:T(8,128)(2,1)}, f32[768,640]{1,0:T(8,128)}, f32[2,2048]{1,0:T(2,128)}) custom-call(bf16[768,2048]{1,0:T(8,128)(2,1)} %join.4.x_ref, bf16[288,1152]{1,0:T(8,128)(2,1)} %copy-done.11, bf16[288,1152]{1,0:T(8,128)(2,1)} %copy-done.20, bf16[288,1152]{1,0:T(8,128)(2,1)} %copy-done.21, bf16[288,1152]{1,0:T(8,128)(2,1)} %copy-done.22, ...), custom_call_target="tpu_custom_call" | custom-call | flops 7699999744 | tf_op jit(solution)/shard_map/first/pallas_call | solution.py:387
  94.2 15.0 %attend.1 = (bf16[768,512]{1,0:T(8,128)(2,1)}, bf16[768,128]{1,0:T(8,128)(2,1)}, bf16[768,512]{1,0:T(8,128)(2,1)}, f32[8,1,768]{2,1,0:T(1,128)}) custom-call(f32[768,640]{1,0:T(8,128)} %get-tuple-element.55.joined_ref, f32[768,128]{1,0:T(8,128)} %copy.57.cos_ref, f32[768,128]{1,0:T(8,128)} %pad_maximum_fusion.11.sin_ref, ...), custom_call_target="tpu_custom_call" | custom-call | flops 14300000256 | tf_op jit(solution)/shard_map/attend/pallas_call | solution.py:127
  109.3 6.6 %output.1 = bf16[768,2048]{1,0:T(8,128)(2,1)} custom-call(bf16[768,512]{1,0:T(8,128)(2,1)} %get-tuple-element.57.x_ref, bf16[288,1152]{1,0:T(8,128)(2,1)} %copy-done.11, bf16[288,1152]{1,0:T(8,128)(2,1)} %copy-done.20, bf16[288,1152]{1,0:T(8,128)(2,1)} %copy-done.21, bf16[288,1152]{1,0:T(8,128)(2,1)} %copy-done.22, ...), custom_call_target="tpu_custom_call" | custom-call | flops 5720000000 | tf_op jit(solution)/shard_map/output/pallas_call | solution.py:350
  122.4 30.5 %collective-permute-done.27.refs_1_ = bf16[256,2816]{1,0:T(8,128)(2,1)} collective-permute-done((bf16[256,2816]{1,0:T(8,128)(2,1)S(1)}, bf16[256,2816]{1,0:T(8,128)(2,1)}, u32[]{:S(2)}, u32[]{:S(2)}) %collective-permute-start.27) | collective-permute-done | bytes 1441824 | tf_op jit(solution)/shard_map/ppermute | solution.py:484
  161.0 17.1 %collective-permute-done.18 = bf16[192,2048]{1,0:T(8,128)(2,1)} collective-permute-done((bf16[192,2048]{1,0:T(8,128)(2,1)}, bf16[192,2048]{1,0:T(8,128)(2,1)}, u32[]{:S(2)}, u32[]{:S(2)}) %collective-permute-start.18) | collective-permute-done | bytes 786464 | tf_op jit(solution)/shard_map/ppermute | solution.py:604
  198.0 9.3 %collective-permute-done.20.refs_2_ = bf16[192,2048]{1,0:T(8,128)(2,1)} collective-permute-done((bf16[192,2048]{1,0:T(8,128)(2,1)S(1)}, bf16[192,2048]{1,0:T(8,128)(2,1)}, u32[]{:S(2)}, u32[]{:S(2)}) %collective-permute-start.20) | collective-permute-done | bytes 786464 | tf_op jit(solution)/shard_map/ppermute | solution.py:583
  207.3 13.9 %collective-permute-done.31.refs_5_ = bf16[256,2816]{1,0:T(8,128)(2,1)S(1)} collective-permute-done((bf16[256,2816]{1,0:T(8,128)(2,1)}, bf16[256,2816]{1,0:T(8,128)(2,1)S(1)}, u32[]{:S(2)}, u32[]{:S(2)}) %collective-permute-start.31) | collective-permute-done | bytes 1441824 | tf_op jit(solution)/shard_map/ppermute | solution.py:484
  230.5 9.6 %hidden_back.1.grad_ref = f32[768,1408]{1,0:T(8,128)} custom-call(bf16[768,2048]{1,0:T(8,128)(2,1)} %join.6.x_ref.grad_ref, bf16[1408,256]{1,0:T(8,128)(2,1)} %copy-done.19, bf16[1408,256]{1,0:T(8,128)(2,1)} %collective-permute-done.9.refs_1_, bf16[1408,256]{1,0:T(8,128)(2,1)} %collective-permute-done.10.refs_2_, bf16[1408,256]{1,0:T(8,128)(2,1)} %copy-done.35, ...), custom_call_target="tpu_custom_call" | custom-call | flops 11879999488 | tf_op jit(solution)/shard_map/hidden_back/pallas_call | solution.py:272
  245.7 16.9 %gate_up.1 = (bf16[768,1408]{1,0:T(8,128)(2,1)}, bf16[768,2816]{1,0:T(8,128)(2,1)}) custom-call(bf16[768,2048]{1,0:T(8,128)(2,1)} %join.5.x_ref, f32[768,1408]{1,0:T(8,128)} %hidden_back.1.grad_ref, bf16[256,2816]{1,0:T(8,128)(2,1)} %copy-done.12, bf16[256,2816]{1,0:T(8,128)(2,1)} %collective-permute-done.27.refs_1_, ...), custom_call_target="tpu_custom_call" | custom-call | flops 18150000640 | tf_op jit(solution)/shard_map/gate_up/pallas_call | solution.py:244
  262.6 11.2 %feed_grads.2 = (bf16[128,4224]{1,0:T(8,128)(2,1)}, bf16[128,4224]{1,0:T(8,128)(2,1)}, bf16[512,4224]{1,0:T(8,128)(2,1)}) custom-call(bf16[768,2048]{1,0:T(8,128)(2,1)} %join.5.x_ref, bf16[768,2816]{1,0:T(8,128)(2,1)} %get-tuple-element.66.feed_ref.x_ref, bf16[768,2048]{1,0:T(8,128)(2,1)} %join.6.x_ref.grad_ref, ...), custom_call_target="tpu_custom_call" | custom-call | tf_op jit(solution)/shard_map/feed_grads/pallas_call | solution.py:327
  275.9 15.3 %feed_back.1 = bf16[768,2048]{1,0:T(8,128)(2,1)} custom-call(bf16[768,2816]{1,0:T(8,128)(2,1)} %get-tuple-element.66.feed_ref.x_ref, bf16[256,2816]{1,0:T(8,128)(2,1)} %copy-done.12, bf16[256,2816]{1,0:T(8,128)(2,1)} %collective-permute-done.27.refs_1_, bf16[256,2816]{1,0:T(8,128)(2,1)} %collective-permute-done.28.refs_2_, ...), custom_call_target="tpu_custom_call" | custom-call | tf_op jit(solution)/shard_map/feed_back/pallas_call | solution.py:350
  305.8 10.9 %collective-permute-done.38 = bf16[192,2048]{1,0:T(8,128)(2,1)S(1)} collective-permute-done((bf16[192,2048]{1,0:T(8,128)(2,1)S(1)}, bf16[192,2048]{1,0:T(8,128)(2,1)S(1)}, u32[]{:S(2)}, u32[]{:S(2)}) %collective-permute-start.38) | collective-permute-done | bytes 786464 | tf_op jit(solution)/shard_map/ppermute | solution.py:604
  323.2 14.3 %feed_grads.3 = bf16[1280,4224]{1,0:T(8,128)(2,1)} custom-call(bf16[768,2048]{1,0:T(8,128)(2,1)} %join.5.x_ref, bf16[768,2816]{1,0:T(8,128)(2,1)} %get-tuple-element.66.feed_ref.x_ref, bf16[768,2048]{1,0:T(8,128)(2,1)} %join.6.x_ref.grad_ref, bf16[768,1408]{1,0:T(8,128)(2,1)} %get-tuple-element.70.hidden_ref.x_ref), custom_call_target="tpu_custom_call" | custom-call | tf_op jit(solution)/shard_map/feed_grads/pallas_call | solution.py:327
  337.6 9.3 %down.1 = bf16[768,2048]{1,0:T(8,128)(2,1)} custom-call(bf16[768,1408]{1,0:T(8,128)(2,1)} %get-tuple-element.70.hidden_ref.x_ref, bf16[1408,256]{1,0:T(8,128)(2,1)} %copy-done.19, bf16[1408,256]{1,0:T(8,128)(2,1)} %collective-permute-done.9.refs_1_, bf16[1408,256]{1,0:T(8,128)(2,1)} %collective-permute-done.10.refs_2_, bf16[1408,256]{1,0:T(8,128)(2,1)} %copy-done.35, ...), custom_call_target="tpu_custom_call" | custom-call | tf_op jit(solution)/shard_map/down/pallas_call | solution.py:350
  360.5 6.4 %mixed_back.1.do_ref = bf16[768,512]{1,0:T(8,128)(2,1)} custom-call(bf16[768,2048]{1,0:T(8,128)(2,1)} %join.7.x_ref, bf16[288,1152]{1,0:T(8,128)(2,1)} %copy-done.11, bf16[288,1152]{1,0:T(8,128)(2,1)} %copy-done.20, bf16[288,1152]{1,0:T(8,128)(2,1)} %copy-done.21, bf16[288,1152]{1,0:T(8,128)(2,1)} %copy-done.22, ...), custom_call_target="tpu_custom_call" | custom-call | tf_op jit(solution)/shard_map/mixed_back/pallas_call | solution.py:437
  366.9 16.5 %attend_back.1.grad_ref = bf16[768,640]{1,0:T(8,128)(2,1)} custom-call(bf16[768,512]{1,0:T(8,128)(2,1)} %get-tuple-element.71.q_ref, bf16[768,128]{1,0:T(8,128)(2,1)} %get-tuple-element.72.kv_ref, bf16[768,512]{1,0:T(8,128)(2,1)} %mixed_back.1.do_ref, f32[8,1,768]{2,1,0:T(1,128)} %get-tuple-element.76.lse_ref, f32[768,128]{1,0:T(8,128)} %copy.57.cos_ref, ...), custom_call_target="tpu_custom_call" | custom-call | tf_op jit(solution)/shard_map/attend_back/pallas_call | solution.py:193
  392.6 6.9 %first_back.1 = bf16[768,2048]{1,0:T(8,128)(2,1)} custom-call(bf16[768,640]{1,0:T(8,128)(2,1)} %attend_back.1.grad_ref, bf16[288,1152]{1,0:T(8,128)(2,1)} %copy-done.11, bf16[288,1152]{1,0:T(8,128)(2,1)} %copy-done.20, bf16[288,1152]{1,0:T(8,128)(2,1)} %copy-done.21, bf16[288,1152]{1,0:T(8,128)(2,1)} %copy-done.22, ...), custom_call_target="tpu_custom_call" | custom-call | tf_op jit(solution)/shard_map/first_back/pallas_call | solution.py:412
  413.2 6.6 %add_convert_fusion = (bf16[256,4224]{1,0:T(8,128)(2,1)}, bf16[256,4224]{1,0:T(8,128)(2,1)}) fusion(bf16[256,4224]{1,0:T(8,128)(2,1)} %collective-permute-done.53, bf16[1280,4224]{1,0:T(8,128)(2,1)} %feed_grads.3, bf16[256,4224]{1,0:T(8,128)(2,1)} %collective-permute-done.52), kind=kLoop, calls=%fused_computation.24 | loop fusion | flops 8650752 | bytes 12976128 | tf_op jit(solution)/shard_map/convert_element_type | solution.py:512
  434.0 12.1 %collective-permute-done.47 = bf16[192,2048]{1,0:T(8,128)(2,1)S(1)} collective-permute-done((bf16[192,2048]{1,0:T(8,128)(2,1)S(1)}, bf16[192,2048]{1,0:T(8,128)(2,1)S(1)}, u32[]{:S(2)}, u32[]{:S(2)}) %collective-permute-start.47) | collective-permute-done | bytes 786464 | tf_op jit(solution)/shard_map/ppermute | solution.py:604
  449.8 11.7 %collective-permute-done.40 = bf16[192,2048]{1,0:T(8,128)(2,1)S(1)} collective-permute-done((bf16[192,2048]{1,0:T(8,128)(2,1)S(1)}, bf16[192,2048]{1,0:T(8,128)(2,1)S(1)}, u32[]{:S(2)}, u32[]{:S(2)}) %collective-permute-start.40) | collective-permute-done | bytes 786464 | tf_op jit(solution)/shard_map/ppermute | solution.py:604
  466.3 18.3 %collective-permute-done.54 = bf16[256,1152]{1,0:T(8,128)(2,1)S(1)} collective-permute-done((bf16[256,1152]{1,0:T(8,128)(2,1)}, bf16[256,1152]{1,0:T(8,128)(2,1)S(1)}, u32[]{:S(2)}, u32[]{:S(2)}) %collective-permute-start.54) | collective-permute-done | bytes 589856 | tf_op jit(solution)/shard_map/ppermute | solution.py:504
  (313 shorter events, 215.5 us)
Async XLA Ops:
  27.3 33.4 %collective-permute-start = (bf16[192,2048]{1,0:T(8,128)(2,1)}, bf16[192,2048]{1,0:T(8,128)(2,1)}, u32[]{:S(2)}, u32[]{:S(2)}) collective-permute-start(bf16[192,2048]{1,0:T(8,128)(2,1)} %get-tuple-element.51.refs_0_), channel_id=1, source_target_pairs={{0,1},{1,0},{2,3},{3,2},{4,5},{5,4},{6,7},{7,6},{8,9},{9,8},{10,11... | collective-permute-start | bytes 2359304 | tf_op jit(solution)/shard_map/ppermute | solution.py:584
  118.7 36.3 %collective-permute-start.17 = (bf16[384,2048]{1,0:T(8,128)(2,1)}, bf16[384,2048]{1,0:T(8,128)(2,1)}, u32[]{:S(2)}, u32[]{:S(2)}) collective-permute-start(bf16[384,2048]{1,0:T(8,128)(2,1)} %pad_maximum_fusion.3), channel_id=1, source_target_pairs={{0,1},{1,0},{2,3},{3,2},{4,5},{5,4},{6,7},{7,6},{8,9},{9,8},{10,11... | collective-permute-start | bytes 4718600 | tf_op jit(solution)/shard_map/ppermute | solution.py:602
  118.8 34.1 %collective-permute-start.27 = (bf16[256,2816]{1,0:T(8,128)(2,1)S(1)}, bf16[256,2816]{1,0:T(8,128)(2,1)}, u32[]{:S(2)}, u32[]{:S(2)}) collective-permute-start(bf16[256,2816]{1,0:T(8,128)(2,1)S(1)} %pad_maximum_fusion.7.refs_0_), channel_id=1, source_target_pairs={{0,8},{8,16},{16,24},{24,28},{28,20},{20,12},{12,4},{4,0},{1,9},{9... | collective-permute-start | bytes 4325384 | tf_op jit(solution)/shard_map/ppermute | solution.py:484
  120.7 34.1 %collective-permute-start.28 = (bf16[256,2816]{1,0:T(8,128)(2,1)S(1)}, bf16[256,2816]{1,0:T(8,128)(2,1)}, u32[]{:S(2)}, u32[]{:S(2)}) collective-permute-start(bf16[256,2816]{1,0:T(8,128)(2,1)S(1)} %pad_maximum_fusion.7.refs_0_), channel_id=1, source_target_pairs={{8,0},{16,8},{24,16},{28,24},{20,28},{12,20},{4,12},{0,4},{9,1},{1... | collective-permute-start | bytes 4325384 | tf_op jit(solution)/shard_map/ppermute | solution.py:485
  120.9 39.6 %collective-permute-start.23 = (bf16[192,2048]{1,0:T(8,128)(2,1)}, bf16[192,2048]{1,0:T(8,128)(2,1)}, u32[]{:S(2)}, u32[]{:S(2)}) collective-permute-start(bf16[192,2048]{1,0:T(8,128)(2,1)} %get-tuple-element.59.refs_0_), channel_id=1, source_target_pairs={{0,2},{1,3},{2,0},{3,1},{4,6},{5,7},{6,4},{7,5},{8,10},{9,11},{10,... | collective-permute-start | bytes 2359304 | tf_op jit(solution)/shard_map/ppermute | solution.py:583
  152.9 33.5 %collective-permute-start.29 = (bf16[256,2816]{1,0:T(8,128)(2,1)}, bf16[256,2816]{1,0:T(8,128)(2,1)}, u32[]{:S(2)}, u32[]{:S(2)}) collective-permute-start(bf16[256,2816]{1,0:T(8,128)(2,1)} %collective-permute-done.27.refs_1_), channel_id=1, source_target_pairs={{0,8},{8,16},{16,24},{24,28},{28,20},{20,12},{12,4},{4,0},{1,9},{9... | collective-permute-start | bytes 4325384 | tf_op jit(solution)/shard_map/ppermute | solution.py:484
  154.8 33.5 %collective-permute-start.30 = (bf16[256,2816]{1,0:T(8,128)(2,1)}, bf16[256,2816]{1,0:T(8,128)(2,1)}, u32[]{:S(2)}, u32[]{:S(2)}) collective-permute-start(bf16[256,2816]{1,0:T(8,128)(2,1)} %collective-permute-done.28.refs_2_), channel_id=1, source_target_pairs={{8,0},{16,8},{24,16},{28,24},{20,28},{12,20},{4,12},{0,4},{9,1},{1... | collective-permute-start | bytes 4325384 | tf_op jit(solution)/shard_map/ppermute | solution.py:485
  160.5 31.8 %collective-permute-start.22 = (bf16[192,2048]{1,0:T(8,128)(2,1)}, bf16[192,2048]{1,0:T(8,128)(2,1)}, u32[]{:S(2)}, u32[]{:S(2)}) collective-permute-start(bf16[192,2048]{1,0:T(8,128)(2,1)} %get-tuple-element.59.refs_0_), channel_id=1, source_target_pairs={{0,1},{1,0},{2,3},{3,2},{4,5},{5,4},{6,7},{7,6},{8,9},{9,8},{10,11... | collective-permute-start | bytes 2359304 | tf_op jit(solution)/shard_map/ppermute | solution.py:584
  160.5 33.7 %collective-permute-start.24 = (bf16[192,2048]{1,0:T(8,128)(2,1)}, bf16[192,2048]{1,0:T(8,128)(2,1)}, u32[]{:S(2)}, u32[]{:S(2)}) collective-permute-start(bf16[192,2048]{1,0:T(8,128)(2,1)} %collective-permute-done.23.refs_2_), channel_id=1, source_target_pairs={{0,1},{1,0},{2,3},{3,2},{4,5},{5,4},{6,7},{7,6},{8,9},{9,8},{10,11... | collective-permute-start | bytes 2359304 | tf_op jit(solution)/shard_map/ppermute | solution.py:585
  186.5 34.7 %collective-permute-start.31 = (bf16[256,2816]{1,0:T(8,128)(2,1)}, bf16[256,2816]{1,0:T(8,128)(2,1)S(1)}, u32[]{:S(2)}, u32[]{:S(2)}) collective-permute-start(bf16[256,2816]{1,0:T(8,128)(2,1)} %collective-permute-done.29.refs_3_), channel_id=1, source_target_pairs={{0,8},{8,16},{16,24},{24,28},{28,20},{20,12},{12,4},{4,0},{1,9},{9... | collective-permute-start | bytes 4325384 | tf_op jit(solution)/shard_map/ppermute | solution.py:484
  188.4 35.2 %collective-permute-start.32 = (bf16[256,2816]{1,0:T(8,128)(2,1)}, bf16[256,2816]{1,0:T(8,128)(2,1)S(1)}, u32[]{:S(2)}, u32[]{:S(2)}) collective-permute-start(bf16[256,2816]{1,0:T(8,128)(2,1)} %collective-permute-done.30.refs_4_), channel_id=1, source_target_pairs={{8,0},{16,8},{24,16},{28,24},{20,28},{12,20},{4,12},{0,4},{9,1},{1... | collective-permute-start | bytes 4325384 | tf_op jit(solution)/shard_map/ppermute | solution.py:485
  192.3 36.8 %collective-permute-start.25 = (bf16[704,256]{1,0:T(8,128)(2,1)}, bf16[704,256]{1,0:T(8,128)(2,1)}, u32[]{:S(2)}, u32[]{:S(2)}) collective-permute-start(bf16[704,256]{1,0:T(8,128)(2,1)} %slice.221), channel_id=1, source_target_pairs={{0,8},{8,16},{16,24},{24,28},{28,20},{20,12},{12,4},{4,0},{1,9},{9... | collective-permute-start | bytes 1081352 | tf_op jit(solution)/shard_map/ppermute | solution.py:484
  194.2 36.4 %collective-permute-start.26 = (bf16[704,256]{1,0:T(8,128)(2,1)}, bf16[704,256]{1,0:T(8,128)(2,1)}, u32[]{:S(2)}, u32[]{:S(2)}) collective-permute-start(bf16[704,256]{1,0:T(8,128)(2,1)} %slice.222), channel_id=1, source_target_pairs={{8,0},{16,8},{24,16},{28,24},{20,28},{12,20},{4,12},{0,4},{9,1},{1... | collective-permute-start | bytes 1081352 | tf_op jit(solution)/shard_map/ppermute | solution.py:485
  207.3 32.8 %collective-permute-start.19 = (bf16[192,2048]{1,0:T(8,128)(2,1)S(1)}, bf16[192,2048]{1,0:T(8,128)(2,1)}, u32[]{:S(2)}, u32[]{:S(2)}) collective-permute-start(bf16[192,2048]{1,0:T(8,128)(2,1)S(1)} %multiply_convert_fusion.refs_0_), channel_id=1, source_target_pairs={{0,1},{1,0},{2,3},{3,2},{4,5},{5,4},{6,7},{7,6},{8,9},{9,8},{10,11... | collective-permute-start | bytes 2359304 | tf_op jit(solution)/shard_map/ppermute | solution.py:584
  298.7 48.6 %collective-permute-start.45 = (bf16[256,4224]{1,0:T(8,128)(2,1)S(1)}, bf16[256,4224]{1,0:T(8,128)(2,1)S(1)}, u32[]{:S(2)}, u32[]{:S(2)}) collective-permute-start(bf16[256,4224]{1,0:T(8,128)(2,1)S(1)} %pad_maximum_fusion.2), channel_id=1, source_target_pairs={{8,0},{16,8},{24,16},{28,24},{20,28},{12,20},{4,12},{0,4},{9,1},{1... | collective-permute-start | bytes 6488072 | tf_op jit(solution)/shard_map/ppermute | solution.py:505
  304.0 45.2 %collective-permute-start.44 = (bf16[256,4224]{1,0:T(8,128)(2,1)}, bf16[256,4224]{1,0:T(8,128)(2,1)S(1)}, u32[]{:S(2)}, u32[]{:S(2)}) collective-permute-start(bf16[256,4224]{1,0:T(8,128)(2,1)} %pad_maximum_fusion.1), channel_id=1, source_target_pairs={{0,8},{8,16},{16,24},{24,28},{28,20},{20,12},{12,4},{4,0},{1,9},{9... | collective-permute-start | bytes 6488072 | tf_op jit(solution)/shard_map/ppermute | solution.py:504
  320.3 26.6 %collective-permute-start.42 = (bf16[192,2048]{1,0:T(8,128)(2,1)}, bf16[192,2048]{1,0:T(8,128)(2,1)}, u32[]{:S(2)}, u32[]{:S(2)}) collective-permute-start(bf16[192,2048]{1,0:T(8,128)(2,1)} %get-tuple-element.135.refs_0_), channel_id=1, source_target_pairs={{0,2},{1,3},{2,0},{3,1},{4,6},{5,7},{6,4},{7,5},{8,10},{9,11},{10,... | collective-permute-start | bytes 2359304 | tf_op jit(solution)/shard_map/ppermute | solution.py:583
  323.2 33.5 %collective-permute-start.41 = (bf16[192,2048]{1,0:T(8,128)(2,1)}, bf16[192,2048]{1,0:T(8,128)(2,1)}, u32[]{:S(2)}, u32[]{:S(2)}) collective-permute-start(bf16[192,2048]{1,0:T(8,128)(2,1)} %get-tuple-element.135.refs_0_), channel_id=1, source_target_pairs={{0,1},{1,0},{2,3},{3,2},{4,5},{5,4},{6,7},{7,6},{8,9},{9,8},{10,11... | collective-permute-start | bytes 2359304 | tf_op jit(solution)/shard_map/ppermute | solution.py:584
  354.6 57.0 %collective-permute-start.52 = (bf16[256,4224]{1,0:T(8,128)(2,1)}, bf16[256,4224]{1,0:T(8,128)(2,1)}, u32[]{:S(2)}, u32[]{:S(2)}) collective-permute-start(bf16[256,4224]{1,0:T(8,128)(2,1)} %get-tuple-element.142), channel_id=1, source_target_pairs={{0,8},{8,16},{16,24},{24,28},{28,20},{20,12},{12,4},{4,0},{1,9},{9... | collective-permute-start | bytes 6488072 | tf_op jit(solution)/shard_map/ppermute | solution.py:504
  356.2 57.0 %collective-permute-start.53 = (bf16[256,4224]{1,0:T(8,128)(2,1)}, bf16[256,4224]{1,0:T(8,128)(2,1)}, u32[]{:S(2)}, u32[]{:S(2)}) collective-permute-start(bf16[256,4224]{1,0:T(8,128)(2,1)} %get-tuple-element.141), channel_id=1, source_target_pairs={{8,0},{16,8},{24,16},{28,24},{20,28},{12,20},{4,12},{0,4},{9,1},{1... | collective-permute-start | bytes 6488072 | tf_op jit(solution)/shard_map/ppermute | solution.py:505
  419.8 65.7 %collective-permute-start.56 = (bf16[256,4224]{1,0:T(8,128)(2,1)}, bf16[256,4224]{1,0:T(8,128)(2,1)}, u32[]{:S(2)}, u32[]{:S(2)}) collective-permute-start(bf16[256,4224]{1,0:T(8,128)(2,1)} %get-tuple-element.140), channel_id=1, source_target_pairs={{0,8},{8,16},{16,24},{24,28},{28,20},{20,12},{12,4},{4,0},{1,9},{9... | collective-permute-start | bytes 6488072 | tf_op jit(solution)/shard_map/ppermute | solution.py:504
  425.2 60.4 %collective-permute-start.57 = (bf16[256,4224]{1,0:T(8,128)(2,1)}, bf16[256,4224]{1,0:T(8,128)(2,1)}, u32[]{:S(2)}, u32[]{:S(2)}) collective-permute-start(bf16[256,4224]{1,0:T(8,128)(2,1)} %get-tuple-element.139), channel_id=1, source_target_pairs={{8,0},{16,8},{24,16},{28,24},{20,28},{12,20},{4,12},{0,4},{9,1},{1... | collective-permute-start | bytes 6488072 | tf_op jit(solution)/shard_map/ppermute | solution.py:505
  430.3 54.3 %collective-permute-start.54 = (bf16[256,1152]{1,0:T(8,128)(2,1)}, bf16[256,1152]{1,0:T(8,128)(2,1)S(1)}, u32[]{:S(2)}, u32[]{:S(2)}) collective-permute-start(bf16[256,1152]{1,0:T(8,128)(2,1)} %get-tuple-element.146), channel_id=1, source_target_pairs={{0,8},{8,16},{16,24},{24,28},{28,20},{20,12},{12,4},{4,0},{1,9},{9... | collective-permute-start | bytes 1769480 | tf_op jit(solution)/shard_map/ppermute | solution.py:504
  431.9 53.6 %collective-permute-start.55 = (bf16[256,1152]{1,0:T(8,128)(2,1)}, bf16[256,1152]{1,0:T(8,128)(2,1)}, u32[]{:S(2)}, u32[]{:S(2)}) collective-permute-start(bf16[256,1152]{1,0:T(8,128)(2,1)} %get-tuple-element.145), channel_id=1, source_target_pairs={{8,0},{16,8},{24,16},{28,24},{20,28},{12,20},{4,12},{0,4},{9,1},{1... | collective-permute-start | bytes 1769480 | tf_op jit(solution)/shard_map/ppermute | solution.py:505
  (88 other events, 1221.2 us)

commit v4 on v3

--- a/solution.py
+++ b/solution.py
@@ -55,7 +55,7 @@
 
 
 TILE = 256
-VMEM = 56 * 2**20
+VMEM = 24 * 2**20
 
 def lasting(time):
     return pl.CostEstimate(flops=int(time * 1.1e9), bytes_accessed=0, transcendentals=0)
@@ -138,7 +138,7 @@
             pltpu.VMEM((64, total), HALF),
         ],
         compiler_params=pltpu.CompilerParams(vmem_limit_bytes=VMEM),
-        cost_estimate=lasting(13.0),
+        cost_estimate=lasting(0.0),
         name="attend",
     )(joined, cosine, sine, begin, valid)
 
@@ -215,7 +215,7 @@
 
 
 def whole(array):
-    return pl.BlockSpec(array.shape, lambda i: (0,) * array.ndim)
+    return pl.BlockSpec(memory_space=pltpu.VMEM)
 
 def rows_of(width, tile=TILE):
     return pl.BlockSpec((tile, width), lambda i: (i, 0))
@@ -395,7 +395,7 @@
             jax.ShapeDtypeStruct((2, wide), FULL),
         ),
         compiler_params=pltpu.CompilerParams(vmem_limit_bytes=VMEM),
-        cost_estimate=lasting(7.0),
+        cost_estimate=lasting(0.0),
         name="first",
     )(x, *pieces)
 
@@ -587,7 +587,7 @@
             join_kernel,
             out_shape=jax.ShapeDtypeStruct((4 * rows.shape[0], rows.shape[1]), rows.dtype),
             compiler_params=pltpu.CompilerParams(vmem_limit_bytes=VMEM),
-            cost_estimate=lasting(2.0),
+            cost_estimate=lasting(0.0),
             name="join",
         )(rows, near, first, far)
 
@@ -649,11 +649,14 @@
     whole_way = ring.half
     first_travel = ring.gather(first_shard).steps(whole_way)
     first_pieces, first_marks = first_travel.pieces, first_travel.marks
-    down_travel = ring.gather(tie(down_weight.astype(HALF), first_marks[-2])).steps(whole_way)
+    tokens, cotangent = ring.shuffle(tie(tokens, first_shard), cotangent)
+    rows_in = ring.gather_rows(tokens)
+    down_shard = tie(down_weight.astype(HALF), first_marks[-1], rows_in)
+    down_travel = ring.gather(down_shard).steps(whole_way)
     down_pieces, down_marks = down_travel.pieces, down_travel.marks
     feed_shard = jnp.concatenate([gate_weight, up_weight], axis=1).astype(HALF)
-    feed_pieces = ring.gather(tie(feed_shard, down_marks[-2])).steps(whole_way).pieces
-    tokens, cotangent = ring.shuffle(tie(tokens, first_shard), cotangent)
+    feed_travel = ring.gather(tie(feed_shard, first_marks[-1])).steps(whole_way)
+    feed_pieces, feed_marks = feed_travel.pieces, feed_travel.marks
     view = functools.partial(output_view, block, joint)
 
     total = own_rows * lax.axis_size("tensor")
@@ -664,28 +667,27 @@
     sine = jnp.concatenate([-sine, sine, -sine, sine], axis=1)
     resid = tokens.astype(FULL)
     scale_one = rms_scale(resid)
-    rows_in = ring.gather_rows(tokens)
     grad_rows = ring.gather_rows(cotangent)
     rows_one, joined, gains = first(
-        tie(rows_in, down_marks[0]), first_pieces, slots, block, joint
+        rows_in, first_pieces, slots, block, joint
     )
     gain_one, gain_two = gains[0], gains[1]
     queries, keys_values, attended, logsum = attend(
-        tie(joined, down_marks[1]), cosine, sine, begin, valid.reshape(1, total)
-    )
-    middle = resid + ring.scatter_rows(
-        outward(
-            tie(attended, down_marks[2]),
-            first_pieces,
-            slots,
-            first_shard.shape[0],
-            block,
-            False,
-            5.2,
-            "output",
-            view,
-        )
-    )
+        tie(joined, down_marks[0]), cosine, sine, begin, valid.reshape(1, total)
+    )
+    partial_mixed = outward(
+        tie(attended, grad_rows),
+        first_pieces,
+        slots,
+        first_shard.shape[0],
+        block,
+        False,
+        0.0,
+        "output",
+        view,
+    )
+    middle = resid + ring.scatter_rows(tie(partial_mixed, down_marks[1], feed_marks[0]))
+    middle = tie(middle, feed_marks[1])
     scale_two = rms_scale(middle)
     rows_two = ring.gather_rows((middle * scale_two * gain_two).astype(HALF))
     grad_out = cotangent.astype(FULL)

time: 524 us -> 502 us (0.958)
  Pallas kernels: 157 us -> 100 us
  waiting for transfers between devices: 206 us -> 239 us
  local copies, waits for them, and re-layouts: 26.3 us -> 34.5 us
  other arithmetic: 57.4 us -> 50.3 us
    ppermute x12, waiting for transfers between devices: 9.33 us -> 39.9 us  [step(): self.below = lax.ppermute(self.below, 'dp', ring.down)]
    ppermute x8, waiting for transfers between devices: 30.6 us -> 56.2 us  [send(): self.above = lax.ppermute(top, 'dp', self.ring.up)]
    ppermute x4, waiting for transfers between devices: 51.9 us -> 34.6 us  [scatter_rows(): far = lax.ppermute(send, 'tensor', beside(2)).astype(FULL)]
    unnamed x110 -> x172, local copies, waits for them, and re-layouts: 12.1 us -> 25.9 us
    pallas_call x4, Pallas kernels: 15 us -> 2.61 us  [gather_rows(): pl.pallas_call(join_kernel, out_shape=jax.ShapeDtypeStruct((4 * rows.shap...]
    ppermute x4, waiting for transfers between devices: 13.1 us -> 1.64 us  [gather_rows(): first = lax.ppermute(rows, 'tensor', beside(2))]
    ppermute x12, starting transfers between devices: 3.8 us -> 13.3 us  [step(): self.below = lax.ppermute(self.below, 'dp', ring.down)]
    ppermute x12, starting transfers between devices: 22.5 us -> 13.2 us  [step(): self.above = lax.ppermute(self.above, 'dp', ring.up)]
  transfers between devices with their start and end apart: 60 -> 60, of which waited for: 33 -> 30; matrix products, arithmetic and copies ran while one was open for 14% -> 12% of each run, Pallas kernels for 24% -> 16%
where the time goes in v4:
time: 502 us; the launch traced here: 493 us
  waiting for transfers between devices  239 us (48%)
  Pallas kernels  100 us (20%)
  starting transfers between devices  55.7 us (11%)
  other arithmetic  50.3 us (10%)
  local copies, waits for them, and re-layouts  34.5 us (7%)
  blocking collectives  5.99 us (1%)
    ppermute x12, waiting for transfers between devices, step(): self.above = lax.ppermute(self.above, 'dp', ring.up)  91.3 us
    ppermute x8, waiting for transfers between devices, send(): self.above = lax.ppermute(top, 'dp', self.ring.up)  56.2 us
    ppermute x12, waiting for transfers between devices, step(): self.below = lax.ppermute(self.below, 'dp', ring.down)  39.9 us
    ppermute x4, waiting for transfers between devices, scatter_rows(): far = lax.ppermute(send, 'tensor', beside(2)).astype(FULL)  34.6 us
    unnamed x172, local copies, waits for them, and re-layouts  25.9 us
    pallas_call x3, Pallas kernels, outward(): pl.pallas_call(functools.partial(outward_kernel, slots, depth, view, tran...  22.2 us
    pallas_call x2, Pallas kernels, feed_grads(): pl.pallas_call(functools.partial(feed_grads_kernel, early), grid=(3 if ea...  16.8 us
    convert_element_type x6, other arithmetic, total(): joined = (own[first:last].astype(FULL) + arrived.astype(FULL)).astype(HALF)  14.6 us
  transfers between devices with their start and end apart: 60, of which 30 were waited for; matrix products, arithmetic and copies ran while one was open for 12% of the time, Pallas kernels for 16%

profile of v4, /device:TPU:0, one launch (start us, length us, event | category | flops | bytes accessed | tf_op | source)
XLA Modules:
  0.0 493.3 jit_solution(8325433991713312151)
XLA Ops:
  6.7 14.0 %collective-permute-done.4.refs_2_ = bf16[288,1152]{1,0:T(8,128)(2,1)S(1)} collective-permute-done((bf16[288,1152]{1,0:T(8,128)(2,1)S(1)}, bf16[288,1152]{1,0:T(8,128)(2,1)S(1)}, u32[]{:S(2)}, u32[]{:S(2)}) %collective-permute-start.4) | collective-permute-done | bytes 663584 | tf_op jit(solution)/shard_map/ppermute | solution.py:485
  24.7 12.0 %collective-permute-done.6.refs_4_ = bf16[288,1152]{1,0:T(8,128)(2,1)S(1)} collective-permute-done((bf16[288,1152]{1,0:T(8,128)(2,1)S(1)}, bf16[288,1152]{1,0:T(8,128)(2,1)S(1)}, u32[]{:S(2)}, u32[]{:S(2)}) %collective-permute-start.6) | collective-permute-done | bytes 663584 | tf_op jit(solution)/shard_map/ppermute | solution.py:485
  42.8 9.1 %collective-permute-done.8.refs_6_ = bf16[288,1152]{1,0:T(8,128)(2,1)S(1)} collective-permute-done((bf16[288,1152]{1,0:T(8,128)(2,1)S(1)}, bf16[288,1152]{1,0:T(8,128)(2,1)S(1)}, u32[]{:S(2)}, u32[]{:S(2)}) %collective-permute-start.8) | collective-permute-done | bytes 663584 | tf_op jit(solution)/shard_map/ppermute | solution.py:485
  69.6 12.1 %collective-permute-done.11.refs_1_ = bf16[1408,256]{1,0:T(8,128)(2,1)} collective-permute-done((bf16[1408,256]{1,0:T(8,128)(2,1)S(1)}, bf16[1408,256]{1,0:T(8,128)(2,1)}, u32[]{:S(2)}, u32[]{:S(2)}) %collective-permute-start.11) | collective-permute-done | bytes 720928 | tf_op jit(solution)/shard_map/ppermute | solution.py:484
  104.2 12.4 %attend.1 = (bf16[768,512]{1,0:T(8,128)(2,1)S(1)}, bf16[768,128]{1,0:T(8,128)(2,1)S(1)}, bf16[768,512]{1,0:T(8,128)(2,1)S(1)}, f32[8,1,768]{2,1,0:T(1,128)S(1)}) custom-call(f32[768,640]{1,0:T(8,128)S(1)} %get-tuple-element.55.joined_ref, f32[768,128]{1,0:T(8,128)S(1)} %copy-done.29, f32[768,128]{1,0:T(8,128)S(1)} %pad_maximum_fusion.11.sin_ref, ...), custom_call_target="tpu_custom_call" | custom-call | tf_op jit(solution)/shard_map/attend/pallas_call | solution.py:127
  119.0 8.0 %collective-permute-done.16.refs_3_ = bf16[1408,256]{1,0:T(8,128)(2,1)} collective-permute-done((bf16[1408,256]{1,0:T(8,128)(2,1)}, bf16[1408,256]{1,0:T(8,128)(2,1)}, u32[]{:S(2)}, u32[]{:S(2)}) %collective-permute-start.16) | collective-permute-done | bytes 720928 | tf_op jit(solution)/shard_map/ppermute | solution.py:484
  141.3 22.7 %collective-permute-done.22.refs_3_ = bf16[256,2816]{1,0:T(8,128)(2,1)} collective-permute-done((bf16[256,2816]{1,0:T(8,128)(2,1)}, bf16[256,2816]{1,0:T(8,128)(2,1)}, u32[]{:S(2)}, u32[]{:S(2)}) %collective-permute-start.22) | collective-permute-done | bytes 1441824 | tf_op jit(solution)/shard_map/ppermute | solution.py:484
  171.1 8.3 %collective-permute-done.27.refs_5_ = bf16[1408,256]{1,0:T(8,128)(2,1)S(1)} collective-permute-done((bf16[1408,256]{1,0:T(8,128)(2,1)}, bf16[1408,256]{1,0:T(8,128)(2,1)S(1)}, u32[]{:S(2)}, u32[]{:S(2)}) %collective-permute-start.27) | collective-permute-done | bytes 720928 | tf_op jit(solution)/shard_map/ppermute | solution.py:484
  181.6 28.7 %collective-permute-done.31.refs_5_ = bf16[256,2816]{1,0:T(8,128)(2,1)S(1)} collective-permute-done((bf16[256,2816]{1,0:T(8,128)(2,1)}, bf16[256,2816]{1,0:T(8,128)(2,1)S(1)}, u32[]{:S(2)}, u32[]{:S(2)}) %collective-permute-start.31) | collective-permute-done | bytes 1441824 | tf_op jit(solution)/shard_map/ppermute | solution.py:484
  218.9 7.3 %hidden_back.1.grad_ref = f32[768,1408]{1,0:T(8,128)S(1)} custom-call(bf16[768,2048]{1,0:T(8,128)(2,1)S(1)} %join.5.x_ref.grad_ref, bf16[1408,256]{1,0:T(8,128)(2,1)S(1)} %copy-done.37, bf16[1408,256]{1,0:T(8,128)(2,1)} %collective-permute-done.11.refs_1_, bf16[1408,256]{1,0:T(8,128)(2,1)} %collective-permute-done.12.refs_2_, ...), custom_call_target="tpu_custom_call" | custom-call | flops 11879999488 | tf_op jit(solution)/shard_map/hidden_back/pallas_call | solution.py:272
  226.4 6.6 %collective-permute-done.33.refs_7_ = bf16[128,2816]{1,0:T(8,128)(2,1)S(1)} collective-permute-done((bf16[128,2816]{1,0:T(8,128)(2,1)S(1)}, bf16[128,2816]{1,0:T(8,128)(2,1)S(1)}, u32[]{:S(2)}, u32[]{:S(2)}) %collective-permute-start.33) | collective-permute-done | bytes 720928 | tf_op jit(solution)/shard_map/ppermute | solution.py:484
  235.4 13.9 %gate_up.1 = (bf16[768,1408]{1,0:T(8,128)(2,1)S(1)}, bf16[768,2816]{1,0:T(8,128)(2,1)S(1)}) custom-call(bf16[768,2048]{1,0:T(8,128)(2,1)S(1)} %join.6.x_ref, f32[768,1408]{1,0:T(8,128)S(1)} %hidden_back.1.grad_ref, bf16[256,2816]{1,0:T(8,128)(2,1)} %pad_maximum_fusion.7.refs_0_, bf16[256,2816]{1,0:T(8,128)(2,1)} %collective-permute-done.18.refs_1_, ...), custom_call_target="tpu_custom_call" | custom-call | flops 18150000640 | tf_op jit(solution)/shard_map/gate_up/pallas_call | solution.py:244
  249.3 6.3 %feed_grads.2 = (bf16[128,4224]{1,0:T(8,128)(2,1)S(1)}, bf16[128,4224]{1,0:T(8,128)(2,1)S(1)}, bf16[512,4224]{1,0:T(8,128)(2,1)S(1)}) custom-call(bf16[768,2048]{1,0:T(8,128)(2,1)S(1)} %join.6.x_ref, bf16[768,2816]{1,0:T(8,128)(2,1)S(1)} %get-tuple-element.68.feed_ref.x_ref, bf16[768,2048]{1,0:T(8,128)(2,1)S(1)} %join.5.x_ref.grad_ref, ...), custom_call_target="tpu_custom_call" | custom-call | tf_op jit(solution)/shard_map/feed_grads/pallas_call | solution.py:327
  257.9 12.7 %feed_back.1 = bf16[768,2048]{1,0:T(8,128)(2,1)S(1)} custom-call(bf16[768,2816]{1,0:T(8,128)(2,1)S(1)} %get-tuple-element.68.feed_ref.x_ref, bf16[256,2816]{1,0:T(8,128)(2,1)} %pad_maximum_fusion.7.refs_0_, bf16[256,2816]{1,0:T(8,128)(2,1)} %collective-permute-done.18.refs_1_, bf16[256,2816]{1,0:T(8,128)(2,1)} %collective-permute-done.19.refs_2_, ...), custom_call_target="tpu_custom_call" | custom-call | tf_op jit(solution)/shard_map/feed_back/pallas_call | solution.py:350
  271.1 8.7 %collective-permute-done.35 = bf16[128,4224]{1,0:T(8,128)(2,1)S(1)} collective-permute-done((bf16[128,4224]{1,0:T(8,128)(2,1)S(1)}, bf16[128,4224]{1,0:T(8,128)(2,1)S(1)}, u32[]{:S(2)}, u32[]{:S(2)}) %collective-permute-start.35) | collective-permute-done | bytes 1081376 | tf_op jit(solution)/shard_map/ppermute | solution.py:504
  287.8 11.7 %collective-permute-done.38 = bf16[192,2048]{1,0:T(8,128)(2,1)S(1)} collective-permute-done((bf16[192,2048]{1,0:T(8,128)(2,1)S(1)}, bf16[192,2048]{1,0:T(8,128)(2,1)S(1)}, u32[]{:S(2)}, u32[]{:S(2)}) %collective-permute-start.38) | collective-permute-done | bytes 786464 | tf_op jit(solution)/shard_map/ppermute | solution.py:604
  304.1 10.4 %feed_grads.3 = bf16[1280,4224]{1,0:T(8,128)(2,1)S(1)} custom-call(bf16[768,2048]{1,0:T(8,128)(2,1)S(1)} %join.6.x_ref, bf16[768,2816]{1,0:T(8,128)(2,1)S(1)} %get-tuple-element.68.feed_ref.x_ref, bf16[768,2048]{1,0:T(8,128)(2,1)S(1)} %join.5.x_ref.grad_ref, bf16[768,1408]{1,0:T(8,128)(2,1)S(1)} %get-tuple-element.72.hidden_ref.x_ref), custom_call_target="tpu_custom_call" | custom-call | tf_op jit(solution)/shard_map/feed_grads/pallas_call | solution.py:327
  314.6 7.2 %down.1 = bf16[768,2048]{1,0:T(8,128)(2,1)S(1)} custom-call(bf16[768,1408]{1,0:T(8,128)(2,1)S(1)} %get-tuple-element.72.hidden_ref.x_ref, bf16[1408,256]{1,0:T(8,128)(2,1)S(1)} %copy-done.37, bf16[1408,256]{1,0:T(8,128)(2,1)} %collective-permute-done.11.refs_1_, bf16[1408,256]{1,0:T(8,128)(2,1)} %collective-permute-done.12.refs_2_, ...), custom_call_target="tpu_custom_call" | custom-call | tf_op jit(solution)/shard_map/down/pallas_call | solution.py:350
  344.4 13.7 %attend_back.1.grad_ref = bf16[768,640]{1,0:T(8,128)(2,1)S(1)} custom-call(bf16[768,512]{1,0:T(8,128)(2,1)S(1)} %copy-done.43, bf16[768,128]{1,0:T(8,128)(2,1)S(1)} %copy-done.51, bf16[768,512]{1,0:T(8,128)(2,1)S(1)} %mixed_back.1.do_ref, f32[8,1,768]{2,1,0:T(1,128)S(1)} %get-tuple-element.78.lse_ref, f32[768,128]{1,0:T(8,128)S(1)} %copy-done.30, ...), custom_call_target="tpu_custom_call" | custom-call | tf_op jit(solution)/shard_map/attend_back/pallas_call | solution.py:193
  371.4 17.5 %collective-permute-done.48 = bf16[128,1152]{1,0:T(8,128)(2,1)S(1)} collective-permute-done((bf16[128,1152]{1,0:T(8,128)(2,1)S(1)}, bf16[128,1152]{1,0:T(8,128)(2,1)S(1)}, u32[]{:S(2)}, u32[]{:S(2)}) %collective-permute-start.48) | collective-permute-done | bytes 294944 | tf_op jit(solution)/shard_map/ppermute | solution.py:504
  415.8 11.8 %collective-permute-done.47 = bf16[192,2048]{1,0:T(8,128)(2,1)S(1)} collective-permute-done((bf16[192,2048]{1,0:T(8,128)(2,1)S(1)}, bf16[192,2048]{1,0:T(8,128)(2,1)S(1)}, u32[]{:S(2)}, u32[]{:S(2)}) %collective-permute-start.47) | collective-permute-done | bytes 786464 | tf_op jit(solution)/shard_map/ppermute | solution.py:604
  431.1 11.2 %collective-permute-done.40 = bf16[192,2048]{1,0:T(8,128)(2,1)S(1)} collective-permute-done((bf16[192,2048]{1,0:T(8,128)(2,1)S(1)}, bf16[192,2048]{1,0:T(8,128)(2,1)S(1)}, u32[]{:S(2)}, u32[]{:S(2)}) %collective-permute-start.40) | collective-permute-done | bytes 786464 | tf_op jit(solution)/shard_map/ppermute | solution.py:604
  444.5 20.6 %collective-permute-done.54 = bf16[256,1152]{1,0:T(8,128)(2,1)S(1)} collective-permute-done((bf16[256,1152]{1,0:T(8,128)(2,1)S(1)}, bf16[256,1152]{1,0:T(8,128)(2,1)S(1)}, u32[]{:S(2)}, u32[]{:S(2)}) %collective-permute-start.54) | collective-permute-done | bytes 589856 | tf_op jit(solution)/shard_map/ppermute | solution.py:504
  483.9 6.0 %psum.7 = f32[2,256]{1,0:T(2,128)S(1)} all-reduce(f32[2,256]{1,0:T(2,128)S(1)} %pad_maximum_fusion.12), channel_id=1, replica_groups=mesh['dp'=8,'tensor'=4] {'tensor'}, use_global_device_ids=true, to_apply=%region_9.10 | all-reduce | flops 512 | bytes 4096 | tf_op jit(solution)/shard_map/psum | solution.py:768
  (376 shorter events, 197.8 us)
Async XLA Ops:
  66.6 61.3 %collective-permute-start.18 = (bf16[256,2816]{1,0:T(8,128)(2,1)}, bf16[256,2816]{1,0:T(8,128)(2,1)}, u32[]{:S(2)}, u32[]{:S(2)}) collective-permute-start(bf16[256,2816]{1,0:T(8,128)(2,1)} %pad_maximum_fusion.7.refs_0_), channel_id=1, source_target_pairs={{0,8},{8,16},{16,24},{24,28},{28,20},{20,12},{12,4},{4,0},{1,9},{9... | collective-permute-start | bytes 4325384 | tf_op jit(solution)/shard_map/ppermute | solution.py:484
  67.6 60.3 %collective-permute-start.19 = (bf16[256,2816]{1,0:T(8,128)(2,1)}, bf16[256,2816]{1,0:T(8,128)(2,1)}, u32[]{:S(2)}, u32[]{:S(2)}) collective-permute-start(bf16[256,2816]{1,0:T(8,128)(2,1)} %pad_maximum_fusion.7.refs_0_), channel_id=1, source_target_pairs={{8,0},{16,8},{24,16},{28,24},{20,28},{12,20},{4,12},{0,4},{9,1},{1... | collective-permute-start | bytes 4325384 | tf_op jit(solution)/shard_map/ppermute | solution.py:485
  81.7 45.3 %collective-permute-start.16 = (bf16[1408,256]{1,0:T(8,128)(2,1)}, bf16[1408,256]{1,0:T(8,128)(2,1)}, u32[]{:S(2)}, u32[]{:S(2)}) collective-permute-start(bf16[1408,256]{1,0:T(8,128)(2,1)} %collective-permute-done.11.refs_1_), channel_id=1, source_target_pairs={{0,8},{8,16},{16,24},{24,28},{28,20},{20,12},{12,4},{4,0},{1,9},{9... | collective-permute-start | bytes 2162696 | tf_op jit(solution)/shard_map/ppermute | solution.py:484
  82.8 45.1 %collective-permute-start.17 = (bf16[1408,256]{1,0:T(8,128)(2,1)}, bf16[1408,256]{1,0:T(8,128)(2,1)}, u32[]{:S(2)}, u32[]{:S(2)}) collective-permute-start(bf16[1408,256]{1,0:T(8,128)(2,1)} %collective-permute-done.12.refs_2_), channel_id=1, source_target_pairs={{8,0},{16,8},{24,16},{28,24},{20,28},{12,20},{4,12},{0,4},{9,1},{1... | collective-permute-start | bytes 2162696 | tf_op jit(solution)/shard_map/ppermute | solution.py:485
  129.3 34.7 %collective-permute-start.22 = (bf16[256,2816]{1,0:T(8,128)(2,1)}, bf16[256,2816]{1,0:T(8,128)(2,1)}, u32[]{:S(2)}, u32[]{:S(2)}) collective-permute-start(bf16[256,2816]{1,0:T(8,128)(2,1)} %collective-permute-done.18.refs_1_), channel_id=1, source_target_pairs={{0,8},{8,16},{16,24},{24,28},{28,20},{20,12},{12,4},{4,0},{1,9},{9... | collective-permute-start | bytes 4325384 | tf_op jit(solution)/shard_map/ppermute | solution.py:484
  130.9 34.7 %collective-permute-start.23 = (bf16[256,2816]{1,0:T(8,128)(2,1)}, bf16[256,2816]{1,0:T(8,128)(2,1)}, u32[]{:S(2)}, u32[]{:S(2)}) collective-permute-start(bf16[256,2816]{1,0:T(8,128)(2,1)} %collective-permute-done.19.refs_2_), channel_id=1, source_target_pairs={{8,0},{16,8},{24,16},{28,24},{20,28},{12,20},{4,12},{0,4},{9,1},{1... | collective-permute-start | bytes 4325384 | tf_op jit(solution)/shard_map/ppermute | solution.py:485
  137.7 28.9 %collective-permute-start.21 = (bf16[192,2048]{1,0:T(8,128)(2,1)}, bf16[192,2048]{1,0:T(8,128)(2,1)}, u32[]{:S(2)}, u32[]{:S(2)}) collective-permute-start(bf16[192,2048]{1,0:T(8,128)(2,1)} %fusion.15), channel_id=1, source_target_pairs={{0,2},{1,3},{2,0},{3,1},{4,6},{5,7},{6,4},{7,5},{8,10},{9,11},{10,... | collective-permute-start | bytes 2359304 | tf_op jit(solution)/shard_map/ppermute | solution.py:604
  139.2 40.2 %collective-permute-start.27 = (bf16[1408,256]{1,0:T(8,128)(2,1)}, bf16[1408,256]{1,0:T(8,128)(2,1)S(1)}, u32[]{:S(2)}, u32[]{:S(2)}) collective-permute-start(bf16[1408,256]{1,0:T(8,128)(2,1)} %collective-permute-done.16.refs_3_), channel_id=1, source_target_pairs={{0,8},{8,16},{16,24},{24,28},{28,20},{20,12},{12,4},{4,0},{1,9},{9... | collective-permute-start | bytes 2162696 | tf_op jit(solution)/shard_map/ppermute | solution.py:484
  140.8 40.2 %collective-permute-start.28 = (bf16[1408,256]{1,0:T(8,128)(2,1)}, bf16[1408,256]{1,0:T(8,128)(2,1)S(1)}, u32[]{:S(2)}, u32[]{:S(2)}) collective-permute-start(bf16[1408,256]{1,0:T(8,128)(2,1)} %collective-permute-done.17.refs_4_), channel_id=1, source_target_pairs={{8,0},{16,8},{24,16},{28,24},{20,28},{12,20},{4,12},{0,4},{9,1},{1... | collective-permute-start | bytes 2162696 | tf_op jit(solution)/shard_map/ppermute | solution.py:485
  164.0 46.2 %collective-permute-start.31 = (bf16[256,2816]{1,0:T(8,128)(2,1)}, bf16[256,2816]{1,0:T(8,128)(2,1)S(1)}, u32[]{:S(2)}, u32[]{:S(2)}) collective-permute-start(bf16[256,2816]{1,0:T(8,128)(2,1)} %collective-permute-done.22.refs_3_), channel_id=1, source_target_pairs={{0,8},{8,16},{16,24},{24,28},{28,20},{20,12},{12,4},{4,0},{1,9},{9... | collective-permute-start | bytes 4325384 | tf_op jit(solution)/shard_map/ppermute | solution.py:484
  165.6 46.2 %collective-permute-start.32 = (bf16[256,2816]{1,0:T(8,128)(2,1)}, bf16[256,2816]{1,0:T(8,128)(2,1)S(1)}, u32[]{:S(2)}, u32[]{:S(2)}) collective-permute-start(bf16[256,2816]{1,0:T(8,128)(2,1)} %collective-permute-done.23.refs_4_), channel_id=1, source_target_pairs={{8,0},{16,8},{24,16},{28,24},{20,28},{12,20},{4,12},{0,4},{9,1},{1... | collective-permute-start | bytes 4325384 | tf_op jit(solution)/shard_map/ppermute | solution.py:485
  169.5 49.4 %collective-permute-start.25 = (bf16[192,2048]{1,0:T(8,128)(2,1)S(1)}, bf16[192,2048]{1,0:T(8,128)(2,1)S(1)}, u32[]{:S(2)}, u32[]{:S(2)}) collective-permute-start(bf16[192,2048]{1,0:T(8,128)(2,1)S(1)} %multiply_convert_fusion.refs_0_), channel_id=1, source_target_pairs={{0,2},{1,3},{2,0},{3,1},{4,6},{5,7},{6,4},{7,5},{8,10},{9,11},{10,... | collective-permute-start | bytes 2359304 | tf_op jit(solution)/shard_map/ppermute | solution.py:583
  179.4 38.6 %collective-permute-start.29 = (bf16[704,256]{1,0:T(8,128)(2,1)S(1)}, bf16[704,256]{1,0:T(8,128)(2,1)S(1)}, u32[]{:S(2)}, u32[]{:S(2)}) collective-permute-start(bf16[704,256]{1,0:T(8,128)(2,1)S(1)} %slice.221), channel_id=1, source_target_pairs={{0,8},{8,16},{16,24},{24,28},{28,20},{20,12},{12,4},{4,0},{1,9},{9... | collective-permute-start | bytes 1081352 | tf_op jit(solution)/shard_map/ppermute | solution.py:484
  181.1 37.9 %collective-permute-start.30 = (bf16[704,256]{1,0:T(8,128)(2,1)S(1)}, bf16[704,256]{1,0:T(8,128)(2,1)S(1)}, u32[]{:S(2)}, u32[]{:S(2)}) collective-permute-start(bf16[704,256]{1,0:T(8,128)(2,1)S(1)} %slice.222), channel_id=1, source_target_pairs={{8,0},{16,8},{24,16},{28,24},{20,28},{12,20},{4,12},{0,4},{9,1},{1... | collective-permute-start | bytes 1081352 | tf_op jit(solution)/shard_map/ppermute | solution.py:485
  282.0 46.3 %collective-permute-start.45 = (bf16[256,4224]{1,0:T(8,128)(2,1)S(1)}, bf16[256,4224]{1,0:T(8,128)(2,1)}, u32[]{:S(2)}, u32[]{:S(2)}) collective-permute-start(bf16[256,4224]{1,0:T(8,128)(2,1)S(1)} %pad_maximum_fusion.2), channel_id=1, source_target_pairs={{8,0},{16,8},{24,16},{28,24},{20,28},{12,20},{4,12},{0,4},{9,1},{1... | collective-permute-start | bytes 6488072 | tf_op jit(solution)/shard_map/ppermute | solution.py:505
  286.2 45.9 %collective-permute-start.44 = (bf16[256,4224]{1,0:T(8,128)(2,1)}, bf16[256,4224]{1,0:T(8,128)(2,1)}, u32[]{:S(2)}, u32[]{:S(2)}) collective-permute-start(bf16[256,4224]{1,0:T(8,128)(2,1)} %pad_maximum_fusion.1), channel_id=1, source_target_pairs={{0,8},{8,16},{16,24},{24,28},{28,20},{20,12},{12,4},{4,0},{1,9},{9... | collective-permute-start | bytes 6488072 | tf_op jit(solution)/shard_map/ppermute | solution.py:504
  304.0 35.9 %collective-permute-start.41 = (bf16[192,2048]{1,0:T(8,128)(2,1)S(1)}, bf16[192,2048]{1,0:T(8,128)(2,1)}, u32[]{:S(2)}, u32[]{:S(2)}) collective-permute-start(bf16[192,2048]{1,0:T(8,128)(2,1)S(1)} %get-tuple-element.137.refs_0_), channel_id=1, source_target_pairs={{0,1},{1,0},{2,3},{3,2},{4,5},{5,4},{6,7},{7,6},{8,9},{9,8},{10,11... | collective-permute-start | bytes 2359304 | tf_op jit(solution)/shard_map/ppermute | solution.py:584
  337.6 54.4 %collective-permute-start.52 = (bf16[256,4224]{1,0:T(8,128)(2,1)}, bf16[256,4224]{1,0:T(8,128)(2,1)}, u32[]{:S(2)}, u32[]{:S(2)}) collective-permute-start(bf16[256,4224]{1,0:T(8,128)(2,1)} %get-tuple-element.142), channel_id=1, source_target_pairs={{0,8},{8,16},{16,24},{24,28},{28,20},{20,12},{12,4},{4,0},{1,9},{9... | collective-permute-start | bytes 6488072 | tf_op jit(solution)/shard_map/ppermute | solution.py:504
  339.2 54.4 %collective-permute-start.53 = (bf16[256,4224]{1,0:T(8,128)(2,1)}, bf16[256,4224]{1,0:T(8,128)(2,1)}, u32[]{:S(2)}, u32[]{:S(2)}) collective-permute-start(bf16[256,4224]{1,0:T(8,128)(2,1)} %get-tuple-element.141), channel_id=1, source_target_pairs={{8,0},{16,8},{24,16},{28,24},{20,28},{12,20},{4,12},{0,4},{9,1},{1... | collective-permute-start | bytes 6488072 | tf_op jit(solution)/shard_map/ppermute | solution.py:505
  370.1 38.4 %collective-permute-start.46 = (bf16[384,2048]{1,0:T(8,128)(2,1)}, bf16[384,2048]{1,0:T(8,128)(2,1)}, u32[]{:S(2)}, u32[]{:S(2)}) collective-permute-start(bf16[384,2048]{1,0:T(8,128)(2,1)} %pad_maximum_fusion.6), channel_id=1, source_target_pairs={{0,1},{1,0},{2,3},{3,2},{4,5},{5,4},{6,7},{7,6},{8,9},{9,8},{10,11... | collective-permute-start | bytes 4718600 | tf_op jit(solution)/shard_map/ppermute | solution.py:602
  399.1 65.9 %collective-permute-start.56 = (bf16[256,4224]{1,0:T(8,128)(2,1)}, bf16[256,4224]{1,0:T(8,128)(2,1)S(1)}, u32[]{:S(2)}, u32[]{:S(2)}) collective-permute-start(bf16[256,4224]{1,0:T(8,128)(2,1)} %get-tuple-element.140), channel_id=1, source_target_pairs={{0,8},{8,16},{16,24},{24,28},{28,20},{20,12},{12,4},{4,0},{1,9},{9... | collective-permute-start | bytes 6488072 | tf_op jit(solution)/shard_map/ppermute | solution.py:504
  404.9 60.2 %collective-permute-start.57 = (bf16[256,4224]{1,0:T(8,128)(2,1)}, bf16[256,4224]{1,0:T(8,128)(2,1)S(1)}, u32[]{:S(2)}, u32[]{:S(2)}) collective-permute-start(bf16[256,4224]{1,0:T(8,128)(2,1)} %get-tuple-element.139), channel_id=1, source_target_pairs={{8,0},{16,8},{24,16},{28,24},{20,28},{12,20},{4,12},{0,4},{9,1},{1... | collective-permute-start | bytes 6488072 | tf_op jit(solution)/shard_map/ppermute | solution.py:505
  412.9 52.1 %collective-permute-start.54 = (bf16[256,1152]{1,0:T(8,128)(2,1)S(1)}, bf16[256,1152]{1,0:T(8,128)(2,1)S(1)}, u32[]{:S(2)}, u32[]{:S(2)}) collective-permute-start(bf16[256,1152]{1,0:T(8,128)(2,1)S(1)} %get-tuple-element.146), channel_id=1, source_target_pairs={{0,8},{8,16},{16,24},{24,28},{28,20},{20,12},{12,4},{4,0},{1,9},{9... | collective-permute-start | bytes 1769480 | tf_op jit(solution)/shard_map/ppermute | solution.py:504
  414.6 50.5 %collective-permute-start.55 = (bf16[256,1152]{1,0:T(8,128)(2,1)S(1)}, bf16[256,1152]{1,0:T(8,128)(2,1)S(1)}, u32[]{:S(2)}, u32[]{:S(2)}) collective-permute-start(bf16[256,1152]{1,0:T(8,128)(2,1)S(1)} %get-tuple-element.145), channel_id=1, source_target_pairs={{8,0},{16,8},{24,16},{28,24},{20,28},{12,20},{4,12},{0,4},{9,1},{1... | collective-permute-start | bytes 1769480 | tf_op jit(solution)/shard_map/ppermute | solution.py:505
  (119 other events, 1354.8 us)

commit v5 on v4

--- a/solution.py
+++ b/solution.py
@@ -220,15 +220,44 @@
 def rows_of(width, tile=TILE):
     return pl.BlockSpec((tile, width), lambda i: (i, 0))
 
-def gate_up_kernel(units, x_ref, grad_ref, *refs):
-    pieces, hidden_ref, out_ref = refs[:-2], refs[-2], refs[-1]
+def gate_up_start_kernel(units, x_ref, *refs):
+    pieces, out_ref = refs[:-1], refs[-1]
     for start in range(0, units, 128):
         there = slice(start, start + 128)
         pairs = [
             jnp.concatenate([ref[:, there], ref[:, units + start : units + start + 128]], axis=1)
             for ref in pieces
         ]
-        both = nn(x_ref[...], jnp.concatenate(pairs, axis=0))
+        depth = len(pairs) * pieces[0].shape[0]
+        out_ref[:, 2 * start : 2 * start + 256] = nn(x_ref[:, :depth], jnp.concatenate(pairs, axis=0))
+
+
+def gate_up_start(x, pieces):
+    total, wide = x.shape
+    units = pieces[0].shape[1] // 2
+    return pl.pallas_call(
+        functools.partial(gate_up_start_kernel, units),
+        grid=(total // TILE,),
+        in_specs=[rows_of(wide)] + [whole(p) for p in pieces],
+        out_specs=rows_of(2 * units),
+        out_shape=jax.ShapeDtypeStruct((total, 2 * units), FULL),
+        compiler_params=pltpu.CompilerParams(vmem_limit_bytes=VMEM),
+        cost_estimate=lasting(12.0),
+        name="gate_up_start",
+    )(x, *pieces)
+
+
+def gate_up_kernel(units, x_ref, grad_ref, sum_ref, *refs):
+    pieces, hidden_ref, out_ref = refs[:-2], refs[-2], refs[-1]
+    depth = x_ref.shape[1] - sum(ref.shape[0] for ref in pieces)
+    for start in range(0, units, 128):
+        there = slice(start, start + 128)
+        pairs = [
+            jnp.concatenate([ref[:, there], ref[:, units + start : units + start + 128]], axis=1)
+            for ref in pieces
+        ]
+        both = nn(x_ref[:, depth:], jnp.concatenate(pairs, axis=0))
+        both = both + sum_ref[:, 2 * start : 2 * start + 256]
         gate, up = both[:, :128], both[:, 128:]
         sigma = jax.nn.sigmoid(gate)
         swish = gate * sigma
@@ -238,22 +267,22 @@
         out_ref[:, units + start : units + start + 128] = (grad * swish).astype(HALF)
 
 
-def gate_up(x, grad, pieces):
+def gate_up(x, grad, sums, pieces):
     total, wide = x.shape
     units = pieces[0].shape[1] // 2
     return pl.pallas_call(
         functools.partial(gate_up_kernel, units),
         grid=(total // TILE,),
-        in_specs=[rows_of(wide), rows_of(units)] + [whole(p) for p in pieces],
+        in_specs=[rows_of(wide), rows_of(units), rows_of(2 * units)] + [whole(p) for p in pieces],
         out_specs=[rows_of(units), rows_of(2 * units)],
         out_shape=(
             jax.ShapeDtypeStruct((total, units), HALF),
             jax.ShapeDtypeStruct((total, 2 * units), HALF),
         ),
         compiler_params=pltpu.CompilerParams(vmem_limit_bytes=VMEM),
-        cost_estimate=lasting(16.5),
+        cost_estimate=lasting(6.0),
         name="gate_up",
-    )(x, grad, *pieces)
+    )(x, grad, sums, *pieces)
 
 
 def hidden_back_kernel(slots, x_ref, *refs):
@@ -301,37 +330,28 @@
         out_refs[0][:, there] = part[:half]
         out_refs[1][:, there] = part[half:]
 
-    if early:
-        pl.when(pl.program_id(0) == 0)(functools.partial(make, write_halves))
-        pl.when(pl.program_id(0) > 0)(functools.partial(make, write_whole))
-    else:
-        make(write_whole)
-
-
-def feed_grads(x, feed, grad, hidden, slots, block, early):
+    make(write_halves if early else write_whole)
+
+
+def feed_grads(x, feed, grad, hidden, slots, block, which):
     total = x.shape[0]
     units = hidden.shape[1]
+    start, stop = ((slots - 1, slots), (slots - 3, slots - 1), (0, slots - 3))[which]
     if block % 128:
-        parts = []
-        for start, stop in ((slots - 1, slots), (slots - 3, slots - 1)) if early else ((0, slots - 3),):
-            there = slice(start * block, stop * block)
-            part = [contract_rows(x[:, there], feed), contract_rows(grad[:, there], hidden)]
-            parts.append(jnp.concatenate(part, axis=1).astype(HALF))
-        return [*jnp.split(parts[0], 2), parts[1]] if early else parts
-    place = (lambda i: (0, slots - 1 - i)) if early else (lambda i: (0, i))
-    columns = pl.BlockSpec((total, block), place)
-    shapes = [(block // 2, 3 * units)] * 2 + [(2 * block, 3 * units)] if early else [((slots - 3) * block, 3 * units)]
-    out_specs = [pl.BlockSpec((block, 3 * units), (lambda i: (2 - jnp.maximum(i, 1), 0)) if early else (lambda i: (i, 0)))]
-    if early:
-        out_specs = [pl.BlockSpec((block // 2, 3 * units), lambda i: (0, 0))] * 2 + out_specs
-    return pl.pallas_call(
-        functools.partial(feed_grads_kernel, early),
-        grid=(3 if early else slots - 3,),
+        there = slice(start * block, stop * block)
+        part = [contract_rows(x[:, there], feed), contract_rows(grad[:, there], hidden)]
+        part = jnp.concatenate(part, axis=1).astype(HALF)
+        return jnp.split(part, 2) if which == 0 else [part]
+    columns = pl.BlockSpec((total, block), lambda i: (0, start + i))
+    count = 2 if which == 0 else 1
+    return pl.pallas_call(
+        functools.partial(feed_grads_kernel, which == 0),
+        grid=(stop - start,),
         in_specs=[columns, whole(feed), columns, whole(hidden)],
-        out_specs=out_specs,
-        out_shape=[jax.ShapeDtypeStruct(shape, HALF) for shape in shapes],
-        compiler_params=pltpu.CompilerParams(vmem_limit_bytes=VMEM),
-        cost_estimate=lasting(0.0),
+        out_specs=[pl.BlockSpec((block // count, 3 * units), lambda i: (i, 0))] * count,
+        out_shape=[jax.ShapeDtypeStruct(((stop - start) * block // count, 3 * units), HALF)] * count,
+        compiler_params=pltpu.CompilerParams(vmem_limit_bytes=VMEM),
+        cost_estimate=lasting((0.0, 20.0, 0.0)[which]),
         name="feed_grads",
     )(x, feed, grad, hidden)
 
@@ -479,7 +499,7 @@
         if after:
             self.above, self.below = tie((self.above, self.below), *after)
         if len(self.marks) == ring.half - 1:
-            cut = self.above.shape[0] // 2
+            cut = self.above.shape[0] // 32 * 16
             self.above, self.below = self.above[:cut], self.below[cut:]
         self.above = lax.ppermute(self.above, "dp", ring.up)
         self.below = lax.ppermute(self.below, "dp", ring.down)
@@ -591,7 +611,7 @@
             name="join",
         )(rows, near, first, far)
 
-    def scatter_rows(self, values):
+    def scatter_rows(self, values, *after):
         mine = lax.axis_index("tensor")
         count = values.shape[0] // 4
 
@@ -599,6 +619,8 @@
             return lax.dynamic_slice_in_dim(values, (mine ^ index) * count, count, 0)
 
         given = jnp.concatenate([piece(3), piece(1)], axis=0)
+        if after:
+            given = tie(given, *after)
         given = lax.ppermute(given, "tensor", beside(1)).astype(FULL)
         send = (piece(2).astype(FULL) + given[:count]).astype(HALF)
         far = lax.ppermute(send, "tensor", beside(2)).astype(FULL)
@@ -644,7 +666,7 @@
         ],
         axis=1,
     )
-    gains = jnp.pad(gains, ((0, 30), (0, first_shard.shape[1] - block)))
+    gains = jnp.pad(gains, ((0, 14), (0, first_shard.shape[1] - block)))
     first_shard = jnp.concatenate([first_shard, gains], axis=0)
     whole_way = ring.half
     first_travel = ring.gather(first_shard).steps(whole_way)
@@ -686,15 +708,17 @@
         "output",
         view,
     )
-    middle = resid + ring.scatter_rows(tie(partial_mixed, down_marks[1], feed_marks[0]))
+    middle = resid + ring.scatter_rows(partial_mixed, down_marks[1], feed_marks[0])
     middle = tie(middle, feed_marks[1])
     scale_two = rms_scale(middle)
     rows_two = ring.gather_rows((middle * scale_two * gain_two).astype(HALF))
     grad_out = cotangent.astype(FULL)
     grad_hidden = hidden_back(grad_rows, down_pieces, slots)
-    hidden, grad_feed = gate_up(rows_two, grad_hidden, feed_pieces)
-
-    *feed_far, feed_mid = feed_grads(rows_two, grad_feed, grad_rows, hidden, slots, block, True)
+    feed_start = gate_up_start(rows_two, feed_pieces[:-2])
+    hidden, grad_feed = gate_up(rows_two, grad_hidden, feed_start, feed_pieces[-2:])
+
+    feed_far = feed_grads(rows_two, grad_feed, grad_rows, hidden, slots, block, 0)
+    (feed_mid,) = feed_grads(tie(rows_two, feed_far), grad_feed, grad_rows, hidden, slots, block, 1)
     feed_near = None
 
     def feed_part(slot):
@@ -717,7 +741,7 @@
     middle_given = grad_middle.astype(HALF)
     middle_rows = ring.gather_rows(middle_given)
     (feed_near,) = feed_grads(
-        tie(rows_two, feed_sums.sent, middle_given), grad_feed, grad_rows, hidden, slots, block, False
+        tie(rows_two, feed_sums.sent, middle_given), grad_feed, grad_rows, hidden, slots, block, 2
     )
     partial_out = outward(
         tie(hidden, feed_near), down_pieces, slots, units, block, False, 0.0, "down"
@@ -765,7 +789,9 @@
             (feed_sum[:, : 2 * units], feed_shard, feed_gain),
         )
     ]
-    gain_sums = lax.psum(jnp.stack(gain_sums), "tensor")
+    gain_sums = jnp.stack(gain_sums)
+    for index in (1, 2):
+        gain_sums = gain_sums + lax.ppermute(gain_sums, "tensor", beside(index))
     return (
         layer_out,
         input_grad,

time: 502 us -> 480 us (0.956)
  waiting for transfers between devices: 239 us -> 222 us
  blocking collectives: 5.99 us -> 0 us
    ppermute x12, waiting for transfers between devices: 91.3 us -> 71.5 us  [step(): self.above = lax.ppermute(self.above, 'dp', ring.up)]
    ppermute x4, waiting for transfers between devices: 34.6 us -> 52.8 us  [scatter_rows(): far = lax.ppermute(send, 'tensor', beside(2)).astype(FULL)]
    ppermute x12, waiting for transfers between devices: 39.9 us -> 26.9 us  [step(): self.below = lax.ppermute(self.below, 'dp', ring.down)]
    pallas_call x2 -> x4, Pallas kernels: 16.8 us -> 27.9 us  [the longest x3 16.4 us: feed_grads(): pl.pallas_call(functools.partial(feed_grads_kernel, which == 0), grid=(st...]
    pallas_call x1, Pallas kernels: 13.9 us -> 3.36 us  [gate_up(): pl.pallas_call(functools.partial(gate_up_kernel, units), grid=(total // T...]
    ppermute x8, waiting for transfers between devices: 56.2 us -> 47.6 us  [send(): self.above = lax.ppermute(top, 'dp', self.ring.up)]
    psum x1 -> x0, blocking collectives: 5.99 us -> none  [per_device(): gain_sums = lax.psum(jnp.stack(gain_sums), 'tensor')]
    ppermute x4, waiting for transfers between devices: 1.64 us -> 7.22 us  [gather_rows(): first = lax.ppermute(rows, 'tensor', beside(2))]
  transfers between devices with their start and end apart: 60 -> 62, of which waited for: 30 -> 35; matrix products, arithmetic and copies ran while one was open for 12% -> 13% of each run, Pallas kernels for 16% -> 21%
where the time goes in v5:
time: 480 us; the launch traced here: 471 us
  waiting for transfers between devices  222 us (46%)
  Pallas kernels  105 us (22%)
  starting transfers between devices  56.1 us (12%)
  other arithmetic  49.7 us (10%)
  local copies, waits for them, and re-layouts  31.2 us (6%)
  matrix products  4.83 us (1%)
    ppermute x12, waiting for transfers between devices, step(): self.above = lax.ppermute(self.above, 'dp', ring.up)  71.5 us
    ppermute x4, waiting for transfers between devices, scatter_rows(): far = lax.ppermute(send, 'tensor', beside(2)).astype(FULL)  52.8 us
    ppermute x8, waiting for transfers between devices, send(): self.above = lax.ppermute(top, 'dp', self.ring.up)  47.6 us
    ppermute x12, waiting for transfers between devices, step(): self.below = lax.ppermute(self.below, 'dp', ring.down)  26.9 us
    unnamed x164, local copies, waits for them, and re-layouts  24.5 us
    pallas_call x3, Pallas kernels, outward(): pl.pallas_call(functools.partial(outward_kernel, slots, depth, view, tran...  22.4 us
    pallas_call x3, Pallas kernels, feed_grads(): pl.pallas_call(functools.partial(feed_grads_kernel, which == 0), grid=(st...  16.4 us
    convert_element_type x6, other arithmetic, total(): joined = (own[first:last].astype(FULL) + arrived.astype(FULL)).astype(HALF)  15.1 us
  transfers between devices with their start and end apart: 62, of which 35 were waited for; matrix products, arithmetic and copies ran while one was open for 13% of the time, Pallas kernels for 21%

profile of v5, /device:TPU:0, one launch (start us, length us, event | category | flops | bytes accessed | tf_op | source)
XLA Modules:
  0.0 471.1 jit_solution(10857486470357291983)
XLA Ops:
  6.6 13.2 %collective-permute-done.4.refs_2_ = bf16[272,1152]{1,0:T(8,128)(2,1)S(1)} collective-permute-done((bf16[272,1152]{1,0:T(8,128)(2,1)S(1)}, bf16[272,1152]{1,0:T(8,128)(2,1)S(1)}, u32[]{:S(2)}, u32[]{:S(2)}) %collective-permute-start.4) | collective-permute-done | bytes 626720 | tf_op jit(solution)/shard_map/ppermute | solution.py:505
  27.1 8.0 %collective-permute-done.6.refs_4_ = bf16[272,1152]{1,0:T(8,128)(2,1)S(1)} collective-permute-done((bf16[272,1152]{1,0:T(8,128)(2,1)S(1)}, bf16[272,1152]{1,0:T(8,128)(2,1)S(1)}, u32[]{:S(2)}, u32[]{:S(2)}) %collective-permute-start.6) | collective-permute-done | bytes 626720 | tf_op jit(solution)/shard_map/ppermute | solution.py:505
  38.8 7.2 %collective-permute-done.1.refs_2_ = bf16[192,2048]{1,0:T(8,128)(2,1)} collective-permute-done((bf16[192,2048]{1,0:T(8,128)(2,1)S(1)}, bf16[192,2048]{1,0:T(8,128)(2,1)}, u32[]{:S(2)}, u32[]{:S(2)}) %collective-permute-start.1) | collective-permute-done | bytes 786464 | tf_op jit(solution)/shard_map/ppermute | solution.py:603
  70.0 12.5 %collective-permute-done.11.refs_1_ = bf16[1408,256]{1,0:T(8,128)(2,1)} collective-permute-done((bf16[1408,256]{1,0:T(8,128)(2,1)}, bf16[1408,256]{1,0:T(8,128)(2,1)}, u32[]{:S(2)}, u32[]{:S(2)}) %collective-permute-start.11) | collective-permute-done | bytes 720928 | tf_op jit(solution)/shard_map/ppermute | solution.py:504
  97.9 12.4 %attend.1 = (bf16[768,512]{1,0:T(8,128)(2,1)S(1)}, bf16[768,128]{1,0:T(8,128)(2,1)S(1)}, bf16[768,512]{1,0:T(8,128)(2,1)S(1)}, f32[8,1,768]{2,1,0:T(1,128)S(1)}) custom-call(f32[768,640]{1,0:T(8,128)S(1)} %get-tuple-element.55.joined_ref, f32[768,128]{1,0:T(8,128)S(1)} %copy-done.29, f32[768,128]{1,0:T(8,128)S(1)} %pad_maximum_fusion.11.sin_ref, ...), custom_call_target="tpu_custom_call" | custom-call | tf_op jit(solution)/shard_map/attend/pallas_call | solution.py:127
  115.7 10.7 %collective-permute-done.16.refs_3_ = bf16[1408,256]{1,0:T(8,128)(2,1)} collective-permute-done((bf16[1408,256]{1,0:T(8,128)(2,1)}, bf16[1408,256]{1,0:T(8,128)(2,1)}, u32[]{:S(2)}, u32[]{:S(2)}) %collective-permute-start.16) | collective-permute-done | bytes 720928 | tf_op jit(solution)/shard_map/ppermute | solution.py:504
  139.9 16.2 %collective-permute-done.21 = bf16[192,2048]{1,0:T(8,128)(2,1)} collective-permute-done((bf16[192,2048]{1,0:T(8,128)(2,1)}, bf16[192,2048]{1,0:T(8,128)(2,1)}, u32[]{:S(2)}, u32[]{:S(2)}) %collective-permute-start.21) | collective-permute-done | bytes 786464 | tf_op jit(solution)/shard_map/ppermute | solution.py:626
  165.7 10.7 %collective-permute-done.27.refs_5_ = bf16[1408,256]{1,0:T(8,128)(2,1)S(1)} collective-permute-done((bf16[1408,256]{1,0:T(8,128)(2,1)}, bf16[1408,256]{1,0:T(8,128)(2,1)S(1)}, u32[]{:S(2)}, u32[]{:S(2)}) %collective-permute-start.27) | collective-permute-done | bytes 720928 | tf_op jit(solution)/shard_map/ppermute | solution.py:504
  180.7 7.1 %collective-permute-done.29.refs_7_ = bf16[704,256]{1,0:T(8,128)(2,1)S(1)} collective-permute-done((bf16[704,256]{1,0:T(8,128)(2,1)S(1)}, bf16[704,256]{1,0:T(8,128)(2,1)S(1)}, u32[]{:S(2)}, u32[]{:S(2)}) %collective-permute-start.29) | collective-permute-done | bytes 360480 | tf_op jit(solution)/shard_map/ppermute | solution.py:504
  189.7 7.6 %hidden_back.1.grad_ref = f32[768,1408]{1,0:T(8,128)S(1)} custom-call(bf16[768,2048]{1,0:T(8,128)(2,1)S(1)} %join.5.x_ref.grad_ref, bf16[1408,256]{1,0:T(8,128)(2,1)} %convert_element_type.282.refs_0_, bf16[1408,256]{1,0:T(8,128)(2,1)} %collective-permute-done.11.refs_1_, bf16[1408,256]{1,0:T(8,128)(2,1)} %collective-permute-done.12.refs_2_, ...), custom_call_target="tpu_custom_call" | custom-call | flops 11879999488 | tf_op jit(solution)/shard_map/hidden_back/pallas_call | solution.py:301
  197.4 20.0 %collective-permute-done.31.refs_5_ = bf16[256,2816]{1,0:T(8,128)(2,1)S(1)} collective-permute-done((bf16[256,2816]{1,0:T(8,128)(2,1)}, bf16[256,2816]{1,0:T(8,128)(2,1)S(1)}, u32[]{:S(2)}, u32[]{:S(2)}) %collective-permute-start.31) | collective-permute-done | bytes 1441824 | tf_op jit(solution)/shard_map/ppermute | solution.py:504
  219.8 11.5 %gate_up_start.1.sum_ref = f32[768,2816]{1,0:T(8,128)S(1)} custom-call(bf16[768,2048]{1,0:T(8,128)(2,1)S(1)} %join.6.x_ref, bf16[256,2816]{1,0:T(8,128)(2,1)} %pad_maximum_fusion.7.refs_0_, bf16[256,2816]{1,0:T(8,128)(2,1)} %collective-permute-done.18.refs_1_, bf16[256,2816]{1,0:T(8,128)(2,1)} %collective-permute-done.19.refs_2_, ...), custom_call_target="tpu_custom_call" | custom-call | flops 13200000000 | tf_op jit(solution)/shard_map/gate_up_start/pallas_call | solution.py:238
  247.5 12.7 %feed_back.1 = bf16[768,2048]{1,0:T(8,128)(2,1)S(1)} custom-call(bf16[768,2816]{1,0:T(8,128)(2,1)S(1)} %get-tuple-element.68.feed_ref.x_ref, bf16[256,2816]{1,0:T(8,128)(2,1)} %pad_maximum_fusion.7.refs_0_, bf16[256,2816]{1,0:T(8,128)(2,1)} %collective-permute-done.18.refs_1_, bf16[256,2816]{1,0:T(8,128)(2,1)} %collective-permute-done.19.refs_2_, ...), custom_call_target="tpu_custom_call" | custom-call | tf_op jit(solution)/shard_map/feed_back/pallas_call | solution.py:370
  272.4 12.2 %collective-permute-done.38 = bf16[192,2048]{1,0:T(8,128)(2,1)S(1)} collective-permute-done((bf16[192,2048]{1,0:T(8,128)(2,1)S(1)}, bf16[192,2048]{1,0:T(8,128)(2,1)S(1)}, u32[]{:S(2)}, u32[]{:S(2)}) %collective-permute-start.38) | collective-permute-done | bytes 786464 | tf_op jit(solution)/shard_map/ppermute | solution.py:626
  290.3 10.3 %feed_grads.5 = bf16[1280,4224]{1,0:T(8,128)(2,1)S(1)} custom-call(bf16[768,2048]{1,0:T(8,128)(2,1)S(1)} %join.6.x_ref, bf16[768,2816]{1,0:T(8,128)(2,1)S(1)} %get-tuple-element.68.feed_ref.x_ref, bf16[768,2048]{1,0:T(8,128)(2,1)S(1)} %join.5.x_ref.grad_ref, bf16[768,1408]{1,0:T(8,128)(2,1)S(1)} %get-tuple-element.72.hidden_ref.x_ref), custom_call_target="tpu_custom_call" | custom-call | tf_op jit(solution)/shard_map/feed_grads/pallas_call | solution.py:347
  300.7 7.4 %down.1 = bf16[768,2048]{1,0:T(8,128)(2,1)S(1)} custom-call(bf16[768,1408]{1,0:T(8,128)(2,1)S(1)} %get-tuple-element.72.hidden_ref.x_ref, bf16[1408,256]{1,0:T(8,128)(2,1)} %convert_element_type.282.refs_0_, bf16[1408,256]{1,0:T(8,128)(2,1)} %collective-permute-done.11.refs_1_, bf16[1408,256]{1,0:T(8,128)(2,1)} %collective-permute-done.12.refs_2_, ...), custom_call_target="tpu_custom_call" | custom-call | tf_op jit(solution)/shard_map/down/pallas_call | solution.py:370
  308.7 4.7 %collective-permute-done.45 = bf16[256,4224]{1,0:T(8,128)(2,1)} collective-permute-done((bf16[256,4224]{1,0:T(8,128)(2,1)S(1)}, bf16[256,4224]{1,0:T(8,128)(2,1)}, u32[]{:S(2)}, u32[]{:S(2)}) %collective-permute-start.45) | collective-permute-done | bytes 2162720 | tf_op jit(solution)/shard_map/ppermute | solution.py:525
  315.6 5.2 %add_convert_fusion.2 = (bf16[256,4224]{1,0:T(8,128)(2,1)}, bf16[256,4224]{1,0:T(8,128)(2,1)}) fusion(bf16[256,4224]{1,0:T(8,128)(2,1)} %collective-permute-done.45, bf16[1280,4224]{1,0:T(8,128)(2,1)S(1)} %feed_grads.5, bf16[256,4224]{1,0:T(8,128)(2,1)} %collective-permute-done.44), kind=kLoop, calls=%fused_computation.26 | loop fusion | flops 8650752 | bytes 12976128 | tf_op jit(solution)/shard_map/convert_element_type | solution.py:532
  327.6 13.7 %attend_back.1.grad_ref = bf16[768,640]{1,0:T(8,128)(2,1)S(1)} custom-call(bf16[768,512]{1,0:T(8,128)(2,1)S(1)} %copy-done.40, bf16[768,128]{1,0:T(8,128)(2,1)S(1)} %copy-done.46, bf16[768,512]{1,0:T(8,128)(2,1)S(1)} %mixed_back.1.do_ref, f32[8,1,768]{2,1,0:T(1,128)S(1)} %get-tuple-element.78.lse_ref, f32[768,128]{1,0:T(8,128)S(1)} %copy-done.30, ...), custom_call_target="tpu_custom_call" | custom-call | tf_op jit(solution)/shard_map/attend_back/pallas_call | solution.py:193
  354.6 16.6 %collective-permute-done.48 = bf16[128,1152]{1,0:T(8,128)(2,1)S(1)} collective-permute-done((bf16[128,1152]{1,0:T(8,128)(2,1)S(1)}, bf16[128,1152]{1,0:T(8,128)(2,1)S(1)}, u32[]{:S(2)}, u32[]{:S(2)}) %collective-permute-start.48) | collective-permute-done | bytes 294944 | tf_op jit(solution)/shard_map/ppermute | solution.py:524
  376.0 5.3 %add_convert_fusion = (bf16[256,4224]{1,0:T(8,128)(2,1)}, bf16[256,4224]{1,0:T(8,128)(2,1)}) fusion(bf16[256,4224]{1,0:T(8,128)(2,1)} %collective-permute-done.53, bf16[1280,4224]{1,0:T(8,128)(2,1)S(1)} %feed_grads.5, bf16[256,4224]{1,0:T(8,128)(2,1)} %collective-permute-done.52), kind=kLoop, calls=%fused_computation.24 | loop fusion | flops 8650752 | bytes 12976128 | tf_op jit(solution)/shard_map/convert_element_type | solution.py:532
  397.7 12.9 %collective-permute-done.47 = bf16[192,2048]{1,0:T(8,128)(2,1)S(1)} collective-permute-done((bf16[192,2048]{1,0:T(8,128)(2,1)S(1)}, bf16[192,2048]{1,0:T(8,128)(2,1)S(1)}, u32[]{:S(2)}, u32[]{:S(2)}) %collective-permute-start.47) | collective-permute-done | bytes 786464 | tf_op jit(solution)/shard_map/ppermute | solution.py:626
  413.0 11.5 %collective-permute-done.40 = bf16[192,2048]{1,0:T(8,128)(2,1)S(1)} collective-permute-done((bf16[192,2048]{1,0:T(8,128)(2,1)S(1)}, bf16[192,2048]{1,0:T(8,128)(2,1)S(1)}, u32[]{:S(2)}, u32[]{:S(2)}) %collective-permute-start.40) | collective-permute-done | bytes 786464 | tf_op jit(solution)/shard_map/ppermute | solution.py:626
  426.8 20.7 %collective-permute-done.54 = bf16[256,1152]{1,0:T(8,128)(2,1)S(1)} collective-permute-done((bf16[256,1152]{1,0:T(8,128)(2,1)S(1)}, bf16[256,1152]{1,0:T(8,128)(2,1)S(1)}, u32[]{:S(2)}, u32[]{:S(2)}) %collective-permute-start.54) | collective-permute-done | bytes 589856 | tf_op jit(solution)/shard_map/ppermute | solution.py:524
  (375 shorter events, 198.0 us)
Async XLA Ops:
  37.2 28.5 %collective-permute-start.14 = (bf16[192,2048]{1,0:T(8,128)(2,1)}, bf16[192,2048]{1,0:T(8,128)(2,1)}, u32[]{:S(2)}, u32[]{:S(2)}) collective-permute-start(bf16[192,2048]{1,0:T(8,128)(2,1)} %get-tuple-element.57.refs_0_), channel_id=1, source_target_pairs={{0,2},{1,3},{2,0},{3,1},{4,6},{5,7},{6,4},{7,5},{8,10},{9,11},{10,... | collective-permute-start | bytes 2359304 | tf_op jit(solution)/shard_map/ppermute | solution.py:603
  65.2 61.6 %collective-permute-start.18 = (bf16[256,2816]{1,0:T(8,128)(2,1)}, bf16[256,2816]{1,0:T(8,128)(2,1)}, u32[]{:S(2)}, u32[]{:S(2)}) collective-permute-start(bf16[256,2816]{1,0:T(8,128)(2,1)} %pad_maximum_fusion.7.refs_0_), channel_id=1, source_target_pairs={{0,8},{8,16},{16,24},{24,28},{28,20},{20,12},{12,4},{4,0},{1,9},{9... | collective-permute-start | bytes 4325384 | tf_op jit(solution)/shard_map/ppermute | solution.py:504
  65.7 61.0 %collective-permute-start.19 = (bf16[256,2816]{1,0:T(8,128)(2,1)}, bf16[256,2816]{1,0:T(8,128)(2,1)}, u32[]{:S(2)}, u32[]{:S(2)}) collective-permute-start(bf16[256,2816]{1,0:T(8,128)(2,1)} %pad_maximum_fusion.7.refs_0_), channel_id=1, source_target_pairs={{8,0},{16,8},{24,16},{28,24},{20,28},{12,20},{4,12},{0,4},{9,1},{1... | collective-permute-start | bytes 4325384 | tf_op jit(solution)/shard_map/ppermute | solution.py:505
  82.5 43.9 %collective-permute-start.16 = (bf16[1408,256]{1,0:T(8,128)(2,1)}, bf16[1408,256]{1,0:T(8,128)(2,1)}, u32[]{:S(2)}, u32[]{:S(2)}) collective-permute-start(bf16[1408,256]{1,0:T(8,128)(2,1)} %collective-permute-done.11.refs_1_), channel_id=1, source_target_pairs={{0,8},{8,16},{16,24},{24,28},{28,20},{20,12},{12,4},{4,0},{1,9},{9... | collective-permute-start | bytes 2162696 | tf_op jit(solution)/shard_map/ppermute | solution.py:504
  83.0 43.8 %collective-permute-start.17 = (bf16[1408,256]{1,0:T(8,128)(2,1)}, bf16[1408,256]{1,0:T(8,128)(2,1)}, u32[]{:S(2)}, u32[]{:S(2)}) collective-permute-start(bf16[1408,256]{1,0:T(8,128)(2,1)} %collective-permute-done.12.refs_2_), channel_id=1, source_target_pairs={{8,0},{16,8},{24,16},{28,24},{20,28},{12,20},{4,12},{0,4},{9,1},{1... | collective-permute-start | bytes 2162696 | tf_op jit(solution)/shard_map/ppermute | solution.py:505
  126.8 34.8 %collective-permute-start.22 = (bf16[256,2816]{1,0:T(8,128)(2,1)}, bf16[256,2816]{1,0:T(8,128)(2,1)}, u32[]{:S(2)}, u32[]{:S(2)}) collective-permute-start(bf16[256,2816]{1,0:T(8,128)(2,1)} %collective-permute-done.18.refs_1_), channel_id=1, source_target_pairs={{0,8},{8,16},{16,24},{24,28},{28,20},{20,12},{12,4},{4,0},{1,9},{9... | collective-permute-start | bytes 4325384 | tf_op jit(solution)/shard_map/ppermute | solution.py:504
  128.6 35.2 %collective-permute-start.23 = (bf16[256,2816]{1,0:T(8,128)(2,1)}, bf16[256,2816]{1,0:T(8,128)(2,1)}, u32[]{:S(2)}, u32[]{:S(2)}) collective-permute-start(bf16[256,2816]{1,0:T(8,128)(2,1)} %collective-permute-done.19.refs_2_), channel_id=1, source_target_pairs={{8,0},{16,8},{24,16},{28,24},{20,28},{12,20},{4,12},{0,4},{9,1},{1... | collective-permute-start | bytes 4325384 | tf_op jit(solution)/shard_map/ppermute | solution.py:505
  137.8 38.6 %collective-permute-start.27 = (bf16[1408,256]{1,0:T(8,128)(2,1)}, bf16[1408,256]{1,0:T(8,128)(2,1)S(1)}, u32[]{:S(2)}, u32[]{:S(2)}) collective-permute-start(bf16[1408,256]{1,0:T(8,128)(2,1)} %collective-permute-done.16.refs_3_), channel_id=1, source_target_pairs={{0,8},{8,16},{16,24},{24,28},{28,20},{20,12},{12,4},{4,0},{1,9},{9... | collective-permute-start | bytes 2162696 | tf_op jit(solution)/shard_map/ppermute | solution.py:504
  139.5 38.8 %collective-permute-start.28 = (bf16[1408,256]{1,0:T(8,128)(2,1)}, bf16[1408,256]{1,0:T(8,128)(2,1)S(1)}, u32[]{:S(2)}, u32[]{:S(2)}) collective-permute-start(bf16[1408,256]{1,0:T(8,128)(2,1)} %collective-permute-done.17.refs_4_), channel_id=1, source_target_pairs={{8,0},{16,8},{24,16},{28,24},{20,28},{12,20},{4,12},{0,4},{9,1},{1... | collective-permute-start | bytes 2162696 | tf_op jit(solution)/shard_map/ppermute | solution.py:505
  178.7 38.7 %collective-permute-start.31 = (bf16[256,2816]{1,0:T(8,128)(2,1)}, bf16[256,2816]{1,0:T(8,128)(2,1)S(1)}, u32[]{:S(2)}, u32[]{:S(2)}) collective-permute-start(bf16[256,2816]{1,0:T(8,128)(2,1)} %collective-permute-done.22.refs_3_), channel_id=1, source_target_pairs={{0,8},{8,16},{16,24},{24,28},{28,20},{20,12},{12,4},{4,0},{1,9},{9... | collective-permute-start | bytes 4325384 | tf_op jit(solution)/shard_map/ppermute | solution.py:504
  180.4 38.8 %collective-permute-start.32 = (bf16[256,2816]{1,0:T(8,128)(2,1)}, bf16[256,2816]{1,0:T(8,128)(2,1)S(1)}, u32[]{:S(2)}, u32[]{:S(2)}) collective-permute-start(bf16[256,2816]{1,0:T(8,128)(2,1)} %collective-permute-done.23.refs_4_), channel_id=1, source_target_pairs={{8,0},{16,8},{24,16},{28,24},{20,28},{12,20},{4,12},{0,4},{9,1},{1... | collective-permute-start | bytes 4325384 | tf_op jit(solution)/shard_map/ppermute | solution.py:505
  187.8 31.8 %collective-permute-start.24 = (bf16[192,2048]{1,0:T(8,128)(2,1)S(1)}, bf16[192,2048]{1,0:T(8,128)(2,1)S(1)}, u32[]{:S(2)}, u32[]{:S(2)}) collective-permute-start(bf16[192,2048]{1,0:T(8,128)(2,1)S(1)} %multiply_convert_fusion.refs_0_), channel_id=1, source_target_pairs={{0,1},{1,0},{2,3},{3,2},{4,5},{5,4},{6,7},{7,6},{8,9},{9,8},{10,11... | collective-permute-start | bytes 2359304 | tf_op jit(solution)/shard_map/ppermute | solution.py:604
  187.9 31.8 %collective-permute-start.26 = (bf16[192,2048]{1,0:T(8,128)(2,1)S(1)}, bf16[192,2048]{1,0:T(8,128)(2,1)S(1)}, u32[]{:S(2)}, u32[]{:S(2)}) collective-permute-start(bf16[192,2048]{1,0:T(8,128)(2,1)S(1)} %collective-permute-done.25.refs_2_), channel_id=1, source_target_pairs={{0,1},{1,0},{2,3},{3,2},{4,5},{5,4},{6,7},{7,6},{8,9},{9,8},{10,11... | collective-permute-start | bytes 2359304 | tf_op jit(solution)/shard_map/ppermute | solution.py:605
  268.0 45.4 %collective-permute-start.45 = (bf16[256,4224]{1,0:T(8,128)(2,1)S(1)}, bf16[256,4224]{1,0:T(8,128)(2,1)}, u32[]{:S(2)}, u32[]{:S(2)}) collective-permute-start(bf16[256,4224]{1,0:T(8,128)(2,1)S(1)} %pad_maximum_fusion.2), channel_id=1, source_target_pairs={{8,0},{16,8},{24,16},{28,24},{20,28},{12,20},{4,12},{0,4},{9,1},{1... | collective-permute-start | bytes 6488072 | tf_op jit(solution)/shard_map/ppermute | solution.py:525
  270.8 44.9 %collective-permute-start.44 = (bf16[256,4224]{1,0:T(8,128)(2,1)S(1)}, bf16[256,4224]{1,0:T(8,128)(2,1)}, u32[]{:S(2)}, u32[]{:S(2)}) collective-permute-start(bf16[256,4224]{1,0:T(8,128)(2,1)S(1)} %pad_maximum_fusion.1), channel_id=1, source_target_pairs={{0,8},{8,16},{16,24},{24,28},{28,20},{20,12},{12,4},{4,0},{1,9},{9... | collective-permute-start | bytes 6488072 | tf_op jit(solution)/shard_map/ppermute | solution.py:524
  290.2 33.0 %collective-permute-start.41 = (bf16[192,2048]{1,0:T(8,128)(2,1)S(1)}, bf16[192,2048]{1,0:T(8,128)(2,1)}, u32[]{:S(2)}, u32[]{:S(2)}) collective-permute-start(bf16[192,2048]{1,0:T(8,128)(2,1)S(1)} %get-tuple-element.137.refs_0_), channel_id=1, source_target_pairs={{0,1},{1,0},{2,3},{3,2},{4,5},{5,4},{6,7},{7,6},{8,9},{9,8},{10,11... | collective-permute-start | bytes 2359304 | tf_op jit(solution)/shard_map/ppermute | solution.py:604
  320.9 53.5 %collective-permute-start.52 = (bf16[256,4224]{1,0:T(8,128)(2,1)}, bf16[256,4224]{1,0:T(8,128)(2,1)}, u32[]{:S(2)}, u32[]{:S(2)}) collective-permute-start(bf16[256,4224]{1,0:T(8,128)(2,1)} %get-tuple-element.142), channel_id=1, source_target_pairs={{0,8},{8,16},{16,24},{24,28},{28,20},{20,12},{12,4},{4,0},{1,9},{9... | collective-permute-start | bytes 6488072 | tf_op jit(solution)/shard_map/ppermute | solution.py:524
  322.5 53.5 %collective-permute-start.53 = (bf16[256,4224]{1,0:T(8,128)(2,1)}, bf16[256,4224]{1,0:T(8,128)(2,1)}, u32[]{:S(2)}, u32[]{:S(2)}) collective-permute-start(bf16[256,4224]{1,0:T(8,128)(2,1)} %get-tuple-element.141), channel_id=1, source_target_pairs={{8,0},{16,8},{24,16},{28,24},{20,28},{12,20},{4,12},{0,4},{9,1},{1... | collective-permute-start | bytes 6488072 | tf_op jit(solution)/shard_map/ppermute | solution.py:525
  353.3 37.6 %collective-permute-start.46 = (bf16[384,2048]{1,0:T(8,128)(2,1)}, bf16[384,2048]{1,0:T(8,128)(2,1)}, u32[]{:S(2)}, u32[]{:S(2)}) collective-permute-start(bf16[384,2048]{1,0:T(8,128)(2,1)} %pad_maximum_fusion.6), channel_id=1, source_target_pairs={{0,1},{1,0},{2,3},{3,2},{4,5},{5,4},{6,7},{7,6},{8,9},{9,8},{10,11... | collective-permute-start | bytes 4718600 | tf_op jit(solution)/shard_map/ppermute | solution.py:624
  371.2 25.3 %collective-permute-start.39 = (bf16[384,2048]{1,0:T(8,128)(2,1)}, bf16[384,2048]{1,0:T(8,128)(2,1)S(1)}, u32[]{:S(2)}, u32[]{:S(2)}) collective-permute-start(bf16[384,2048]{1,0:T(8,128)(2,1)} %pad_maximum_fusion.5), channel_id=1, source_target_pairs={{0,1},{1,0},{2,3},{3,2},{4,5},{5,4},{6,7},{7,6},{8,9},{9,8},{10,11... | collective-permute-start | bytes 4718600 | tf_op jit(solution)/shard_map/ppermute | solution.py:624
  381.3 66.2 %collective-permute-start.56 = (bf16[256,4224]{1,0:T(8,128)(2,1)}, bf16[256,4224]{1,0:T(8,128)(2,1)S(1)}, u32[]{:S(2)}, u32[]{:S(2)}) collective-permute-start(bf16[256,4224]{1,0:T(8,128)(2,1)} %get-tuple-element.140), channel_id=1, source_target_pairs={{0,8},{8,16},{16,24},{24,28},{28,20},{20,12},{12,4},{4,0},{1,9},{9... | collective-permute-start | bytes 6488072 | tf_op jit(solution)/shard_map/ppermute | solution.py:524
  387.2 60.2 %collective-permute-start.57 = (bf16[256,4224]{1,0:T(8,128)(2,1)}, bf16[256,4224]{1,0:T(8,128)(2,1)S(1)}, u32[]{:S(2)}, u32[]{:S(2)}) collective-permute-start(bf16[256,4224]{1,0:T(8,128)(2,1)} %get-tuple-element.139), channel_id=1, source_target_pairs={{8,0},{16,8},{24,16},{28,24},{20,28},{12,20},{4,12},{0,4},{9,1},{1... | collective-permute-start | bytes 6488072 | tf_op jit(solution)/shard_map/ppermute | solution.py:525
  394.8 52.7 %collective-permute-start.54 = (bf16[256,1152]{1,0:T(8,128)(2,1)S(1)}, bf16[256,1152]{1,0:T(8,128)(2,1)S(1)}, u32[]{:S(2)}, u32[]{:S(2)}) collective-permute-start(bf16[256,1152]{1,0:T(8,128)(2,1)S(1)} %get-tuple-element.146), channel_id=1, source_target_pairs={{0,8},{8,16},{16,24},{24,28},{28,20},{20,12},{12,4},{4,0},{1,9},{9... | collective-permute-start | bytes 1769480 | tf_op jit(solution)/shard_map/ppermute | solution.py:524
  396.5 51.0 %collective-permute-start.55 = (bf16[256,1152]{1,0:T(8,128)(2,1)S(1)}, bf16[256,1152]{1,0:T(8,128)(2,1)S(1)}, u32[]{:S(2)}, u32[]{:S(2)}) collective-permute-start(bf16[256,1152]{1,0:T(8,128)(2,1)S(1)} %get-tuple-element.145), channel_id=1, source_target_pairs={{8,0},{16,8},{24,16},{28,24},{20,28},{12,20},{4,12},{0,4},{9,1},{1... | collective-permute-start | bytes 1769480 | tf_op jit(solution)/shard_map/ppermute | solution.py:525
  (117 other events, 1270.7 us)

commit v6 on v5

--- a/solution.py
+++ b/solution.py
@@ -55,7 +55,7 @@
 
 
 TILE = 256
-VMEM = 24 * 2**20
+VMEM = 16 * 2**20
 
 def lasting(time):
     return pl.CostEstimate(flops=int(time * 1.1e9), bytes_accessed=0, transcendentals=0)
@@ -673,7 +673,7 @@
     first_pieces, first_marks = first_travel.pieces, first_travel.marks
     tokens, cotangent = ring.shuffle(tie(tokens, first_shard), cotangent)
     rows_in = ring.gather_rows(tokens)
-    down_shard = tie(down_weight.astype(HALF), first_marks[-1], rows_in)
+    down_shard = tie(down_weight.astype(HALF), first_marks[-2])
     down_travel = ring.gather(down_shard).steps(whole_way)
     down_pieces, down_marks = down_travel.pieces, down_travel.marks
     feed_shard = jnp.concatenate([gate_weight, up_weight], axis=1).astype(HALF)
@@ -789,9 +789,10 @@
             (feed_sum[:, : 2 * units], feed_shard, feed_gain),
         )
     ]
-    gain_sums = jnp.stack(gain_sums)
     for index in (1, 2):
-        gain_sums = gain_sums + lax.ppermute(gain_sums, "tensor", beside(index))
+        gain_sums[1] = gain_sums[1] + lax.ppermute(gain_sums[1], "tensor", beside(index))
+    for index in (1, 2):
+        gain_sums[0] = gain_sums[0] + lax.ppermute(gain_sums[0], "tensor", beside(index))
     return (
         layer_out,
         input_grad,

time: 480 us -> 478 us (level)
  local copies, waits for them, and re-layouts: 31.2 us -> 25.8 us
    unnamed x164 -> x150, local copies, waits for them, and re-layouts: 24.5 us -> 19.6 us
  transfers between devices with their start and end apart: 62 -> 64, of which waited for: 35 -> 37; matrix products, arithmetic and copies ran while one was open for 13% -> 13% of each run, Pallas kernels for 21% -> 21%
where the time goes in v6:
time: 478 us; the launch traced here: 470 us
  waiting for transfers between devices  222 us (46%)
  Pallas kernels  105 us (22%)
  starting transfers between devices  59.6 us (12%)
  other arithmetic  50.1 us (10%)
  local copies, waits for them, and re-layouts  25.8 us (5%)
  matrix products  4.81 us (1%)
    ppermute x12, waiting for transfers between devices, step(): self.above = lax.ppermute(self.above, 'dp', ring.up)  74.7 us
    ppermute x4, waiting for transfers between devices, scatter_rows(): far = lax.ppermute(send, 'tensor', beside(2)).astype(FULL)  54.5 us
    ppermute x8, waiting for transfers between devices, send(): self.above = lax.ppermute(top, 'dp', self.ring.up)  44.7 us
    ppermute x12, waiting for transfers between devices, step(): self.below = lax.ppermute(self.below, 'dp', ring.down)  24.2 us
    pallas_call x3, Pallas kernels, outward(): pl.pallas_call(functools.partial(outward_kernel, slots, depth, view, tran...  22.4 us
    unnamed x150, local copies, waits for them, and re-layouts  19.6 us
    ppermute x12, starting transfers between devices, step(): self.below = lax.ppermute(self.below, 'dp', ring.down)  17.4 us
    pallas_call x3, Pallas kernels, feed_grads(): pl.pallas_call(functools.partial(feed_grads_kernel, which == 0), grid=(st...  16.4 us
  transfers between devices with their start and end apart: 64, of which 37 were waited for; matrix products, arithmetic and copies ran while one was open for 13% of the time, Pallas kernels for 21%

profile of v6, /device:TPU:0, one launch (start us, length us, event | category | flops | bytes accessed | tf_op | source)
XLA Modules:
  0.0 469.5 jit_solution(15596790904150317586)
XLA Ops:
  6.6 13.2 %collective-permute-done.4.refs_2_ = bf16[272,1152]{1,0:T(8,128)(2,1)S(1)} collective-permute-done((bf16[272,1152]{1,0:T(8,128)(2,1)S(1)}, bf16[272,1152]{1,0:T(8,128)(2,1)S(1)}, u32[]{:S(2)}, u32[]{:S(2)}) %collective-permute-start.4) | collective-permute-done | bytes 626720 | tf_op jit(solution)/shard_map/ppermute | solution.py:505
  27.1 8.0 %collective-permute-done.6.refs_4_ = bf16[272,1152]{1,0:T(8,128)(2,1)S(1)} collective-permute-done((bf16[272,1152]{1,0:T(8,128)(2,1)S(1)}, bf16[272,1152]{1,0:T(8,128)(2,1)S(1)}, u32[]{:S(2)}, u32[]{:S(2)}) %collective-permute-start.6) | collective-permute-done | bytes 626720 | tf_op jit(solution)/shard_map/ppermute | solution.py:505
  38.8 7.2 %collective-permute-done.1.refs_2_ = bf16[192,2048]{1,0:T(8,128)(2,1)} collective-permute-done((bf16[192,2048]{1,0:T(8,128)(2,1)S(1)}, bf16[192,2048]{1,0:T(8,128)(2,1)}, u32[]{:S(2)}, u32[]{:S(2)}) %collective-permute-start.1) | collective-permute-done | bytes 786464 | tf_op jit(solution)/shard_map/ppermute | solution.py:603
  56.3 6.7 %collective-permute-done.9.refs_7_ = bf16[128,1152]{1,0:T(8,128)(2,1)S(1)} collective-permute-done((bf16[128,1152]{1,0:T(8,128)(2,1)S(1)}, bf16[128,1152]{1,0:T(8,128)(2,1)S(1)}, u32[]{:S(2)}, u32[]{:S(2)}) %collective-permute-start.9) | collective-permute-done | bytes 294944 | tf_op jit(solution)/shard_map/ppermute | solution.py:504
  70.9 11.5 %collective-permute-done.11.refs_1_ = bf16[1408,256]{1,0:T(8,128)(2,1)} collective-permute-done((bf16[1408,256]{1,0:T(8,128)(2,1)}, bf16[1408,256]{1,0:T(8,128)(2,1)}, u32[]{:S(2)}, u32[]{:S(2)}) %collective-permute-start.11) | collective-permute-done | bytes 720928 | tf_op jit(solution)/shard_map/ppermute | solution.py:504
  99.0 12.4 %attend.1 = (bf16[768,512]{1,0:T(8,128)(2,1)S(1)}, bf16[768,128]{1,0:T(8,128)(2,1)S(1)}, bf16[768,512]{1,0:T(8,128)(2,1)S(1)}, f32[8,1,768]{2,1,0:T(1,128)S(1)}) custom-call(f32[768,640]{1,0:T(8,128)S(1)} %get-tuple-element.55.joined_ref, f32[768,128]{1,0:T(8,128)S(1)} %copy-done.27, f32[768,128]{1,0:T(8,128)S(1)} %pad_maximum_fusion.11.sin_ref, ...), custom_call_target="tpu_custom_call" | custom-call | tf_op jit(solution)/shard_map/attend/pallas_call | solution.py:127
  116.8 9.6 %collective-permute-done.16.refs_3_ = bf16[1408,256]{1,0:T(8,128)(2,1)} collective-permute-done((bf16[1408,256]{1,0:T(8,128)(2,1)}, bf16[1408,256]{1,0:T(8,128)(2,1)}, u32[]{:S(2)}, u32[]{:S(2)}) %collective-permute-start.16) | collective-permute-done | bytes 720928 | tf_op jit(solution)/shard_map/ppermute | solution.py:504
  140.0 15.8 %collective-permute-done.21 = bf16[192,2048]{1,0:T(8,128)(2,1)} collective-permute-done((bf16[192,2048]{1,0:T(8,128)(2,1)}, bf16[192,2048]{1,0:T(8,128)(2,1)}, u32[]{:S(2)}, u32[]{:S(2)}) %collective-permute-start.21) | collective-permute-done | bytes 786464 | tf_op jit(solution)/shard_map/ppermute | solution.py:626
  164.6 11.6 %collective-permute-done.27.refs_5_ = bf16[1408,256]{1,0:T(8,128)(2,1)S(1)} collective-permute-done((bf16[1408,256]{1,0:T(8,128)(2,1)}, bf16[1408,256]{1,0:T(8,128)(2,1)S(1)}, u32[]{:S(2)}, u32[]{:S(2)}) %collective-permute-start.27) | collective-permute-done | bytes 720928 | tf_op jit(solution)/shard_map/ppermute | solution.py:504
  180.4 7.2 %collective-permute-done.29.refs_7_ = bf16[704,256]{1,0:T(8,128)(2,1)S(1)} collective-permute-done((bf16[704,256]{1,0:T(8,128)(2,1)S(1)}, bf16[704,256]{1,0:T(8,128)(2,1)S(1)}, u32[]{:S(2)}, u32[]{:S(2)}) %collective-permute-start.29) | collective-permute-done | bytes 360480 | tf_op jit(solution)/shard_map/ppermute | solution.py:504
  188.8 7.5 %hidden_back.1.grad_ref = f32[768,1408]{1,0:T(8,128)S(1)} custom-call(bf16[768,2048]{1,0:T(8,128)(2,1)S(1)} %join.5.x_ref.grad_ref, bf16[1408,256]{1,0:T(8,128)(2,1)} %convert_element_type.282.refs_0_, bf16[1408,256]{1,0:T(8,128)(2,1)} %collective-permute-done.11.refs_1_, bf16[1408,256]{1,0:T(8,128)(2,1)} %collective-permute-done.12.refs_2_, ...), custom_call_target="tpu_custom_call" | custom-call | flops 11879999488 | tf_op jit(solution)/shard_map/hidden_back/pallas_call | solution.py:301
  196.3 20.9 %collective-permute-done.31.refs_5_ = bf16[256,2816]{1,0:T(8,128)(2,1)S(1)} collective-permute-done((bf16[256,2816]{1,0:T(8,128)(2,1)}, bf16[256,2816]{1,0:T(8,128)(2,1)S(1)}, u32[]{:S(2)}, u32[]{:S(2)}) %collective-permute-start.31) | collective-permute-done | bytes 1441824 | tf_op jit(solution)/shard_map/ppermute | solution.py:504
  219.6 11.5 %gate_up_start.1.sum_ref = f32[768,2816]{1,0:T(8,128)S(1)} custom-call(bf16[768,2048]{1,0:T(8,128)(2,1)S(1)} %join.6.x_ref, bf16[256,2816]{1,0:T(8,128)(2,1)} %pad_maximum_fusion.7.refs_0_, bf16[256,2816]{1,0:T(8,128)(2,1)} %collective-permute-done.18.refs_1_, bf16[256,2816]{1,0:T(8,128)(2,1)} %collective-permute-done.19.refs_2_, ...), custom_call_target="tpu_custom_call" | custom-call | flops 13200000000 | tf_op jit(solution)/shard_map/gate_up_start/pallas_call | solution.py:238
  246.7 12.7 %feed_back.1 = bf16[768,2048]{1,0:T(8,128)(2,1)S(1)} custom-call(bf16[768,2816]{1,0:T(8,128)(2,1)S(1)} %get-tuple-element.68.feed_ref.x_ref, bf16[256,2816]{1,0:T(8,128)(2,1)} %pad_maximum_fusion.7.refs_0_, bf16[256,2816]{1,0:T(8,128)(2,1)} %collective-permute-done.18.refs_1_, bf16[256,2816]{1,0:T(8,128)(2,1)} %collective-permute-done.19.refs_2_, ...), custom_call_target="tpu_custom_call" | custom-call | tf_op jit(solution)/shard_map/feed_back/pallas_call | solution.py:370
  271.7 12.1 %collective-permute-done.38 = bf16[192,2048]{1,0:T(8,128)(2,1)S(1)} collective-permute-done((bf16[192,2048]{1,0:T(8,128)(2,1)S(1)}, bf16[192,2048]{1,0:T(8,128)(2,1)S(1)}, u32[]{:S(2)}, u32[]{:S(2)}) %collective-permute-start.38) | collective-permute-done | bytes 786464 | tf_op jit(solution)/shard_map/ppermute | solution.py:626
  289.6 10.3 %feed_grads.5 = bf16[1280,4224]{1,0:T(8,128)(2,1)S(1)} custom-call(bf16[768,2048]{1,0:T(8,128)(2,1)S(1)} %join.6.x_ref, bf16[768,2816]{1,0:T(8,128)(2,1)S(1)} %get-tuple-element.68.feed_ref.x_ref, bf16[768,2048]{1,0:T(8,128)(2,1)S(1)} %join.5.x_ref.grad_ref, bf16[768,1408]{1,0:T(8,128)(2,1)S(1)} %get-tuple-element.72.hidden_ref.x_ref), custom_call_target="tpu_custom_call" | custom-call | tf_op jit(solution)/shard_map/feed_grads/pallas_call | solution.py:347
  299.9 7.4 %down.1 = bf16[768,2048]{1,0:T(8,128)(2,1)S(1)} custom-call(bf16[768,1408]{1,0:T(8,128)(2,1)S(1)} %get-tuple-element.72.hidden_ref.x_ref, bf16[1408,256]{1,0:T(8,128)(2,1)} %convert_element_type.282.refs_0_, bf16[1408,256]{1,0:T(8,128)(2,1)} %collective-permute-done.11.refs_1_, bf16[1408,256]{1,0:T(8,128)(2,1)} %collective-permute-done.12.refs_2_, ...), custom_call_target="tpu_custom_call" | custom-call | tf_op jit(solution)/shard_map/down/pallas_call | solution.py:370
  326.9 13.7 %attend_back.1.grad_ref = bf16[768,640]{1,0:T(8,128)(2,1)S(1)} custom-call(bf16[768,512]{1,0:T(8,128)(2,1)S(1)} %copy-done.34, bf16[768,128]{1,0:T(8,128)(2,1)S(1)} %copy-done.38, bf16[768,512]{1,0:T(8,128)(2,1)S(1)} %mixed_back.1.do_ref, f32[8,1,768]{2,1,0:T(1,128)S(1)} %get-tuple-element.78.lse_ref, f32[768,128]{1,0:T(8,128)S(1)} %copy-done.28, ...), custom_call_target="tpu_custom_call" | custom-call | tf_op jit(solution)/shard_map/attend_back/pallas_call | solution.py:193
  352.7 17.8 %collective-permute-done.48 = bf16[128,1152]{1,0:T(8,128)(2,1)S(1)} collective-permute-done((bf16[128,1152]{1,0:T(8,128)(2,1)S(1)}, bf16[128,1152]{1,0:T(8,128)(2,1)S(1)}, u32[]{:S(2)}, u32[]{:S(2)}) %collective-permute-start.48) | collective-permute-done | bytes 294944 | tf_op jit(solution)/shard_map/ppermute | solution.py:524
  396.2 15.6 %collective-permute-done.47 = bf16[192,2048]{1,0:T(8,128)(2,1)S(1)} collective-permute-done((bf16[192,2048]{1,0:T(8,128)(2,1)S(1)}, bf16[192,2048]{1,0:T(8,128)(2,1)S(1)}, u32[]{:S(2)}, u32[]{:S(2)}) %collective-permute-start.47) | collective-permute-done | bytes 786464 | tf_op jit(solution)/shard_map/ppermute | solution.py:626
  413.5 11.0 %collective-permute-done.40 = bf16[192,2048]{1,0:T(8,128)(2,1)S(1)} collective-permute-done((bf16[192,2048]{1,0:T(8,128)(2,1)S(1)}, bf16[192,2048]{1,0:T(8,128)(2,1)S(1)}, u32[]{:S(2)}, u32[]{:S(2)}) %collective-permute-start.40) | collective-permute-done | bytes 786464 | tf_op jit(solution)/shard_map/ppermute | solution.py:626
  427.5 8.1 %collective-permute-done.56 = bf16[256,4224]{1,0:T(8,128)(2,1)S(1)} collective-permute-done((bf16[256,4224]{1,0:T(8,128)(2,1)}, bf16[256,4224]{1,0:T(8,128)(2,1)S(1)}, u32[]{:S(2)}, u32[]{:S(2)}) %collective-permute-start.56) | collective-permute-done | bytes 2162720 | tf_op jit(solution)/shard_map/ppermute | solution.py:524
  440.7 5.7 %collective-permute-done.54 = bf16[256,1152]{1,0:T(8,128)(2,1)S(1)} collective-permute-done((bf16[256,1152]{1,0:T(8,128)(2,1)S(1)}, bf16[256,1152]{1,0:T(8,128)(2,1)S(1)}, u32[]{:S(2)}, u32[]{:S(2)}) %collective-permute-start.54) | collective-permute-done | bytes 589856 | tf_op jit(solution)/shard_map/ppermute | solution.py:524
  456.0 6.0 %collective-permute-done.58 = bf16[256,1152]{1,0:T(8,128)(2,1)S(1)} collective-permute-done((bf16[256,1152]{1,0:T(8,128)(2,1)}, bf16[256,1152]{1,0:T(8,128)(2,1)S(1)}, u32[]{:S(2)}, u32[]{:S(2)}) %collective-permute-start.58) | collective-permute-done | bytes 589856 | tf_op jit(solution)/shard_map/ppermute | solution.py:524
  (365 shorter events, 203.4 us)
Async XLA Ops:
  37.2 28.0 %collective-permute-start.14 = (bf16[192,2048]{1,0:T(8,128)(2,1)}, bf16[192,2048]{1,0:T(8,128)(2,1)}, u32[]{:S(2)}, u32[]{:S(2)}) collective-permute-start(bf16[192,2048]{1,0:T(8,128)(2,1)} %get-tuple-element.57.refs_0_), channel_id=1, source_target_pairs={{0,2},{1,3},{2,0},{3,1},{4,6},{5,7},{6,4},{7,5},{8,10},{9,11},{10,... | collective-permute-start | bytes 2359304 | tf_op jit(solution)/shard_map/ppermute | solution.py:603
  65.2 61.3 %collective-permute-start.18 = (bf16[256,2816]{1,0:T(8,128)(2,1)}, bf16[256,2816]{1,0:T(8,128)(2,1)}, u32[]{:S(2)}, u32[]{:S(2)}) collective-permute-start(bf16[256,2816]{1,0:T(8,128)(2,1)} %pad_maximum_fusion.7.refs_0_), channel_id=1, source_target_pairs={{0,8},{8,16},{16,24},{24,28},{28,20},{20,12},{12,4},{4,0},{1,9},{9... | collective-permute-start | bytes 4325384 | tf_op jit(solution)/shard_map/ppermute | solution.py:504
  65.7 60.8 %collective-permute-start.19 = (bf16[256,2816]{1,0:T(8,128)(2,1)}, bf16[256,2816]{1,0:T(8,128)(2,1)}, u32[]{:S(2)}, u32[]{:S(2)}) collective-permute-start(bf16[256,2816]{1,0:T(8,128)(2,1)} %pad_maximum_fusion.7.refs_0_), channel_id=1, source_target_pairs={{8,0},{16,8},{24,16},{28,24},{20,28},{12,20},{4,12},{0,4},{9,1},{1... | collective-permute-start | bytes 4325384 | tf_op jit(solution)/shard_map/ppermute | solution.py:505
  82.5 43.9 %collective-permute-start.16 = (bf16[1408,256]{1,0:T(8,128)(2,1)}, bf16[1408,256]{1,0:T(8,128)(2,1)}, u32[]{:S(2)}, u32[]{:S(2)}) collective-permute-start(bf16[1408,256]{1,0:T(8,128)(2,1)} %collective-permute-done.11.refs_1_), channel_id=1, source_target_pairs={{0,8},{8,16},{16,24},{24,28},{28,20},{20,12},{12,4},{4,0},{1,9},{9... | collective-permute-start | bytes 2162696 | tf_op jit(solution)/shard_map/ppermute | solution.py:504
  82.9 43.6 %collective-permute-start.17 = (bf16[1408,256]{1,0:T(8,128)(2,1)}, bf16[1408,256]{1,0:T(8,128)(2,1)}, u32[]{:S(2)}, u32[]{:S(2)}) collective-permute-start(bf16[1408,256]{1,0:T(8,128)(2,1)} %collective-permute-done.12.refs_2_), channel_id=1, source_target_pairs={{8,0},{16,8},{24,16},{28,24},{20,28},{12,20},{4,12},{0,4},{9,1},{1... | collective-permute-start | bytes 2162696 | tf_op jit(solution)/shard_map/ppermute | solution.py:505
  126.6 34.8 %collective-permute-start.22 = (bf16[256,2816]{1,0:T(8,128)(2,1)}, bf16[256,2816]{1,0:T(8,128)(2,1)}, u32[]{:S(2)}, u32[]{:S(2)}) collective-permute-start(bf16[256,2816]{1,0:T(8,128)(2,1)} %collective-permute-done.18.refs_1_), channel_id=1, source_target_pairs={{0,8},{8,16},{16,24},{24,28},{28,20},{20,12},{12,4},{4,0},{1,9},{9... | collective-permute-start | bytes 4325384 | tf_op jit(solution)/shard_map/ppermute | solution.py:504
  127.7 34.7 %collective-permute-start.23 = (bf16[256,2816]{1,0:T(8,128)(2,1)}, bf16[256,2816]{1,0:T(8,128)(2,1)}, u32[]{:S(2)}, u32[]{:S(2)}) collective-permute-start(bf16[256,2816]{1,0:T(8,128)(2,1)} %collective-permute-done.19.refs_2_), channel_id=1, source_target_pairs={{8,0},{16,8},{24,16},{28,24},{20,28},{12,20},{4,12},{0,4},{9,1},{1... | collective-permute-start | bytes 4325384 | tf_op jit(solution)/shard_map/ppermute | solution.py:505
  137.5 38.7 %collective-permute-start.27 = (bf16[1408,256]{1,0:T(8,128)(2,1)}, bf16[1408,256]{1,0:T(8,128)(2,1)S(1)}, u32[]{:S(2)}, u32[]{:S(2)}) collective-permute-start(bf16[1408,256]{1,0:T(8,128)(2,1)} %collective-permute-done.16.refs_3_), channel_id=1, source_target_pairs={{0,8},{8,16},{16,24},{24,28},{28,20},{20,12},{12,4},{4,0},{1,9},{9... | collective-permute-start | bytes 2162696 | tf_op jit(solution)/shard_map/ppermute | solution.py:504
  138.7 38.6 %collective-permute-start.28 = (bf16[1408,256]{1,0:T(8,128)(2,1)}, bf16[1408,256]{1,0:T(8,128)(2,1)S(1)}, u32[]{:S(2)}, u32[]{:S(2)}) collective-permute-start(bf16[1408,256]{1,0:T(8,128)(2,1)} %collective-permute-done.17.refs_4_), channel_id=1, source_target_pairs={{8,0},{16,8},{24,16},{28,24},{20,28},{12,20},{4,12},{0,4},{9,1},{1... | collective-permute-start | bytes 2162696 | tf_op jit(solution)/shard_map/ppermute | solution.py:505
  178.4 38.8 %collective-permute-start.31 = (bf16[256,2816]{1,0:T(8,128)(2,1)}, bf16[256,2816]{1,0:T(8,128)(2,1)S(1)}, u32[]{:S(2)}, u32[]{:S(2)}) collective-permute-start(bf16[256,2816]{1,0:T(8,128)(2,1)} %collective-permute-done.22.refs_3_), channel_id=1, source_target_pairs={{0,8},{8,16},{16,24},{24,28},{28,20},{20,12},{12,4},{4,0},{1,9},{9... | collective-permute-start | bytes 4325384 | tf_op jit(solution)/shard_map/ppermute | solution.py:504
  179.5 38.9 %collective-permute-start.32 = (bf16[256,2816]{1,0:T(8,128)(2,1)}, bf16[256,2816]{1,0:T(8,128)(2,1)S(1)}, u32[]{:S(2)}, u32[]{:S(2)}) collective-permute-start(bf16[256,2816]{1,0:T(8,128)(2,1)} %collective-permute-done.23.refs_4_), channel_id=1, source_target_pairs={{8,0},{16,8},{24,16},{28,24},{20,28},{12,20},{4,12},{0,4},{9,1},{1... | collective-permute-start | bytes 4325384 | tf_op jit(solution)/shard_map/ppermute | solution.py:505
  187.6 31.8 %collective-permute-start.24 = (bf16[192,2048]{1,0:T(8,128)(2,1)S(1)}, bf16[192,2048]{1,0:T(8,128)(2,1)S(1)}, u32[]{:S(2)}, u32[]{:S(2)}) collective-permute-start(bf16[192,2048]{1,0:T(8,128)(2,1)S(1)} %multiply_convert_fusion.refs_0_), channel_id=1, source_target_pairs={{0,1},{1,0},{2,3},{3,2},{4,5},{5,4},{6,7},{7,6},{8,9},{9,8},{10,11... | collective-permute-start | bytes 2359304 | tf_op jit(solution)/shard_map/ppermute | solution.py:604
  187.6 31.8 %collective-permute-start.26 = (bf16[192,2048]{1,0:T(8,128)(2,1)S(1)}, bf16[192,2048]{1,0:T(8,128)(2,1)S(1)}, u32[]{:S(2)}, u32[]{:S(2)}) collective-permute-start(bf16[192,2048]{1,0:T(8,128)(2,1)S(1)} %collective-permute-done.25.refs_2_), channel_id=1, source_target_pairs={{0,1},{1,0},{2,3},{3,2},{4,5},{5,4},{6,7},{7,6},{8,9},{9,8},{10,11... | collective-permute-start | bytes 2359304 | tf_op jit(solution)/shard_map/ppermute | solution.py:605
  267.3 45.6 %collective-permute-start.45 = (bf16[256,4224]{1,0:T(8,128)(2,1)}, bf16[256,4224]{1,0:T(8,128)(2,1)}, u32[]{:S(2)}, u32[]{:S(2)}) collective-permute-start(bf16[256,4224]{1,0:T(8,128)(2,1)} %pad_maximum_fusion.2), channel_id=1, source_target_pairs={{8,0},{16,8},{24,16},{28,24},{20,28},{12,20},{4,12},{0,4},{9,1},{1... | collective-permute-start | bytes 6488072 | tf_op jit(solution)/shard_map/ppermute | solution.py:525
  270.0 44.9 %collective-permute-start.44 = (bf16[256,4224]{1,0:T(8,128)(2,1)S(1)}, bf16[256,4224]{1,0:T(8,128)(2,1)}, u32[]{:S(2)}, u32[]{:S(2)}) collective-permute-start(bf16[256,4224]{1,0:T(8,128)(2,1)S(1)} %pad_maximum_fusion.1), channel_id=1, source_target_pairs={{0,8},{8,16},{16,24},{24,28},{28,20},{20,12},{12,4},{4,0},{1,9},{9... | collective-permute-start | bytes 6488072 | tf_op jit(solution)/shard_map/ppermute | solution.py:524
  289.5 33.1 %collective-permute-start.41 = (bf16[192,2048]{1,0:T(8,128)(2,1)S(1)}, bf16[192,2048]{1,0:T(8,128)(2,1)}, u32[]{:S(2)}, u32[]{:S(2)}) collective-permute-start(bf16[192,2048]{1,0:T(8,128)(2,1)S(1)} %get-tuple-element.137.refs_0_), channel_id=1, source_target_pairs={{0,1},{1,0},{2,3},{3,2},{4,5},{5,4},{6,7},{7,6},{8,9},{9,8},{10,11... | collective-permute-start | bytes 2359304 | tf_op jit(solution)/shard_map/ppermute | solution.py:604
  320.2 52.7 %collective-permute-start.52 = (bf16[256,4224]{1,0:T(8,128)(2,1)}, bf16[256,4224]{1,0:T(8,128)(2,1)}, u32[]{:S(2)}, u32[]{:S(2)}) collective-permute-start(bf16[256,4224]{1,0:T(8,128)(2,1)} %get-tuple-element.142), channel_id=1, source_target_pairs={{0,8},{8,16},{16,24},{24,28},{28,20},{20,12},{12,4},{4,0},{1,9},{9... | collective-permute-start | bytes 6488072 | tf_op jit(solution)/shard_map/ppermute | solution.py:524
  321.8 52.7 %collective-permute-start.53 = (bf16[256,4224]{1,0:T(8,128)(2,1)}, bf16[256,4224]{1,0:T(8,128)(2,1)}, u32[]{:S(2)}, u32[]{:S(2)}) collective-permute-start(bf16[256,4224]{1,0:T(8,128)(2,1)} %get-tuple-element.141), channel_id=1, source_target_pairs={{8,0},{16,8},{24,16},{28,24},{20,28},{12,20},{4,12},{0,4},{9,1},{1... | collective-permute-start | bytes 6488072 | tf_op jit(solution)/shard_map/ppermute | solution.py:525
  352.5 36.7 %collective-permute-start.46 = (bf16[384,2048]{1,0:T(8,128)(2,1)}, bf16[384,2048]{1,0:T(8,128)(2,1)}, u32[]{:S(2)}, u32[]{:S(2)}) collective-permute-start(bf16[384,2048]{1,0:T(8,128)(2,1)} %pad_maximum_fusion.6), channel_id=1, source_target_pairs={{0,1},{1,0},{2,3},{3,2},{4,5},{5,4},{6,7},{7,6},{8,9},{9,8},{10,11... | collective-permute-start | bytes 4718600 | tf_op jit(solution)/shard_map/ppermute | solution.py:624
  379.8 55.7 %collective-permute-start.56 = (bf16[256,4224]{1,0:T(8,128)(2,1)}, bf16[256,4224]{1,0:T(8,128)(2,1)S(1)}, u32[]{:S(2)}, u32[]{:S(2)}) collective-permute-start(bf16[256,4224]{1,0:T(8,128)(2,1)} %get-tuple-element.140), channel_id=1, source_target_pairs={{0,8},{8,16},{16,24},{24,28},{28,20},{20,12},{12,4},{4,0},{1,9},{9... | collective-permute-start | bytes 6488072 | tf_op jit(solution)/shard_map/ppermute | solution.py:524
  386.5 50.5 %collective-permute-start.57 = (bf16[256,4224]{1,0:T(8,128)(2,1)}, bf16[256,4224]{1,0:T(8,128)(2,1)}, u32[]{:S(2)}, u32[]{:S(2)}) collective-permute-start(bf16[256,4224]{1,0:T(8,128)(2,1)} %get-tuple-element.139), channel_id=1, source_target_pairs={{8,0},{16,8},{24,16},{28,24},{20,28},{12,20},{4,12},{0,4},{9,1},{1... | collective-permute-start | bytes 6488072 | tf_op jit(solution)/shard_map/ppermute | solution.py:525
  392.3 32.3 %collective-permute-start.40 = (bf16[192,2048]{1,0:T(8,128)(2,1)S(1)}, bf16[192,2048]{1,0:T(8,128)(2,1)S(1)}, u32[]{:S(2)}, u32[]{:S(2)}) collective-permute-start(bf16[192,2048]{1,0:T(8,128)(2,1)S(1)} %fusion.8), channel_id=1, source_target_pairs={{0,2},{1,3},{2,0},{3,1},{4,6},{5,7},{6,4},{7,5},{8,10},{9,11},{10,... | collective-permute-start | bytes 2359304 | tf_op jit(solution)/shard_map/ppermute | solution.py:626
  394.5 52.0 %collective-permute-start.54 = (bf16[256,1152]{1,0:T(8,128)(2,1)S(1)}, bf16[256,1152]{1,0:T(8,128)(2,1)S(1)}, u32[]{:S(2)}, u32[]{:S(2)}) collective-permute-start(bf16[256,1152]{1,0:T(8,128)(2,1)S(1)} %get-tuple-element.146), channel_id=1, source_target_pairs={{0,8},{8,16},{16,24},{24,28},{28,20},{20,12},{12,4},{4,0},{1,9},{9... | collective-permute-start | bytes 1769480 | tf_op jit(solution)/shard_map/ppermute | solution.py:524
  411.8 34.8 %collective-permute-start.55 = (bf16[256,1152]{1,0:T(8,128)(2,1)S(1)}, bf16[256,1152]{1,0:T(8,128)(2,1)S(1)}, u32[]{:S(2)}, u32[]{:S(2)}) collective-permute-start(bf16[256,1152]{1,0:T(8,128)(2,1)S(1)} %get-tuple-element.145), channel_id=1, source_target_pairs={{8,0},{16,8},{24,16},{28,24},{20,28},{12,20},{4,12},{0,4},{9,1},{1... | collective-permute-start | bytes 1769480 | tf_op jit(solution)/shard_map/ppermute | solution.py:525
  (112 other events, 1293.2 us)
